TPU v7x, 128 devices: a whole 4x4x4 slice. The times are simulated.
128 devices in a mesh: wide: 32 (over x, z, core), narrow: 4 (over y).
Axes of the slice: x: 4, y: 4, z: 4, core: 2. Of those that a mesh axis runs over, the one named last changes fastest.
Arguments:
- operator_tiles: float32 [32, 4, 32, 8, 128, 128], P('wide', 'narrow')
- tile_slab: int32 [32, 4, 32, 8], P('wide', 'narrow'), may hold values from 0 to 8, as said below
- tile_column: int32 [32, 4, 32, 8], P('wide', 'narrow'), may hold values from 0 to 31, as said below
- tile_live: int32 [32, 4, 32, 8], P('wide', 'narrow'), may hold values from 0 to 1, as said below
- send_list: int32 [32, 4, 16], P('wide', 'narrow'), may hold values from 0 to 31, as said below
- aggregate: int32 [32, 4, 32], P('wide', 'narrow'), may hold values from 0 to 3
- null_modes: float32 [32, 4, 32, 6, 128], P('wide', 'narrow'), may hold values from -0.5 to 0.5
Outputs:
- prolongator: float32 [32, 4, 32, 216, 128], P('wide', 'narrow')
- coarse_operator: float32 [32, 4, 24, 1176], P('wide', 'narrow')
Inputs may be any that keep to these rules, and one draw needn't show every extreme that they name: Slot 0 of every block row is its own diagonal block: tile_slab 4, tile_column the row itself, tile_live 1. Every neighbour subdomain named lies inside the mesh. `tile_column`: for tile_slab 4 a block row of the same subdomain; otherwise a position in the neighbour's send_list. `tile_live`: the live tiles of a row are a prefix of its slots; in every subdomain some row uses all 8. `send_list`: distinct block rows of the subdomain.
All inputs are finite; a program needn't handle non-finite values.
Results may differ from a plain program's by a relative error of at most 0.0003.
Values sent between devices are 32-bit elements; how exact they have to be, the bound alone decides.
No kernel may reach another device: no remote copies, remote signals or barrier semaphores. Data moves between devices by JAX's collectives and lax.ppermute only.
A program may use at most 256 MiB of HBM per device.

v0:
```python
import jax
import jax.numpy as jnp
import numpy as np
from jax import lax
from jax.sharding import PartitionSpec as P

MODES = 6
AGG = 4


OMEGA = 0.7
HIGH = lax.Precision.HIGHEST


def with_halo(array, sides, width):
    for axis, dim in sides:
        size, length = (lax.axis_size(axis), array.shape[dim])
        up = [(i, (i + 1) % size) for i in range(size - 1)]
        down = [(j, i) for i, j in up]
        last = lax.slice_in_dim(array, length - width, length, axis=dim)
        leading = lax.slice_in_dim(array, 0, width, axis=dim)
        before = lax.ppermute(last, axis, up)
        after = lax.ppermute(leading, axis, down)
        array = jnp.concatenate([before, array, after], axis=dim)
    return array


def shifted(array, axis, by):
    size = lax.axis_size(axis)
    pairs = [(i, i + by) for i in range(size) if 0 <= i + by < size]
    return lax.ppermute(array, axis, pairs)


def spread_lookup():
    lookup = np.zeros((9, 9, 25), np.float32)
    for slab_pos in range(9):
        for inner_pos in range(9):
            rowpos = slab_pos // 3 + inner_pos // 3
            colpos = slab_pos % 3 + inner_pos % 3
            lookup[slab_pos, inner_pos, rowpos * 5 + colpos] = 1.0
    return lookup


def owner_lookup():
    lookup = np.zeros((9, 25, 49), np.float32)
    for owner_pos in range(9):
        for target in range(25):
            rowpos = target // 5 - owner_pos // 3 + 2
            colpos = target % 5 - owner_pos % 3 + 2
            lookup[owner_pos, target, rowpos * 7 + colpos] = 1.0
    return lookup


def tentative(null_modes, aggregate):
    member = (aggregate[:, None] == jnp.arange(AGG, dtype=jnp.int32)[None, :]).astype(jnp.float32)
    spread = member[:, :, None, None] * null_modes[:, None, :, :]
    return spread.reshape(member.shape[0], AGG * MODES, null_modes.shape[-1])


def slab_onehot(slab_dev):
    return (slab_dev[..., None] == jnp.arange(9, dtype=jnp.int32)).astype(jnp.float32)


def smooth(tiles_dev, slab_dev, column_dev, live_dev, tentative_dev, halo_dev):
    block_rows = tentative_dev.shape[0]
    offered = halo_dev.shape[2]
    lookup = jnp.concatenate(
        [tentative_dev, halo_dev.reshape((9 * offered,) + tentative_dev.shape[1:])], 0
    )
    source_row = jnp.where(slab_dev == 4, column_dev, block_rows + slab_dev * offered + column_dev)
    operand = lookup[source_row]
    product = jnp.einsum("rkcj,rkij->rkci", operand, tiles_dev, precision=HIGH)
    weights = live_dev.astype(jnp.float32)[..., None] * slab_onehot(slab_dev)
    gathered = jnp.einsum("rkf,rkci->rfci", weights, product, precision=HIGH)
    inverse_diag = 1.0 / jnp.diagonal(tiles_dev[:, 0], axis1=1, axis2=2)
    centered = jnp.zeros(gathered.shape, jnp.float32).at[:, 4].set(tentative_dev)
    return centered - OMEGA * gathered * inverse_diag[:, None, None, :]


def couple(tiles_dev, slab_dev, column_dev, live_dev, prolong_dev, halo_dev):
    block_rows = prolong_dev.shape[0]
    offered = halo_dev.shape[2]
    lookup = jnp.concatenate(
        [prolong_dev, halo_dev.reshape((9 * offered,) + prolong_dev.shape[1:])], 0
    )
    source_row = jnp.where(
        slab_dev == 4, column_dev, block_rows + slab_dev * offered + column_dev
    ).astype(jnp.int32)
    operand = lookup[source_row]
    product = jnp.einsum("rkfcj,rkij->rkfci", operand, tiles_dev, precision=HIGH)
    spread = jnp.asarray(spread_lookup(), dtype=jnp.float32)
    weights = live_dev.astype(jnp.float32)[..., None, None] * jnp.einsum(
        "rks,sfe->rkfe", slab_onehot(slab_dev), spread, precision=HIGH
    )
    applied = jnp.einsum("rkfe,rkfci->reci", weights, product, precision=HIGH)
    coupled = jnp.einsum("rfci,regi->fceg", prolong_dev, applied, precision=HIGH)
    owners = jnp.asarray(owner_lookup(), dtype=jnp.float32)
    by_owner = jnp.einsum("fceg,feo->fcog", coupled, owners, precision=HIGH)
    width = coupled.shape[1]
    return by_owner.reshape(3, 3, width, 49 * width)


def body(operator_tiles, tile_slab, tile_column, tile_live, send_list, aggregate, null_modes):
    tiles_dev = operator_tiles[0, 0]
    slab_dev = tile_slab[0, 0]
    column_dev = tile_column[0, 0]
    live_dev = tile_live[0, 0]
    offered_rows = send_list[0, 0]
    tentative_dev = tentative(null_modes[0, 0], aggregate[0, 0])
    halo_tent = with_halo(tentative_dev[offered_rows][None, None], (("wide", 0), ("narrow", 1)), 1)
    prolong_dev = smooth(tiles_dev, slab_dev, column_dev, live_dev, tentative_dev, halo_tent)
    outgoing = prolong_dev[offered_rows][None, None]
    halo_prolong = with_halo(outgoing, (("wide", 0), ("narrow", 1)), 1)
    by_owner = couple(tiles_dev, slab_dev, column_dev, live_dev, prolong_dev, halo_prolong)
    merged = by_owner[1]
    for offset in (1, -1):
        merged = merged + shifted(by_owner[offset + 1], "wide", offset)
    coarse = merged[1]
    for offset in (1, -1):
        coarse = coarse + shifted(merged[offset + 1], "narrow", offset)
    block_rows = prolong_dev.shape[0]
    return (prolong_dev.reshape((1, 1, block_rows, -1, prolong_dev.shape[-1])), coarse[None, None])


def solution(mesh):
    in_specs = (
        P("wide", "narrow", None, None, None, None),
        P("wide", "narrow", None, None),
        P("wide", "narrow", None, None),
        P("wide", "narrow", None, None),
        P("wide", "narrow", None),
        P("wide", "narrow", None),
        P("wide", "narrow", None, None, None),
    )
    out_specs = (P("wide", "narrow", None, None, None), P("wide", "narrow", None, None))
    return jax.shard_map(body, mesh=mesh, in_specs=in_specs, out_specs=out_specs, check_vma=False)
```

profile of v0, /device:TPU:14, one launch (start us, length us, event | category | flops | bytes accessed | tf_op | source)
XLA Modules:
  0.0 542.9 jit_solution(7861798008150358983)
XLA Ops:
  2.0 0.9 mul.82
  3.8 1.9 collective-permute-start
  5.8 5.8 %collective-permute-start.1 = (f32[1,1,16,24,128]{4,3,2,1,0:T(8,128)S(1)}, f32[1,1,16,24,128]{4,3,2,1,0:T(8,128)S(1)}, u32[]{:S(2)}, u32[]{:S(2)}) collective-permute-start(f32[1,1,16,24,128]{4,3,2,1,0:T(8,128)S(1)} %bitcast.103), channel_id=1, source_target_pairs={{4,0},{8,4},{12,8},{16,12},{20,16},{24,20},{28,24},{32,28},{36,32}... | collective-permute-start | bytes 589832 | tf_op jit(solution)/shard_map/ppermute | solution.py:23
  12.2 37.9 %copy.56 = f32[1,1,32,8,128,128]{2,5,4,3,1,0:T(8,128)} copy(f32[1,1,32,8,128,128]{5,4,3,2,1,0:T(8,128)} %param.11) | data formatting | bytes 33554432 | tf_op args[0]
  50.1 7.8 %slice_bitcast_fusion = f32[32,128,128]{0,2,1:T(8,128)} fusion(f32[32,8,128,128]{0,3,2,1:T(8,128)} %bitcast.15), kind=kLoop, calls=%fused_computation.16 | loop fusion | bytes 4194304 | tf_op jit(solution)/shard_map/squeeze | solution.py:75
  58.8 3.5 collective-permute-start.2
  62.3 2.4 collective-permute-start.3
  65.7 1.8 gather_fusion.2
  68.1 1.0 copy_multiply_fusion.1
  69.1 5.2 collective-permute-done.2
  74.3 3.2 collective-permute-done.3
  77.7 1.5 pad_maximum_fusion.3
  79.2 2.4 gather_fusion.1
  81.6 28.7 %fusion.4 = f32[32,8,24,128]{3,2,1,0:T(8,128)S(1)} fusion(f32[32,8,24,128]{3,2,1,0:T(8,128)S(1)} %bitcast.97, f32[1,1,32,8,128,128]{5,4,3,2,1,0:T(8,128)} %param.11), kind=kOutput, calls=%fused_computation.11 | convolution fusion | flops 1207959552 | bytes 23068672 | tf_op jit(solution)/shard_map/rkcj,rkij->rkci/dot_general | solution.py:72
  110.2 7.6 %multiply_subtract_fusion = f32[32,9,24,128]{3,1,2,0:T(8,128)} fusion(f32[32,1,24,128]{3,1,2,0:T(1,128)S(1)} %copy_multiply_fusion.1, f32[32,128]{1,0:T(8,128)S(1)} %copy-done.6, f32[32,8,9,1]{2,1,3,0:T(8,128)S(1)} %copy-done.3, f32[32,8,24,128]{3,2,1,0:T(8,128)S(1)} %fusion.4), kind=kOutput, calls=%fused_computation.17 | convolution fusion | flops 86704128 | bytes 7103488 | tf_op jit(solution)/shard_map/rkf,rkci->rfci/dot_general | solution.py:74
  117.9 3.5 gather_fusion.3
  122.0 2.4 collective-permute-start.4
  124.4 5.8 %collective-permute-start.5 = (f32[1,1,16,9,24,128]{5,4,3,2,1,0:T(8,128)S(1)}, f32[1,1,16,9,24,128]{5,4,3,2,1,0:T(8,128)S(1)}, u32[]{:S(2)}, u32[]{:S(2)}) collective-permute-start(f32[1,1,16,9,24,128]{5,4,3,2,1,0:T(8,128)S(1)} %copy.62), channel_id=1, source_target_pairs={{4,0},{8,4},{12,8},{16,12},{20,16},{24,20},{28,24},{32,28},{36,32}... | collective-permute-start | bytes 5308424 | tf_op jit(solution)/shard_map/ppermute | solution.py:23
  130.1 17.8 %collective-permute-done.4 = f32[1,1,16,9,24,128]{5,4,3,2,1,0:T(8,128)S(1)} collective-permute-done((f32[1,1,16,9,24,128]{5,4,3,2,1,0:T(8,128)S(1)}, f32[1,1,16,9,24,128]{5,4,3,2,1,0:T(8,128)S(1)}, u32[]{:S(2)}, u32[]{:S(2)}) %collective-permute-start.4) | collective-permute-done | bytes 1769504 | tf_op jit(solution)/shard_map/ppermute | solution.py:22
  148.4 1.7 collective-permute-done.5
  150.6 0.9 pad_maximum_fusion.2
  151.6 1.1 copy-done.1
  152.7 2.4 copy.66
  155.1 3.2 collective-permute-start.6
  158.3 3.0 collective-permute-start.7
  161.3 1.7 fusion.27
  163.0 110.4 %collective-permute-done.6 = f32[3,1,16,9,24,128]{5,4,3,2,1,0:T(8,128)S(1)} collective-permute-done((f32[3,1,16,9,24,128]{5,4,3,2,1,0:T(8,128)S(1)}, f32[3,1,16,9,24,128]{5,4,3,2,1,0:T(8,128)S(1)}, u32[]{:S(2)}, u32[]{:S(2)}) %collective-permute-start.6) | collective-permute-done | bytes 5308448 | tf_op jit(solution)/shard_map/ppermute | solution.py:22
  273.4 5.2 copy.68
  278.6 5.2 copy.69
  283.8 10.4 %pad_maximum_fusion.1 = f32[3,3,16,9,24,128]{5,3,4,2,1,0:T(8,128)S(1)} fusion(f32[3,1,16,9,24,128]{5,3,4,2,1,0:T(8,128)} %copy.69, f32[1,1,16,9,24,128]{5,3,4,2,1,0:T(8,128)} %copy-done.1, f32[1,1,16,9,24,128]{5,3,4,2,1,0:T(8,128)S(1)} %bitcast.96, f32[1,1,16,9,24,128]{5,3,4,2,1,0:T(8,128)} %copy-done, f32[3,1,16,9,24,128]{5,3,4,2,1,0:T(8,128)} %copy.68), kind=kLoop, calls=%fused_computation.8 | loop fusion | flops 15925248 | bytes 31850496 | tf_op jit(solution)/shard_map/concatenate | solution.py:24
  294.3 12.8 %pad_maximum_fusion = f32[176,9,24,128]{3,1,2,0:T(8,128)} fusion(f32[144,9,24,128]{3,1,2,0:T(8,128)S(1)} %bitcast.88, f32[32,9,24,128]{3,1,2,0:T(8,128)S(1)} %bitcast.90), kind=kLoop, calls=%fused_computation.7 | loop fusion | flops 4866048 | bytes 38928384 | tf_op jit(solution)/shard_map/concatenate | solution.py:83
  307.0 36.8 %gather_fusion.4 = f32[256,9,24,128]{3,1,2,0:T(8,128)} fusion(f32[176,9,24,128]{3,1,2,0:T(8,128)} %pad_maximum_fusion, s32[1024]{0:T(1024)S(1)} %pad_clamp_fusion), kind=kCustom, calls=%fused_computation.4 | custom fusion | bytes 56624128 | tf_op jit(solution)/shard_map/gather | solution.py:89
  343.8 31.3 %copy.70 = f32[256,9,24,128]{3,2,1,0:T(8,128)} copy(f32[256,9,24,128]{3,1,2,0:T(8,128)} %gather_fusion.4) | data formatting | bytes 56623104 | tf_op jit(solution)/shard_map/gather | solution.py:89
  375.1 52.4 %fusion.2 = f32[32,8,9,24,128]{4,3,2,1,0:T(8,128)} fusion(f32[32,8,9,24,128]{4,3,2,1,0:T(8,128)} %bitcast.87, f32[1,1,32,8,128,128]{5,4,3,2,1,0:T(8,128)} %param.11), kind=kOutput, calls=%fused_computation.9 | convolution fusion | flops 10871635968 | bytes 73400320 | tf_op jit(solution)/shard_map/rkfcj,rkij->rkfci/dot_general | solution.py:90
  427.5 39.6 %fusion.8 = f32[32,25,24,128,1]{3,1,2,0,4:T(8,128)} fusion(f32[32,8,9,24,128]{4,3,2,1,0:T(8,128)} %fusion.2, f32[32,8,9,25,1]{3,0,2,1,4:T(8,128)S(1)} %copy-done.2), kind=kOutput, calls=%fused_computation.18 | convolution fusion | flops 2123366400 | bytes 38372352 | tf_op jit(solution)/shard_map/rkfe,rkfci->reci/dot_general | solution.py:95
  467.1 39.1 %fusion.19 = f32[9,24,25,24]{2,1,3,0:T(8,128)S(1)} fusion(f32[32,25,24,128,1]{3,1,2,0,4:T(8,128)} %fusion.8, f32[32,9,24,128,1]{3,1,2,0,4:T(8,128)S(1)} %bitcast.93), kind=kOutput, calls=%fused_computation.27 | convolution fusion | flops 6370099200 | bytes 13887744 | tf_op jit(solution)/shard_map/rfci,regi->fceg/dot_general | solution.py:96
  506.2 2.7 fusion.24
  508.9 1.4 fusion.36
  510.3 1.9 copy.78
  512.8 1.9 collective-permute-start.8
  514.7 1.9 copy.79
  516.6 1.3 squeeze.38
  517.9 5.7 %collective-permute-start.9 = (f32[3,24,1176]{2,1,0:T(8,128)}, f32[3,24,1176]{2,1,0:T(8,128)}, u32[]{:S(2)}, u32[]{:S(2)}) collective-permute-start(f32[3,24,1176]{2,1,0:T(8,128)} %squeeze.38), channel_id=1, source_target_pairs={{4,0},{8,4},{12,8},{16,12},{20,16},{24,20},{28,24},{32,28},{36,32}... | collective-permute-start | bytes 1016072 | tf_op jit(solution)/shard_map/ppermute | solution.py:31
  525.0 4.0 collective-permute-done.9
  529.0 1.2 add_add_fusion
  530.2 2.8 collective-permute-start.10
  533.0 3.1 collective-permute-start.11
  536.0 6.0 %copy.61 = f32[32,9,24,128]{3,2,1,0:T(8,128)} copy(f32[32,9,24,128]{3,1,2,0:T(8,128)} %multiply_subtract_fusion) | data formatting | bytes 7077888 | tf_op jit(solution)/shard_map/sub | solution.py:77
  (61 shorter events, 9.7 us)
Async XLA Ops:
  3.8 54.1 %collective-permute-start = (f32[1,1,16,24,128]{4,3,2,1,0:T(8,128)S(1)}, f32[1,1,16,24,128]{4,3,2,1,0:T(8,128)S(1)}, u32[]{:S(2)}, u32[]{:S(2)}) collective-permute-start(f32[1,1,16,24,128]{4,3,2,1,0:T(8,128)S(1)} %bitcast.102), channel_id=1, source_target_pairs={{0,4},{4,8},{8,12},{12,16},{16,20},{20,24},{24,28},{28,32},{32,36}... | collective-permute-start | bytes 589832 | tf_op jit(solution)/shard_map/ppermute | solution.py:22
  5.8 52.2 %collective-permute-start.1 = (f32[1,1,16,24,128]{4,3,2,1,0:T(8,128)S(1)}, f32[1,1,16,24,128]{4,3,2,1,0:T(8,128)S(1)}, u32[]{:S(2)}, u32[]{:S(2)}) collective-permute-start(f32[1,1,16,24,128]{4,3,2,1,0:T(8,128)S(1)} %bitcast.103), channel_id=1, source_target_pairs={{4,0},{8,4},{12,8},{16,12},{20,16},{24,20},{28,24},{32,28},{36,32}... | collective-permute-start | bytes 589832 | tf_op jit(solution)/shard_map/ppermute | solution.py:23
  50.1 7.8 %copy-start.7 = (s32[1,1,32,8]{2,3,1,0:T(8,128)S(1)}, s32[1,1,32,8]{2,3,1,0:T(8,128)}, u32[]{:S(2)}) copy-start(s32[1,1,32,8]{2,3,1,0:T(8,128)} %param.12) | copy-start | bytes 3076
  50.1 7.8 %copy-start.8 = (s32[1,1,32,8]{2,3,1,0:T(8,128)S(1)}, s32[1,1,32,8]{2,3,1,0:T(8,128)}, u32[]{:S(2)}) copy-start(s32[1,1,32,8]{2,3,1,0:T(8,128)} %param.13) | copy-start | bytes 3076
  58.8 15.5 %collective-permute-start.2 = (f32[3,1,16,24,128]{4,3,2,1,0:T(8,128)}, f32[3,1,16,24,128]{4,3,2,1,0:T(8,128)S(1)}, u32[]{:S(2)}, u32[]{:S(2)}) collective-permute-start(f32[3,1,16,24,128]{4,3,2,1,0:T(8,128)} %pad_maximum_fusion.5), channel_id=1, source_target_pairs={{0,1},{1,2},{2,3},{4,5},{5,6},{6,7},{8,9},{9,10},{10,11},{12,13},{... | collective-permute-start | bytes 1769480 | tf_op jit(solution)/shard_map/ppermute | solution.py:22
  62.3 15.2 %collective-permute-start.3 = (f32[3,1,16,24,128]{4,3,2,1,0:T(8,128)}, f32[3,1,16,24,128]{4,3,2,1,0:T(8,128)S(1)}, u32[]{:S(2)}, u32[]{:S(2)}) collective-permute-start(f32[3,1,16,24,128]{4,3,2,1,0:T(8,128)} %pad_maximum_fusion.5), channel_id=1, source_target_pairs={{1,0},{2,1},{3,2},{5,4},{6,5},{7,6},{9,8},{10,9},{11,10},{13,12},{... | collective-permute-start | bytes 1769480 | tf_op jit(solution)/shard_map/ppermute | solution.py:23
  81.5 28.7 %copy-start.3 = (f32[32,8,9,1]{2,1,3,0:T(8,128)S(1)}, f32[32,8,9,1]{2,1,3,0:T(8,128)}, u32[]{:S(2)}) copy-start(f32[32,8,9,1]{2,1,3,0:T(8,128)} %copy.80) | copy-start | bytes 27652
  81.6 28.7 %copy-start.6 = (f32[32,128]{1,0:T(8,128)S(1)}, f32[32,128]{1,0:T(8,128)}, u32[]{:S(2)}) copy-start(f32[32,128]{1,0:T(8,128)} %copy.60) | copy-start | bytes 49156
  122.0 26.0 %collective-permute-start.4 = (f32[1,1,16,9,24,128]{5,4,3,2,1,0:T(8,128)S(1)}, f32[1,1,16,9,24,128]{5,4,3,2,1,0:T(8,128)S(1)}, u32[]{:S(2)}, u32[]{:S(2)}) collective-permute-start(f32[1,1,16,9,24,128]{5,4,3,2,1,0:T(8,128)S(1)} %copy.62), channel_id=1, source_target_pairs={{0,4},{4,8},{8,12},{12,16},{16,20},{20,24},{24,28},{28,32},{32,36}... | collective-permute-start | bytes 5308424 | tf_op jit(solution)/shard_map/ppermute | solution.py:22
  124.4 25.8 %collective-permute-start.5 = (f32[1,1,16,9,24,128]{5,4,3,2,1,0:T(8,128)S(1)}, f32[1,1,16,9,24,128]{5,4,3,2,1,0:T(8,128)S(1)}, u32[]{:S(2)}, u32[]{:S(2)}) collective-permute-start(f32[1,1,16,9,24,128]{5,4,3,2,1,0:T(8,128)S(1)} %copy.62), channel_id=1, source_target_pairs={{4,0},{8,4},{12,8},{16,12},{20,16},{24,20},{28,24},{32,28},{36,32}... | collective-permute-start | bytes 5308424 | tf_op jit(solution)/shard_map/ppermute | solution.py:23
  148.4 3.2 copy-start
  150.6 2.1 copy-start.1
  152.7 8.6 %copy-start.5 = (f32[9,9,25,1]{2,0,1,3:T(8,128)S(1)}, f32[9,9,25,1]{2,0,1,3:T(8,128)}, u32[]{:S(2)}) copy-start(f32[9,9,25,1]{2,0,1,3:T(8,128)} %constant.78) | copy-start | bytes 24304
  155.1 118.3 %collective-permute-start.6 = (f32[3,1,16,9,24,128]{5,4,3,2,1,0:T(8,128)S(1)}, f32[3,1,16,9,24,128]{5,4,3,2,1,0:T(8,128)S(1)}, u32[]{:S(2)}, u32[]{:S(2)}) collective-permute-start(f32[3,1,16,9,24,128]{5,4,3,2,1,0:T(8,128)S(1)} %copy.66), channel_id=1, source_target_pairs={{0,1},{1,2},{2,3},{4,5},{5,6},{6,7},{8,9},{9,10},{10,11},{12,13},{... | collective-permute-start | bytes 15925256 | tf_op jit(solution)/shard_map/ppermute | solution.py:22
  158.3 120.3 %collective-permute-start.7 = (f32[3,1,16,9,24,128]{5,4,3,2,1,0:T(8,128)S(1)}, f32[3,1,16,9,24,128]{5,4,3,2,1,0:T(8,128)S(1)}, u32[]{:S(2)}, u32[]{:S(2)}) collective-permute-start(f32[3,1,16,9,24,128]{5,4,3,2,1,0:T(8,128)S(1)} %copy.66), channel_id=1, source_target_pairs={{1,0},{2,1},{3,2},{5,4},{6,5},{7,6},{9,8},{10,9},{11,10},{13,12},{... | collective-permute-start | bytes 15925256 | tf_op jit(solution)/shard_map/ppermute | solution.py:23
  278.6 15.6 %slice-start = ((s8[6291456]{0:T(1024)(128)(4,1)}), s8[4194304]{0:T(1024)(128)(4,1)S(1)}, s32[]{:S(2)}) async-start(s8[6291456]{0:T(1024)(128)(4,1)} %bitcast.89), calls=%async_computation | async-start | bytes 8388608
  283.8 10.4 %slice-start.1 = ((s8[6291456]{0:T(1024)(128)(4,1)}), s8[2097152]{0:T(1024)(128)(4,1)S(1)}, s32[]{:S(2)}) async-start(s8[6291456]{0:T(1024)(128)(4,1)} %bitcast.89), calls=%async_computation.1 | async-start | bytes 4194304
  375.1 52.4 %copy-start.2 = (f32[32,8,9,25,1]{3,0,2,1,4:T(8,128)S(1)}, f32[32,8,9,25,1]{3,0,2,1,4:T(8,128)}, u32[]{:S(2)}) copy-start(f32[32,8,9,25,1]{3,0,2,1,4:T(8,128)} %fusion.27) | copy-start | bytes 691204
  375.1 92.0 %slice-start.2 = ((s8[6291456]{0:T(1024)(128)(4,1)}), s8[2097152]{0:T(1024)(128)(4,1)S(1)}, s32[]{:S(2)}) async-start(s8[6291456]{0:T(1024)(128)(4,1)} %bitcast.91), calls=%async_computation.2 | async-start | bytes 4194304
  427.5 39.6 %slice-start.3 = ((s8[6291456]{0:T(1024)(128)(4,1)}), s8[4194304]{0:T(1024)(128)(4,1)S(1)}, s32[]{:S(2)}) async-start(s8[6291456]{0:T(1024)(128)(4,1)} %bitcast.91), calls=%async_computation.3 | async-start | bytes 8388608
  467.1 39.1 %copy-start.4 = (f32[9,25,49,1]{2,1,3,0:T(8,128)S(1)}, f32[9,25,49,1]{2,1,3,0:T(8,128)}, u32[]{:S(2)}) copy-start(f32[9,25,49,1]{2,1,3,0:T(8,128)} %constant.79) | copy-start | bytes 132304
  512.8 12.2 %collective-permute-start.8 = (f32[3,24,1176]{2,1,0:T(8,128)S(1)}, f32[3,24,1176]{2,1,0:T(8,128)}, u32[]{:S(2)}, u32[]{:S(2)}) collective-permute-start(f32[3,24,1176]{2,1,0:T(8,128)S(1)} %squeeze.37), channel_id=1, source_target_pairs={{0,4},{4,8},{8,12},{12,16},{16,20},{20,24},{24,28},{28,32},{32,36}... | collective-permute-start | bytes 1016072 | tf_op jit(solution)/shard_map/ppermute | solution.py:31
  517.9 11.1 %collective-permute-start.9 = (f32[3,24,1176]{2,1,0:T(8,128)}, f32[3,24,1176]{2,1,0:T(8,128)}, u32[]{:S(2)}, u32[]{:S(2)}) collective-permute-start(f32[3,24,1176]{2,1,0:T(8,128)} %squeeze.38), channel_id=1, source_target_pairs={{4,0},{8,4},{12,8},{16,12},{20,16},{24,20},{28,24},{32,28},{36,32}... | collective-permute-start | bytes 1016072 | tf_op jit(solution)/shard_map/ppermute | solution.py:31
  530.2 11.9 %collective-permute-start.10 = (f32[24,1176]{1,0:T(8,128)S(1)}, f32[24,1176]{1,0:T(8,128)S(1)}, u32[]{:S(2)}, u32[]{:S(2)}) collective-permute-start(f32[24,1176]{1,0:T(8,128)S(1)} %get-tuple-element.17), channel_id=1, source_target_pairs={{0,1},{1,2},{2,3},{4,5},{5,6},{6,7},{8,9},{9,10},{10,11},{12,13},{... | collective-permute-start | bytes 338696 | tf_op jit(solution)/shard_map/ppermute | solution.py:31
  533.0 9.1 %collective-permute-start.11 = (f32[24,1176]{1,0:T(8,128)S(1)}, f32[24,1176]{1,0:T(8,128)S(1)}, u32[]{:S(2)}, u32[]{:S(2)}) collective-permute-start(f32[24,1176]{1,0:T(8,128)S(1)} %get-tuple-element.18), channel_id=1, source_target_pairs={{1,0},{2,1},{3,2},{5,4},{6,5},{7,6},{9,8},{10,9},{11,10},{13,12},{... | collective-permute-start | bytes 338696 | tf_op jit(solution)/shard_map/ppermute | solution.py:31
where the time goes:
time: 553 us; the launch traced here: 543 us
  matrix products  172 us (31%)
  local copies, waits for them, and re-layouts  155 us (28%)
  waiting for transfers between devices  142 us (26%)
  starting transfers between devices  41.4 us (7%)
  other arithmetic  31.7 us (6%)
    ppermute x4, waiting for transfers between devices, with_halo(): before = lax.ppermute(last, axis, up)  133 us
    gather x2, local copies, waits for them, and re-layouts, couple(): operand = lookup[source_row]  68.1 us
    dot_general x1, matrix products, couple(): jnp.einsum('rkfcj,rkij->rkfci', operand, tiles_dev, precision=HIGH)  52.4 us
    dot_general x1, matrix products, couple(): applied = jnp.einsum('rkfe,rkfci->reci', weights, product, precision=HIGH)  39.6 us
    unnamed x27, local copies, waits for them, and re-layouts  39.1 us
    dot_general x1, matrix products, couple(): jnp.einsum('rfci,regi->fceg', prolong_dev, applied, precision=HIGH)  39.1 us
    dot_general x1, matrix products, smooth(): product = jnp.einsum('rkcj,rkij->rkci', operand, tiles_dev, precision=HIGH)  28.7 us
    ppermute x4, starting transfers between devices, with_halo(): after = lax.ppermute(leading, axis, down)  16.9 us
  transfers between devices with their start and end apart: 12, of which 6 were waited for; matrix products, arithmetic and copies ran while one was open for 13% of the time, Pallas kernels for 0%

commit v1 on v0

v1 whole, which is shorter than its diff:
```python
import functools

import jax
import jax.numpy as jnp
from jax import lax
from jax.experimental import pallas as pl
from jax.experimental.pallas import tpu as pltpu
from jax.sharding import PartitionSpec as P

MODES = 6
GROUP = 8
AGG = 4
BS = 128
R = 32
K = 8
S = 16
C = 24
OMEGA = 0.7
E_ROWS = 25 * AGG * GROUP
NT = (((1,), (1,)), ((), ()))
VMEM = pl.BlockSpec(memory_space=pltpu.VMEM)
SMEM = pl.BlockSpec(memory_space=pltpu.SMEM)


def params(mib):
    return pltpu.CompilerParams(vmem_limit_bytes=mib * 2**20)


def split(value):
    high = value.astype(jnp.bfloat16)
    return high, (value - high.astype(jnp.float32)).astype(jnp.bfloat16)


def pair_halo(block, axis, dim):
    size = lax.axis_size(axis)
    near = [(i, i ^ 1) for i in range(size)]
    far = [(i, i + 1) if i % 2 else (i, i - 1) for i in range(1, size - 1)]
    return lax.ppermute(block, axis, near), lax.ppermute(block, axis, far)


def pack_kernel(send, aggregate, modes, own, message):
    for b in range(R):
        for m in range(MODES):
            own[b, m] = modes[m, b]
        own[b, MODES] = jnp.full((BS,), aggregate[b].astype(jnp.float32))
        own[b, MODES + 1] = jnp.zeros((BS,), jnp.float32)
    for s in range(S):
        message[s] = own[send[s]]


def smooth_kernel(send, source, base, live, tiles, table, slots, labels, message):
    eye = lax.broadcasted_iota(jnp.int32, (BS, BS), 0) == lax.broadcasted_iota(
        jnp.int32, (BS, BS), 1
    )
    place = lax.broadcasted_iota(jnp.int32, (GROUP, BS), 0) * BS + lax.broadcasted_iota(
        jnp.int32, (GROUP, BS), 1
    )

    def row(b, marks):
        scale = None
        for k in range(K):
            tile = tiles[b, k]
            if k == 0:
                diagonal = jnp.sum(jnp.where(eye, tile, 0.0), axis=0, keepdims=True)
                scale = OMEGA / diagonal
            modes = table[source[k, b]]
            high, low = split(modes)
            tile_high, tile_low = split(tile)
            left = jnp.concatenate(
                [
                    jnp.concatenate([high, high], 1),
                    jnp.concatenate([low, jnp.zeros_like(low)], 1),
                ],
                0,
            )
            right = jnp.concatenate([tile_high, tile_low], 1)
            both = lax.dot_general(left, right, NT, preferred_element_type=jnp.float32)
            used = live[k, b].astype(jnp.float32)
            value = (both[:GROUP] + both[GROUP:]) * (-scale * used)
            if k == 0:
                value = value + modes
            slots[b, GROUP * k : GROUP * (k + 1)] = value
            mark = modes[MODES : MODES + 1] * float(GROUP) + base[k, b].astype(jnp.float32)
            marks = jnp.where(place == b * K + k, mark, marks)
        return marks

    marks = lax.fori_loop(0, R, row, jnp.zeros((GROUP, BS), jnp.float32))
    labels[...] = marks
    sent = jnp.zeros((GROUP, BS), jnp.float32)
    for s in range(S):
        b = send[s]
        for k in range(K):
            first = (s * K + k) * MODES
            message[first : first + MODES, :] = slots[b, GROUP * k : GROUP * k + MODES]
            mark = table[source[k, b]][MODES : MODES + 1] * float(GROUP) + base[k, b].astype(
                jnp.float32
            )
            sent = jnp.where(place == s * K + k, mark, sent)
    message[S * K * MODES :, :] = sent


def dense_kernel(labels, slots, prolong, lab, wide, sem):
    wide[...] = labels[...].astype(jnp.int32)
    copy = pltpu.make_async_copy(wide, lab, sem)
    copy.start()
    copy.wait()

    def row(b, carry):
        prolong[b] = jnp.zeros((9 * C, BS), jnp.float32)
        for k in range(K):
            flat = b * K + k
            mark = lab[flat // BS, flat % BS]
            e = mark // (AGG * GROUP)
            window = (e // 5) * 3 + e % 5
            member = (mark // GROUP) % AGG
            first = (window * AGG + member) * MODES
            at = pl.ds(first, MODES)
            prolong[b, at, :] += slots[b, GROUP * k : GROUP * k + MODES]
        return carry

    lax.fori_loop(0, R, row, 0)


def couple_kernel(
    where, source, base, live, tiles, slots, labels, prolong, near, left, right,
    own_out, near_out, far_out, table, marks, lab, stage, parts, weights, total, turned, sem
):
    entry_rows = S * K * MODES
    marks[0:2, :] = labels[0:2, :].astype(jnp.int32)
    for block in range(9):
        ref = (near, left, right)[block // 3]
        marks[block + 2 : block + 3, :] = ref[block % 3, entry_rows : entry_rows + 1, :].astype(
            jnp.int32
        )
    copy = pltpu.make_async_copy(marks, lab, sem)
    copy.start()

    def own_entry(b, carry):
        high, low = split(slots[b])
        table[b, :, 0:BS] = high
        table[b, :, BS:] = low
        return carry

    lax.fori_loop(0, R, own_entry, 0)
    stage[...] = jnp.zeros_like(stage)
    for block in range(1, 9):
        ref = (near, left, right)[block // 3]

        def halo_entry(s, carry, block=block, ref=ref):
            rows = ref[block % 3, pl.ds(pl.multiple_of(s * K * MODES, 8), K * MODES), :]
            for g in range(K):
                stage[GROUP * g : GROUP * g + MODES, :] = rows[MODES * g : MODES * (g + 1)]
            high, low = split(stage[...])
            table[R + block * S + s, :, 0:BS] = high
            table[R + block * S + s, :, BS:] = low
            return carry

        lax.fori_loop(0, S, halo_entry, 0)

    total[...] = jnp.zeros_like(total)
    weights[...] = jnp.zeros_like(weights)
    copy.wait()

    def row(b, carry):
        high, low = split(prolong[b])
        weights[0 : 9 * C, 0:BS] = high
        weights[0 : 9 * C, BS : 2 * BS] = high
        weights[0 : 9 * C, 2 * BS :] = low
        for k in range(K):
            entry = table[source[k, b]]
            high, low = entry[:, :BS], entry[:, BS:]
            lhs = jnp.concatenate(
                [
                    jnp.concatenate([high, high], 1),
                    jnp.concatenate([low, jnp.zeros_like(low)], 1),
                ],
                0,
            )
            tile_high, tile_low = split(tiles[b, k])
            rhs = jnp.concatenate([tile_high, tile_low], 1)
            both = lax.dot_general(lhs, rhs, NT, preferred_element_type=jnp.float32)
            used = live[k, b].astype(jnp.float32)
            value = (both[: K * GROUP] + both[K * GROUP :]) * used
            high, low = split(value)
            parts[K * GROUP * k : K * GROUP * (k + 1), :] = jnp.concatenate([high, low, high], 1)
        product = lax.dot_general(
            parts[...], weights[...], NT, preferred_element_type=jnp.float32
        )
        for k in range(K):
            src = source[k, b]
            major, minor = src // S, (src % S) * K
            shift = base[k, b]
            for g in range(K):
                first = pl.multiple_of(lab[major, minor + g] + shift, GROUP)
                at = (K * k + g) * GROUP
                total[pl.ds(first, GROUP), :] += product[at : at + GROUP]
        return carry

    lax.fori_loop(0, R, row, 0)
    for g in range(25 * AGG):
        turned[MODES * g : MODES * (g + 1), :] = total[GROUP * g : GROUP * g + MODES, :]
    flat = turned[...].T
    even = where[0] == 0
    low, mid, top = (flat[3 * C * i : 3 * C * (i + 1)] for i in range(3))
    own_out[...] = mid
    near_out[...] = jnp.where(even, top, low)
    far_out[...] = jnp.where(even, low, top)


def merge_kernel(where, own, near, far, own_out, near_out, far_out):
    even = where[0] == 0
    span = 5 * C
    low = jnp.where(even, near[...], far[...])
    top = jnp.where(even, far[...], near[...])
    zeros = jnp.zeros((3 * C, span), jnp.float32)
    mid = own[...]
    length = 5 * span
    summed = (
        jnp.concatenate([top[:, :length], zeros, zeros], 1)
        + jnp.concatenate([zeros, mid[:, :length], zeros], 1)
        + jnp.concatenate([zeros, zeros, low[:, :length]], 1)
    )
    even = where[1] == 0
    low, mid, top = (summed[C * i : C * (i + 1)] for i in range(3))
    own_out[...] = mid
    near_out[...] = jnp.where(even, top, low)
    far_out[...] = jnp.where(even, low, top)


def place_kernel(where, own, near, far, coarse):
    even = where[1] == 0
    low = jnp.where(even, near[...], far[...])
    top = jnp.where(even, far[...], near[...])
    mid = own[...]
    zeros = jnp.zeros((C, C), jnp.float32)
    pieces = []
    for u in range(7):
        lanes = slice(5 * C * u, 5 * C * (u + 1))
        pieces.append(
            jnp.concatenate([top[:, lanes], zeros, zeros], 1)
            + jnp.concatenate([zeros, mid[:, lanes], zeros], 1)
            + jnp.concatenate([zeros, zeros, low[:, lanes]], 1)
        )
    coarse[...] = jnp.concatenate(pieces, 1)


def shape(*dims, dtype=jnp.float32):
    return jax.ShapeDtypeStruct(dims, dtype)


def body(operator_tiles, tile_slab, tile_column, tile_live, send_list, aggregate, null_modes):
    tiles = operator_tiles[0, 0]
    slab = tile_slab[0, 0].T
    column = tile_column[0, 0].T
    live = tile_live[0, 0].T
    send = send_list[0, 0]
    wide_odd = lax.axis_index("wide") % 2
    narrow_odd = lax.axis_index("narrow") % 2
    where = jnp.stack([wide_odd, narrow_odd]).astype(jnp.int32)
    down, across = slab // 3 - 1, slab % 3 - 1
    near_down, near_across = 1 - 2 * wide_odd, 1 - 2 * narrow_odd
    row_block = jnp.where(down == 0, 0, jnp.where(down == near_down, 1, 2))
    col_block = jnp.where(across == 0, 0, jnp.where(across == near_across, 1, 2))
    source = jnp.where(slab == 4, column, R + (row_block * 3 + col_block) * S + column)
    base = (5 * (slab // 3) + slab % 3) * (AGG * GROUP)

    own_modes, packed = pl.pallas_call(
        pack_kernel,
        out_shape=(shape(R, GROUP, BS), shape(S, GROUP, BS)),
        in_specs=[SMEM, SMEM, VMEM],
        out_specs=(VMEM, VMEM),
        name="pack",
    )(send, aggregate[0, 0], null_modes[0, 0].transpose(1, 0, 2))
    near, far = pair_halo(packed, "narrow", 0)
    line = jnp.concatenate([packed, near, far], 0)
    near, far = pair_halo(line, "wide", 0)
    table = jnp.concatenate([own_modes, line, near, far], 0)

    slots, labels, message = pl.pallas_call(
        smooth_kernel,
        out_shape=(
            shape(R, K * GROUP, BS),
            shape(GROUP, BS),
            shape(S * K * MODES + GROUP, BS),
        ),
        in_specs=[SMEM] * 4 + [VMEM] * 2,
        out_specs=(VMEM, VMEM, VMEM),
        compiler_params=params(32),
        name="smooth",
    )(send, source, base, live, tiles, table)

    message = message[None]
    near, far = pair_halo(message, "narrow", 0)
    prolong = pl.pallas_call(
        dense_kernel,
        out_shape=shape(R, 9 * C, BS),
        in_specs=[VMEM, VMEM],
        out_specs=VMEM,
        scratch_shapes=[
            pltpu.SMEM((GROUP, BS), jnp.int32),
            pltpu.VMEM((GROUP, BS), jnp.int32),
            pltpu.SemaphoreType.DMA,
        ],
        compiler_params=params(16),
        name="dense",
    )(labels, slots)
    line = jnp.concatenate([message, near, far], 0)
    near, far = pair_halo(line, "wide", 0)

    rows = 3 * C
    lanes = 25 * C
    own, near, far = pl.pallas_call(
        couple_kernel,
        out_shape=(shape(rows, lanes),) * 3,
        in_specs=[SMEM] * 4 + [VMEM] * 7,
        out_specs=(VMEM,) * 3,
        scratch_shapes=[
            pltpu.VMEM((R + 9 * S, K * GROUP, 2 * BS), jnp.bfloat16),
            pltpu.VMEM((16, BS), jnp.int32),
            pltpu.SMEM((16, BS), jnp.int32),
            pltpu.VMEM((K * GROUP, BS), jnp.float32),
            pltpu.VMEM((K * K * GROUP, 3 * BS), jnp.bfloat16),
            pltpu.VMEM((256, 3 * BS), jnp.bfloat16),
            pltpu.VMEM((E_ROWS, 256), jnp.float32),
            pltpu.VMEM((25 * C, 256), jnp.float32),
            pltpu.SemaphoreType.DMA,
        ],
        compiler_params=params(48),
        name="couple",
    )(where, source, base, live, tiles, slots, labels, prolong, line, near, far)

    size = lax.axis_size("wide")
    pairs = [(i, i ^ 1) for i in range(size)]
    far_pairs = [(i, i + 1) if i % 2 else (i, i - 1) for i in range(1, size - 1)]
    near, far = lax.ppermute(near, "wide", pairs), lax.ppermute(far, "wide", far_pairs)
    own, near, far = pl.pallas_call(
        merge_kernel,
        out_shape=(shape(C, 35 * C),) * 3,
        in_specs=[SMEM] + [VMEM] * 3,
        out_specs=(VMEM,) * 3,
        name="merge",
    )(where, own, near, far)
    size = lax.axis_size("narrow")
    pairs = [(i, i ^ 1) for i in range(size)]
    far_pairs = [(i, i + 1) if i % 2 else (i, i - 1) for i in range(1, size - 1)]
    near, far = lax.ppermute(near, "narrow", pairs), lax.ppermute(far, "narrow", far_pairs)
    coarse = pl.pallas_call(
        place_kernel,
        out_shape=shape(C, 49 * C),
        in_specs=[SMEM] + [VMEM] * 3,
        out_specs=VMEM,
        name="place",
    )(where, own, near, far)
    return prolong[None, None], coarse[None, None]


def solution(mesh):
    in_specs = (
        P("wide", "narrow", None, None, None, None),
        P("wide", "narrow", None, None),
        P("wide", "narrow", None, None),
        P("wide", "narrow", None, None),
        P("wide", "narrow", None),
        P("wide", "narrow", None),
        P("wide", "narrow", None, None, None),
    )
    out_specs = (P("wide", "narrow", None, None, None), P("wide", "narrow", None, None))
    return jax.shard_map(body, mesh=mesh, in_specs=in_specs, out_specs=out_specs, check_vma=False)
```

time: 553 us -> 120 us (0.22); the launches traced: 543 us -> 119 us
  matrix products: 172 us -> 0 us
  local copies, waits for them, and re-layouts: 155 us -> 9.57 us
  waiting for transfers between devices: 142 us -> 28.3 us
  Pallas kernels: 0 us -> 54.8 us
  other arithmetic: 31.7 us -> 0.91 us
  starting transfers between devices: 41.4 us -> 24.7 us
    dot_general x7 -> x0, matrix products: 172 us -> none  [the longest x1 52.4 us: couple(): jnp.einsum('rkfcj,rkij->rkfci', operand, tiles_dev, precision=HIGH)]
    ppermute x12, waiting for transfers between devices: 142 us -> 28.3 us  [the longest x8 21.5 us: pair_halo(): return (lax.ppermute(block, axis, near), lax.ppermute(block, axis, far))]
    gather x6 -> x0, local copies, waits for them, and re-layouts: 76.3 us -> none  [the longest x2 68.1 us: couple(): operand = lookup[source_row]]
    pallas_call x0 -> x6, Pallas kernels: none -> 54.8 us  [the longest x1 31.2 us: body(): pl.pallas_call(couple_kernel, out_shape=(shape(rows, lanes),) * 3, in_spe...]
    unnamed x27 -> x22, local copies, waits for them, and re-layouts: 39.1 us -> 9.54 us
    concatenate x7 -> x1, other arithmetic: 26.6 us -> 0.1 us  [body(): line = jnp.concatenate([message, near, far], 0)]
    ppermute x12, starting transfers between devices: 41.4 us -> 24.7 us  [the longest x8 15.7 us: pair_halo(): return (lax.ppermute(block, axis, near), lax.ppermute(block, axis, far))]
    ppermute x4 -> x0, local copies, waits for them, and re-layouts: 11.4 us -> none  [the longest x2 5.7 us: with_halo(): after = lax.ppermute(leading, axis, down)]
  transfers between devices with their start and end apart: 12 -> 12, of which waited for: 6 -> 9; matrix products, arithmetic and copies ran while one was open for 13% -> 2% of each run, Pallas kernels for 0% -> 7%
where the time goes in v1:
time: 120 us; the launch traced here: 119 us
  Pallas kernels  54.8 us (46%)
  waiting for transfers between devices  28.3 us (24%)
  starting transfers between devices  24.7 us (21%)
  local copies, waits for them, and re-layouts  9.57 us (8%)
    pallas_call x1, Pallas kernels, body(): pl.pallas_call(couple_kernel, out_shape=(shape(rows, lanes),) * 3, in_spe...  31.2 us
    ppermute x8, waiting for transfers between devices, pair_halo(): return (lax.ppermute(block, axis, near), lax.ppermute(block, axis, far))  21.5 us
    ppermute x8, starting transfers between devices, pair_halo(): return (lax.ppermute(block, axis, near), lax.ppermute(block, axis, far))  15.7 us
    unnamed x22, local copies, waits for them, and re-layouts  9.54 us
    pallas_call x1, Pallas kernels, body(): pl.pallas_call(smooth_kernel, out_shape=(shape(R, K * GROUP, BS), shape(G...  9.25 us
    pallas_call x1, Pallas kernels, body(): pl.pallas_call(dense_kernel, out_shape=shape(R, 9 * C, BS), in_specs=[VME...  8.75 us
    ppermute x1, starting transfers between devices, body(): lax.ppermute(far, 'wide', far_pairs)  5.23 us
    ppermute x1, waiting for transfers between devices, body(): lax.ppermute(far, 'wide', far_pairs)  3.69 us
  transfers between devices with their start and end apart: 12, of which 9 were waited for; matrix products, arithmetic and copies ran while one was open for 2% of the time, Pallas kernels for 7%

profile of v1, /device:TPU:14, one launch (start us, length us, event | category | flops | bytes accessed | tf_op | source)
XLA Modules:
  0.0 119.1 jit_solution(12696443082066063536)
XLA Ops:
  0.6 0.0 copy-start.4
  0.6 0.0 copy-start.2
  0.7 1.7 %pack.1 = (f32[32,8,128]{2,1,0:T(8,128)}, f32[16,8,128]{2,1,0:T(8,128)}) custom-call(s32[16]{0:T(128)} %bitcast.71, s32[32]{0:T(128)} %bitcast.76, f32[6,32,128]{2,1,0:T(8,128)} %bitcast.75), custom_call_target="tpu_custom_call" | custom-call | tf_op jit(solution)/shard_map/pack/pallas_call | solution.py:267
  2.3 3.5 %collective-permute-start.1 = (f32[16,8,128]{2,1,0:T(8,128)}, f32[16,8,128]{2,1,0:T(8,128)S(1)}, u32[]{:S(2)}, u32[]{:S(2)}) collective-permute-start(f32[16,8,128]{2,1,0:T(8,128)} %get-tuple-element.14), channel_id=1, source_target_pairs={{1,2},{2,1},{5,6},{6,5},{9,10},{10,9},{13,14},{14,13},{17,18},{18,... | collective-permute-start | bytes 196616 | tf_op jit(solution)/shard_map/ppermute | solution.py:38
  5.8 0.1 collective-permute-start
  5.9 0.9 constant_dynamic-update-slice_fusion.8
  6.8 0.9 constant_dynamic-update-slice_fusion.2
  7.7 2.7 %collective-permute-done = f32[16,8,128]{2,1,0:T(8,128)S(1)} collective-permute-done((f32[16,8,128]{2,1,0:T(8,128)}, f32[16,8,128]{2,1,0:T(8,128)S(1)}, u32[]{:S(2)}, u32[]{:S(2)}) %collective-permute-start) | collective-permute-done | bytes 65568 | tf_op jit(solution)/shard_map/ppermute | solution.py:38
  10.4 0.0 collective-permute-done.1
  10.4 4.3 %collective-permute-start.3 = (f32[48,8,128]{2,1,0:T(8,128)S(1)}, f32[48,8,128]{2,1,0:T(8,128)S(1)}, u32[]{:S(2)}, u32[]{:S(2)}) collective-permute-start(f32[48,8,128]{2,1,0:T(8,128)S(1)} %get-tuple-element.24), channel_id=1, source_target_pairs={{4,8},{8,4},{12,16},{16,12},{20,24},{24,20},{28,32},{32,28},{36,40... | collective-permute-start | bytes 589832 | tf_op jit(solution)/shard_map/ppermute | solution.py:38
  14.7 0.1 collective-permute-start.2
  14.8 0.7 add_multiply_fusion
  15.5 0.7 collective-permute-done.2
  16.2 3.3 %collective-permute-done.3 = f32[48,8,128]{2,1,0:T(8,128)S(1)} collective-permute-done((f32[48,8,128]{2,1,0:T(8,128)S(1)}, f32[48,8,128]{2,1,0:T(8,128)S(1)}, u32[]{:S(2)}, u32[]{:S(2)}) %collective-permute-start.3) | collective-permute-done | bytes 196640 | tf_op jit(solution)/shard_map/ppermute | solution.py:38
  19.5 0.0 copy-done.4
  19.5 0.0 copy-done.2
  19.5 0.0 copy-start
  19.6 5.8 %copy-done = f32[1,1,32,8,128,128]{5,4,3,2,1,0:T(8,128)S(1)} copy-done((f32[1,1,32,8,128,128]{5,4,3,2,1,0:T(8,128)S(1)}, f32[1,1,32,8,128,128]{5,4,3,2,1,0:T(8,128)}, u32[]{:S(2)}) %copy-start) | copy-done | bytes 16777240
  25.3 9.3 %smooth.1 = (f32[32,64,128]{2,1,0:T(8,128)S(1)}, f32[8,128]{1,0:T(8,128)S(1)}, f32[776,128]{1,0:T(8,128)S(1)}) custom-call(s32[16]{0:T(128)S(1)} %bitcast.72, s32[8,32]{1,0:T(8,128)S(1)} %get-tuple-element.31.source, s32[8,32]{1,0:T(8,128)S(1)} %get-tuple-element.30.base, s32[8,32]{1,0:T(8,128)S(1)} %bitcast.69, f32[32,8,128,128]{3,2,1,0:T(8,128)S(1)} %bitcast.65, ...), custom_call_target="tpu_custom_call" | custom-call | tf_op jit(solution)/shard_map/smooth/pallas_call | solution.py:279
  34.6 2.4 %collective-permute-start.5 = (f32[1,776,128]{2,1,0:T(8,128)S(1)}, f32[1,776,128]{2,1,0:T(8,128)S(1)}, u32[]{:S(2)}, u32[]{:S(2)}) collective-permute-start(f32[1,776,128]{2,1,0:T(8,128)S(1)} %bitcast.66), channel_id=1, source_target_pairs={{1,2},{2,1},{5,6},{6,5},{9,10},{10,9},{13,14},{14,13},{17,18},{18,... | collective-permute-start | bytes 1191944 | tf_op jit(solution)/shard_map/ppermute | solution.py:38
  37.0 0.1 collective-permute-start.4
  37.0 9.0 %collective-permute-done.5 = f32[1,776,128]{2,1,0:T(8,128)S(1)} collective-permute-done((f32[1,776,128]{2,1,0:T(8,128)S(1)}, f32[1,776,128]{2,1,0:T(8,128)S(1)}, u32[]{:S(2)}, u32[]{:S(2)}) %collective-permute-start.5) | collective-permute-done | bytes 397344 | tf_op jit(solution)/shard_map/ppermute | solution.py:38
  46.1 0.3 collective-permute-done.4
  46.3 0.1 pad_maximum_fusion.near
  46.4 5.3 %collective-permute-start.7 = (f32[3,776,128]{2,1,0:T(8,128)S(1)}, f32[3,776,128]{2,1,0:T(8,128)S(1)}, u32[]{:S(2)}, u32[]{:S(2)}) collective-permute-start(f32[3,776,128]{2,1,0:T(8,128)S(1)} %pad_maximum_fusion.near), channel_id=1, source_target_pairs={{4,8},{8,4},{12,16},{16,12},{20,24},{24,20},{28,32},{32,28},{36,40... | collective-permute-start | bytes 3575816 | tf_op jit(solution)/shard_map/ppermute | solution.py:38
  51.7 0.1 collective-permute-start.6
  51.8 0.1 pad_add_fusion.where
  51.9 8.8 %dense.1.prolong = f32[32,216,128]{2,1,0:T(8,128)} custom-call(f32[8,128]{1,0:T(8,128)S(1)} %get-tuple-element.15.labels, f32[32,64,128]{2,1,0:T(8,128)S(1)} %get-tuple-element.16.slots), custom_call_target="tpu_custom_call" | custom-call | tf_op jit(solution)/shard_map/dense/pallas_call | solution.py:294
  60.7 5.6 %collective-permute-done.7.right = f32[3,776,128]{2,1,0:T(8,128)S(1)} collective-permute-done((f32[3,776,128]{2,1,0:T(8,128)S(1)}, f32[3,776,128]{2,1,0:T(8,128)S(1)}, u32[]{:S(2)}, u32[]{:S(2)}) %collective-permute-start.7) | collective-permute-done | bytes 1191968 | tf_op jit(solution)/shard_map/ppermute | solution.py:38
  66.2 0.0 collective-permute-done.6.left
  66.2 0.0 copy-done.3
  66.2 31.2 %couple.1 = (f32[72,600]{1,0:T(8,128)S(1)}, f32[72,600]{1,0:T(8,128)S(1)}, f32[72,600]{1,0:T(8,128)S(1)}) custom-call(s32[2]{0:T(128)S(1)} %pad_add_fusion.where, s32[8,32]{1,0:T(8,128)S(1)} %get-tuple-element.31.source, s32[8,32]{1,0:T(8,128)S(1)} %get-tuple-element.30.base, s32[8,32]{1,0:T(8,128)S(1)} %bitcast.70, f32[32,8,128,128]{3,2,1,0:T(8,128)} %bitcast.64, ...), custom_call_target="tpu_custom_call" | custom-call | tf_op jit(solution)/shard_map/couple/pallas_call | solution.py:312
  97.5 0.0 copy-start.1
  97.5 0.7 copy-done.1
  98.1 0.0 collective-permute-start.8
  98.2 5.2 %collective-permute-start.9 = (f32[72,600]{1,0:T(8,128)S(1)}, f32[72,600]{1,0:T(8,128)S(1)}, u32[]{:S(2)}, u32[]{:S(2)}) collective-permute-start(f32[72,600]{1,0:T(8,128)S(1)} %get-tuple-element.20), channel_id=1, source_target_pairs={{4,8},{8,4},{12,16},{16,12},{20,24},{24,20},{28,32},{32,28},{36,40... | collective-permute-start | bytes 518408 | tf_op jit(solution)/shard_map/ppermute | solution.py:335
  103.4 0.0 collective-permute-done.8.near
  103.4 0.0 copy-start.5
  103.4 3.7 %collective-permute-done.9.far = f32[72,600]{1,0:T(8,128)S(1)} collective-permute-done((f32[72,600]{1,0:T(8,128)S(1)}, f32[72,600]{1,0:T(8,128)S(1)}, u32[]{:S(2)}, u32[]{:S(2)}) %collective-permute-start.9) | collective-permute-done | bytes 172832 | tf_op jit(solution)/shard_map/ppermute | solution.py:335
  107.1 0.0 copy-done.5
  107.1 0.7 copy-done.6
  107.8 1.9 %merge.1 = (f32[24,840]{1,0:T(8,128)}, f32[24,840]{1,0:T(8,128)}, f32[24,840]{1,0:T(8,128)}) custom-call(s32[2]{0:T(128)} %copy-done.3, f32[72,600]{1,0:T(8,128)} %copy-done.1, f32[72,600]{1,0:T(8,128)} %copy-done.5, f32[72,600]{1,0:T(8,128)} %copy-done.6), custom_call_target="tpu_custom_call" | custom-call | tf_op jit(solution)/shard_map/merge/pallas_call | solution.py:336
  109.7 0.3 collective-permute-start.10
  110.0 3.5 %collective-permute-start.11 = (f32[24,840]{1,0:T(8,128)}, f32[24,840]{1,0:T(8,128)S(1)}, u32[]{:S(2)}, u32[]{:S(2)}) collective-permute-start(f32[24,840]{1,0:T(8,128)} %get-tuple-element.23), channel_id=1, source_target_pairs={{1,2},{2,1},{5,6},{6,5},{9,10},{10,9},{13,14},{14,13},{17,18},{18,... | collective-permute-start | bytes 241928 | tf_op jit(solution)/shard_map/ppermute | solution.py:346
  113.5 0.9 collective-permute-done.10.near
  114.4 2.1 %collective-permute-done.11.far = f32[24,840]{1,0:T(8,128)S(1)} collective-permute-done((f32[24,840]{1,0:T(8,128)}, f32[24,840]{1,0:T(8,128)S(1)}, u32[]{:S(2)}, u32[]{:S(2)}) %collective-permute-start.11) | collective-permute-done | bytes 80672 | tf_op jit(solution)/shard_map/ppermute | solution.py:346
  116.6 0.6 copy-done.8
  117.2 1.9 %place.1 = f32[24,1176]{1,0:T(8,128)} custom-call(s32[2]{0:T(128)} %copy-done.3, f32[24,840]{1,0:T(8,128)} %get-tuple-element.21.own, f32[24,840]{1,0:T(8,128)} %copy-done.7, f32[24,840]{1,0:T(8,128)} %copy-done.8), custom_call_target="tpu_custom_call" | custom-call | tf_op jit(solution)/shard_map/place/pallas_call | solution.py:347
  (9 shorter events, 0.1 us)
Async XLA Ops:
  0.6 18.9 %copy-start.4 = (s32[1,1,16]{2,1,0:T(1,128)S(1)}, s32[1,1,16]{2,1,0:T(1,128)}, u32[]{:S(2)}) copy-start(s32[1,1,16]{2,1,0:T(1,128)} %param.11) | copy-start | bytes 196
  0.6 18.9 %copy-start.2 = (s32[1,1,32,8]{2,3,1,0:T(8,128)S(1)}, s32[1,1,32,8]{2,3,1,0:T(8,128)}, u32[]{:S(2)}) copy-start(s32[1,1,32,8]{2,3,1,0:T(8,128)} %param.10) | copy-start | bytes 3076
  2.3 8.1 %collective-permute-start.1 = (f32[16,8,128]{2,1,0:T(8,128)}, f32[16,8,128]{2,1,0:T(8,128)S(1)}, u32[]{:S(2)}, u32[]{:S(2)}) collective-permute-start(f32[16,8,128]{2,1,0:T(8,128)} %get-tuple-element.14), channel_id=1, source_target_pairs={{1,2},{2,1},{5,6},{6,5},{9,10},{10,9},{13,14},{14,13},{17,18},{18,... | collective-permute-start | bytes 196616 | tf_op jit(solution)/shard_map/ppermute | solution.py:38
  5.8 4.6 %collective-permute-start = (f32[16,8,128]{2,1,0:T(8,128)}, f32[16,8,128]{2,1,0:T(8,128)S(1)}, u32[]{:S(2)}, u32[]{:S(2)}) collective-permute-start(f32[16,8,128]{2,1,0:T(8,128)} %get-tuple-element.14), channel_id=1, source_target_pairs={{0,1},{1,0},{2,3},{3,2},{4,5},{5,4},{6,7},{7,6},{8,9},{9,8},{10,11... | collective-permute-start | bytes 196616 | tf_op jit(solution)/shard_map/ppermute | solution.py:38
  10.4 9.1 %collective-permute-start.3 = (f32[48,8,128]{2,1,0:T(8,128)S(1)}, f32[48,8,128]{2,1,0:T(8,128)S(1)}, u32[]{:S(2)}, u32[]{:S(2)}) collective-permute-start(f32[48,8,128]{2,1,0:T(8,128)S(1)} %get-tuple-element.24), channel_id=1, source_target_pairs={{4,8},{8,4},{12,16},{16,12},{20,24},{24,20},{28,32},{32,28},{36,40... | collective-permute-start | bytes 589832 | tf_op jit(solution)/shard_map/ppermute | solution.py:38
  14.7 1.5 %collective-permute-start.2 = (f32[48,8,128]{2,1,0:T(8,128)S(1)}, f32[48,8,128]{2,1,0:T(8,128)S(1)}, u32[]{:S(2)}, u32[]{:S(2)}) collective-permute-start(f32[48,8,128]{2,1,0:T(8,128)S(1)} %get-tuple-element.24), channel_id=1, source_target_pairs={{0,4},{4,0},{8,12},{12,8},{16,20},{20,16},{24,28},{28,24},{32,36},... | collective-permute-start | bytes 589832 | tf_op jit(solution)/shard_map/ppermute | solution.py:38
  19.5 5.8 %copy-start = (f32[1,1,32,8,128,128]{5,4,3,2,1,0:T(8,128)S(1)}, f32[1,1,32,8,128,128]{5,4,3,2,1,0:T(8,128)}, u32[]{:S(2)}) copy-start(f32[1,1,32,8,128,128]{5,4,3,2,1,0:T(8,128)} %param.7) | copy-start | bytes 50331652
  34.6 11.5 %collective-permute-start.5 = (f32[1,776,128]{2,1,0:T(8,128)S(1)}, f32[1,776,128]{2,1,0:T(8,128)S(1)}, u32[]{:S(2)}, u32[]{:S(2)}) collective-permute-start(f32[1,776,128]{2,1,0:T(8,128)S(1)} %bitcast.66), channel_id=1, source_target_pairs={{1,2},{2,1},{5,6},{6,5},{9,10},{10,9},{13,14},{14,13},{17,18},{18,... | collective-permute-start | bytes 1191944 | tf_op jit(solution)/shard_map/ppermute | solution.py:38
  37.0 9.4 %collective-permute-start.4 = (f32[1,776,128]{2,1,0:T(8,128)S(1)}, f32[1,776,128]{2,1,0:T(8,128)S(1)}, u32[]{:S(2)}, u32[]{:S(2)}) collective-permute-start(f32[1,776,128]{2,1,0:T(8,128)S(1)} %bitcast.67), channel_id=1, source_target_pairs={{0,1},{1,0},{2,3},{3,2},{4,5},{5,4},{6,7},{7,6},{8,9},{9,8},{10,11... | collective-permute-start | bytes 1191944 | tf_op jit(solution)/shard_map/ppermute | solution.py:38
  46.4 19.8 %collective-permute-start.7 = (f32[3,776,128]{2,1,0:T(8,128)S(1)}, f32[3,776,128]{2,1,0:T(8,128)S(1)}, u32[]{:S(2)}, u32[]{:S(2)}) collective-permute-start(f32[3,776,128]{2,1,0:T(8,128)S(1)} %pad_maximum_fusion.near), channel_id=1, source_target_pairs={{4,8},{8,4},{12,16},{16,12},{20,24},{24,20},{28,32},{32,28},{36,40... | collective-permute-start | bytes 3575816 | tf_op jit(solution)/shard_map/ppermute | solution.py:38
  51.7 14.5 %collective-permute-start.6 = (f32[3,776,128]{2,1,0:T(8,128)S(1)}, f32[3,776,128]{2,1,0:T(8,128)S(1)}, u32[]{:S(2)}, u32[]{:S(2)}) collective-permute-start(f32[3,776,128]{2,1,0:T(8,128)S(1)} %pad_maximum_fusion.near), channel_id=1, source_target_pairs={{0,4},{4,0},{8,12},{12,8},{16,20},{20,16},{24,28},{28,24},{32,36},... | collective-permute-start | bytes 3575816 | tf_op jit(solution)/shard_map/ppermute | solution.py:38
  51.9 14.3 %copy-start.3 = (s32[2]{0:T(128)}, s32[2]{0:T(128)S(1)}, u32[]{:S(2)}) copy-start(s32[2]{0:T(128)S(1)} %pad_add_fusion.where) | copy-start | bytes 28
  97.5 0.7 copy-start.1
  98.1 5.2 %collective-permute-start.8 = (f32[72,600]{1,0:T(8,128)S(1)}, f32[72,600]{1,0:T(8,128)S(1)}, u32[]{:S(2)}, u32[]{:S(2)}) collective-permute-start(f32[72,600]{1,0:T(8,128)S(1)} %get-tuple-element.19), channel_id=1, source_target_pairs={{0,4},{4,0},{8,12},{12,8},{16,20},{20,16},{24,28},{28,24},{32,36},... | collective-permute-start | bytes 518408 | tf_op jit(solution)/shard_map/ppermute | solution.py:335
  98.2 9.0 %collective-permute-start.9 = (f32[72,600]{1,0:T(8,128)S(1)}, f32[72,600]{1,0:T(8,128)S(1)}, u32[]{:S(2)}, u32[]{:S(2)}) collective-permute-start(f32[72,600]{1,0:T(8,128)S(1)} %get-tuple-element.20), channel_id=1, source_target_pairs={{4,8},{8,4},{12,16},{16,12},{20,24},{24,20},{28,32},{32,28},{36,40... | collective-permute-start | bytes 518408 | tf_op jit(solution)/shard_map/ppermute | solution.py:335
  103.4 3.7 %copy-start.5 = (f32[72,600]{1,0:T(8,128)}, f32[72,600]{1,0:T(8,128)S(1)}, u32[]{:S(2)}) copy-start(f32[72,600]{1,0:T(8,128)S(1)} %collective-permute-done.8.near) | copy-start | bytes 518404
  107.1 0.7 copy-start.6
  109.7 4.7 %collective-permute-start.10 = (f32[24,840]{1,0:T(8,128)}, f32[24,840]{1,0:T(8,128)S(1)}, u32[]{:S(2)}, u32[]{:S(2)}) collective-permute-start(f32[24,840]{1,0:T(8,128)} %get-tuple-element.22), channel_id=1, source_target_pairs={{0,1},{1,0},{2,3},{3,2},{4,5},{5,4},{6,7},{7,6},{8,9},{9,8},{10,11... | collective-permute-start | bytes 241928 | tf_op jit(solution)/shard_map/ppermute | solution.py:346
  110.0 6.6 %collective-permute-start.11 = (f32[24,840]{1,0:T(8,128)}, f32[24,840]{1,0:T(8,128)S(1)}, u32[]{:S(2)}, u32[]{:S(2)}) collective-permute-start(f32[24,840]{1,0:T(8,128)} %get-tuple-element.23), channel_id=1, source_target_pairs={{1,2},{2,1},{5,6},{6,5},{9,10},{10,9},{13,14},{14,13},{17,18},{18,... | collective-permute-start | bytes 241928 | tf_op jit(solution)/shard_map/ppermute | solution.py:346
  114.4 2.1 %copy-start.7 = (f32[24,840]{1,0:T(8,128)}, f32[24,840]{1,0:T(8,128)S(1)}, u32[]{:S(2)}) copy-start(f32[24,840]{1,0:T(8,128)S(1)} %collective-permute-done.10.near) | copy-start | bytes 241924
  116.6 0.6 copy-start.8

commit v2 on v1

v2 whole, which is shorter than its diff:
```python
import functools

import jax
import jax.numpy as jnp
from jax import lax
from jax.experimental import pallas as pl
from jax.experimental.pallas import tpu as pltpu
from jax.sharding import PartitionSpec as P

MODES = 6
GROUP = 8
AGG = 4
BS = 128
R = 32
K = 8
S = 16
C = 24
OMEGA = 0.7
UNROLL = 16
BLOCK = S * K * MODES + GROUP
T_ENTRIES = R + 8 * S
NT = (((1,), (1,)), ((), ()))
VMEM = pl.BlockSpec(memory_space=pltpu.VMEM)
SMEM = pl.BlockSpec(memory_space=pltpu.SMEM)
HBM = pl.BlockSpec(memory_space=pltpu.HBM)


def params(mib):
    return pltpu.CompilerParams(vmem_limit_bytes=mib * 2**20)


def split(value):
    high = value.astype(jnp.bfloat16)
    return high, (value - high.astype(jnp.float32)).astype(jnp.bfloat16)


def pair_halo(block, axis, dim):
    size = lax.axis_size(axis)
    near = [(i, i ^ 1) for i in range(size)]
    far = [(i, i + 1) if i % 2 else (i, i - 1) for i in range(1, size - 1)]
    return lax.ppermute(block, axis, near), lax.ppermute(block, axis, far)


def pack_kernel(send_hbm, aggregate_hbm, modes_hbm, own, message, send, aggregate, modes, sems):
    copies = [
        pltpu.make_async_copy(source, target, sems.at[i])
        for i, (source, target) in enumerate(
            ((modes_hbm, modes), (aggregate_hbm, aggregate), (send_hbm, send))
        )
    ]
    for copy in copies:
        copy.start()
    for copy in copies:
        copy.wait()
    for b in range(R):
        for m in range(MODES):
            own[b, m] = modes[m, b]
        own[b, MODES] = jnp.full((BS,), aggregate[b].astype(jnp.float32))
        own[b, MODES + 1] = jnp.zeros((BS,), jnp.float32)
    for s in range(S):
        message[s] = own[send[s]]


def pair_rows(high, low):
    zero = jnp.zeros_like(low)
    return jnp.concatenate(
        [jnp.concatenate([high, high], 1), jnp.concatenate([low, zero], 1)], 0
    )


def times_tile(value, tile):
    length = value.shape[0]
    both = lax.dot_general(
        pair_rows(*split(value)),
        jnp.concatenate(split(tile), 1),
        NT,
        preferred_element_type=jnp.float32,
    )
    return both[:length] + both[length:]


def scale_of(tile):
    eye = lax.broadcasted_iota(jnp.int32, (BS, BS), 0) == lax.broadcasted_iota(
        jnp.int32, (BS, BS), 1
    )
    diagonal = jnp.sum(jnp.where(eye, tile, 0.0), axis=0, keepdims=True)
    return jnp.broadcast_to(-OMEGA / diagonal, (GROUP, BS))


def member_marks(ints, table):
    source = (ints[0:K, :] >> 8) & 255

    def some(i, marks):
        for j in range(8):
            at = i * 8 + j
            marks = jnp.where(source == at, table[at, MODES : MODES + 1, :], marks)
        return marks

    return lax.fori_loop(0, T_ENTRIES // 8, some, jnp.zeros((K, BS), jnp.float32))


def coarse_marks(ints, members):
    return members + (((ints[0:K, :] >> 16) & 31) * AGG).astype(jnp.float32)


def live_of(entry):
    return (((entry >> 21) & 3) != 0).astype(jnp.int32)


def fetch(tiles, entry, taken, at, sems):
    return pltpu.make_async_copy(tiles.at[entry & 255], taken.at[at], sems.at[at])


def start_tiles(rows, scalars, tiles, work, taken, sems):
    for s in range(S):
        work[s] = scalars[0, rows(s)]
        fetch(tiles, work[s], taken, s, sems).start()

    def row(s, count):
        b = rows(s)
        for k in range(1, K):
            entry = scalars[k, b]
            work[count] = entry
            live = live_of(entry)

            @pl.when(live != 0)
            def _(entry=entry, count=count):
                fetch(tiles, entry, taken, count, sems).start()

            count = count + live
        return count

    return lax.fori_loop(0, S, row, S)


def smooth_tiles(count, tiles, table, slots, scale, work, taken, sems):
    for s in range(S):
        fetch(tiles, work[s], taken, s, sems).wait()
    for s in range(S):
        entry = work[s]
        at = entry & 255
        tile = taken[s]
        modes = table[(entry >> 8) & 255]
        factor = scale_of(tile)
        scale[at // K] = factor
        slots[at] = times_tile(modes, tile) * factor + modes

    def some(i, carry):
        for j in range(UNROLL):
            at = i * UNROLL + j

            @pl.when(at < count)
            def _(at=at):
                fetch(tiles, work[at], taken, at, sems).wait()

        for j in range(UNROLL):
            place = jnp.minimum(i * UNROLL + j, count - 1)
            entry = work[place]
            at = entry & 255
            value = times_tile(table[(entry >> 8) & 255], taken[place])
            slots[at] = value * scale[at // K]
        return carry

    lax.fori_loop(1, (count + UNROLL - 1) // UNROLL, some, 0)


def offer_kernel(scalars, ints, tiles, table, slots, message, scale, work, taken, sems):
    count = start_tiles(lambda s: scalars[K, s], scalars, tiles, work, taken, sems)
    slots[...] = jnp.zeros_like(slots)
    marks = coarse_marks(ints, member_marks(ints, table))
    chosen = lax.broadcasted_iota(jnp.int32, (BS, BS), 0) == ints[K : K + 1, :]
    message[S * K * MODES :, :] = jnp.dot(
        marks, chosen.astype(jnp.float32), preferred_element_type=jnp.float32
    )
    smooth_tiles(count, tiles, table, slots, scale, work, taken, sems)
    for s in range(S):
        b = scalars[K, s]
        for k in range(K):
            first = (s * K + k) * MODES
            message[first : first + MODES, :] = slots[b * K + k, :MODES]


def rest_kernel(
    scalars, ints, tiles, table, begun, prolong_hbm, blocks, weights,
    prolong, slots, scale, work, rest, flags, marks, lab, dense_even, dense_odd, taken, sem, sems, tile_sems
):
    for b in range(R):
        flags[b] = 0
    for s in range(S):
        flags[scalars[K, s]] = 1
    count = 0
    for b in range(R):
        rest[count] = b
        count = count + 1 - flags[b]
    count = start_tiles(lambda s: rest[s], scalars, tiles, work, taken, tile_sems)
    members = member_marks(ints, table)
    coarse = coarse_marks(ints, members)
    blocks[S * K * MODES : BLOCK, :] = coarse
    blocks[BLOCK + S * K * MODES :, :] = jnp.concatenate([coarse[:, S:], coarse[:, :S]], 1)
    marks[...] = members.astype(jnp.int32) + ((ints[0:K, :] >> 23) & 15) * AGG
    copy = pltpu.make_async_copy(marks, lab, sem)
    copy.start()
    slots[...] = begun[...]
    smooth_tiles(count, tiles, table, slots, scale, work, taken, tile_sems)
    copy.wait()

    def send_row(b):
        return pltpu.make_async_copy(prolong.at[b], prolong_hbm.at[b], sems.at[b])

    def rows(i, carry):
        for j, dense in enumerate((dense_even, dense_odd)):
            b = i * 2 + j
            dense[...] = jnp.zeros_like(dense)
            for k in range(K):
                dense[lab[k, b]] += slots[b * K + k]
            for g in range(9 * AGG):
                prolong[b, MODES * g : MODES * (g + 1), :] = dense[g, :MODES]
            block, place = b // S, b % S
            start = pl.multiple_of(block * BLOCK + place * K * MODES, GROUP)
            own = jnp.concatenate([slots[b * K + k, :MODES] for k in range(K)], 0)
            blocks[pl.ds(start, K * MODES), :] = own
            high, low = split(prolong[b])
            weights[b, 0 : 9 * C, 0:BS] = high
            weights[b, 0 : 9 * C, BS:] = low
        for j in range(2):
            send_row(i * 2 + j).start()
        return carry

    lax.fori_loop(0, R // 2, rows, 0)

    def finish(b, carry):
        send_row(b).wait()
        return carry

    lax.fori_loop(0, R, finish, 0)


def couple_tiles(
    kind, first_block, scalars, tiles, weights, table, marks, lab, work, parts, products, total, sem
):
    for i in range(table.shape[0] // BLOCK):
        first = i * BLOCK + S * K * MODES
        marks[i * K : (i + 1) * K, :] = table[first : first + K, :].astype(jnp.int32)
    copy = pltpu.make_async_copy(marks, lab, sem)
    copy.start()
    dummy = (25 << 16) + (first_block * S << 8)
    ahead = 2 * UNROLL
    for j in range(ahead):
        work[j] = dummy

    def row(b, count):
        for k in range(K):
            entry = scalars[k, b]
            work[count] = entry
            count = count + (((entry >> 21) & 3) == kind).astype(jnp.int32)
        work[count] = dummy + b * K
        return count + (count & 1)

    count = lax.fori_loop(0, R, row, ahead)
    for j in range(3 * UNROLL):
        work[count + j] = dummy
    length = K * MODES
    copy.wait()

    def step(i, carry):
        start = i * UNROLL
        for j in range(UNROLL):
            entry = work[start + j]
            source = (entry >> 8) & 255
            shift = ((entry >> 16) & 31) * AGG
            major, minor = ((source >> 4) - first_block) * K, source & 15
            for g in range(K):
                at = (K * j + g) * MODES
                total[lab[major + g, minor] + shift] += products[at : at + GROUP, :]
        for j in range(0, UNROLL, 2):
            b = (work[start + UNROLL + j] & 255) // K
            both = weights[b]
            at = slice(j * length, (j + 2) * length)
            products[at, :] = lax.dot_general(
                parts[at, :],
                jnp.concatenate([both[:, :BS], both], 1),
                NT,
                preferred_element_type=jnp.float32,
            )
        for j in range(UNROLL):
            entry = work[start + ahead + j]
            source = (entry >> 8) & 255
            first = ((source >> 4) - first_block) * BLOCK + (source & 15) * length
            rows = table[pl.ds(pl.multiple_of(first, GROUP), length), :]
            high, low = split(times_tile(rows, tiles[entry & 255]))
            parts[length * j : length * (j + 1), :] = jnp.concatenate([high, low, high], 1)
        return carry

    lax.fori_loop(0, (count - ahead + UNROLL - 1) // UNROLL + 2, step, 0)


def beside_kernel(
    scalars, tiles, weights, table, out, marks, lab, work, parts, products, total, sem
):
    total[0 : 25 * AGG] = jnp.zeros((25 * AGG, GROUP, 256), jnp.float32)
    couple_tiles(
        1, 0, scalars, tiles, weights, table, marks, lab, work, parts, products, total, sem
    )
    out[...] = total[0 : 25 * AGG]


def corner_kernel(
    scalars, tiles, weights, begun, table, own_out, near_out, far_out,
    marks, lab, work, parts, products, total, turned, sem
):
    total[0 : 25 * AGG] = begun[...]
    couple_tiles(
        2, 7, scalars, tiles, weights, table, marks, lab, work, parts, products, total, sem
    )
    for g in range(25 * AGG):
        turned[MODES * g : MODES * (g + 1), :] = total[g, :MODES, :]
    flat = turned[...].T
    even = scalars[K + 1, 0] == 0
    low, mid, top = (flat[3 * C * i : 3 * C * (i + 1)] for i in range(3))
    own_out[...] = mid
    near_out[...] = jnp.where(even, top, low)
    far_out[...] = jnp.where(even, low, top)


def merge_kernel(where, own, near, far, own_out, near_out, far_out):
    even = where[K + 1, 0] == 0
    span = 5 * C
    low = jnp.where(even, near[...], far[...])
    top = jnp.where(even, far[...], near[...])
    zeros = jnp.zeros((3 * C, span), jnp.float32)
    mid = own[...]
    length = 5 * span
    summed = (
        jnp.concatenate([top[:, :length], zeros, zeros], 1)
        + jnp.concatenate([zeros, mid[:, :length], zeros], 1)
        + jnp.concatenate([zeros, zeros, low[:, :length]], 1)
    )
    even = where[K + 1, 1] == 0
    low, mid, top = (summed[C * i : C * (i + 1)] for i in range(3))
    own_out[...] = mid
    near_out[...] = jnp.where(even, top, low)
    far_out[...] = jnp.where(even, low, top)


def place_kernel(where, own, near, far, coarse):
    even = where[K + 1, 1] == 0
    low = jnp.where(even, near[...], far[...])
    top = jnp.where(even, far[...], near[...])
    mid = own[...]
    zeros = jnp.zeros((C, C), jnp.float32)
    pieces = []
    for u in range(7):
        lanes = slice(5 * C * u, 5 * C * (u + 1))
        pieces.append(
            jnp.concatenate([top[:, lanes], zeros, zeros], 1)
            + jnp.concatenate([zeros, mid[:, lanes], zeros], 1)
            + jnp.concatenate([zeros, zeros, low[:, lanes]], 1)
        )
    coarse[...] = jnp.concatenate(pieces, 1)


def shape(*dims, dtype=jnp.float32):
    return jax.ShapeDtypeStruct(dims, dtype)


def body(operator_tiles, tile_slab, tile_column, tile_live, send_list, aggregate, null_modes):
    tiles = operator_tiles[0, 0]
    slab = tile_slab[0, 0].T
    column = tile_column[0, 0].T
    live = tile_live[0, 0].T
    send = send_list[0, 0]
    wide_odd = lax.axis_index("wide") % 2
    narrow_odd = lax.axis_index("narrow") % 2
    down, across = slab // 3 - 1, slab % 3 - 1
    row_block = jnp.where(down == 0, 0, jnp.where(down == 1 - 2 * wide_odd, 1, 2))
    col_block = jnp.where(across == 0, 0, jnp.where(across == 1 - 2 * narrow_odd, 1, 2))
    block = 1 + 3 * row_block + col_block
    source = jnp.where(slab == 4, column, block * S + column)
    kind = jnp.where(live == 0, 0, jnp.where(row_block == 2, 2, 1))
    place = lax.broadcasted_iota(jnp.int32, (K, R), 1) * K + lax.broadcasted_iota(
        jnp.int32, (K, R), 0
    )
    entries = (
        place
        + (source << 8)
        + ((5 * (slab // 3) + slab % 3) << 16)
        + (kind << 21)
        + (slab << 23)
    )
    lanes = lax.broadcasted_iota(jnp.int32, (1, BS), 1)
    parity = jnp.where(lanes == 0, wide_odd, narrow_odd).astype(jnp.int32)
    scalars = jnp.concatenate(
        [
            jnp.pad(entries, ((0, 0), (0, BS - R))),
            jnp.pad(send[None], ((0, 0), (0, BS - S))),
            parity,
            jnp.zeros((6, BS), jnp.int32),
        ],
        0,
    )

    own_modes, offered = pl.pallas_call(
        pack_kernel,
        out_shape=(shape(R, GROUP, BS), shape(S, GROUP, BS)),
        in_specs=[HBM] * 3,
        out_specs=(VMEM, VMEM),
        scratch_shapes=[
            pltpu.SMEM((S,), jnp.int32),
            pltpu.SMEM((R,), jnp.int32),
            pltpu.VMEM((MODES, R, BS), jnp.float32),
            pltpu.SemaphoreType.DMA((3,)),
        ],
        compiler_params=params(4),
        name="pack",
    )(
        *(
            pltpu.with_memory_space_constraint(x, pltpu.HBM)
            for x in (send, aggregate[0, 0], null_modes[0, 0].transpose(1, 0, 2))
        )
    )
    near, far = pair_halo(offered, "narrow", 0)
    line = jnp.concatenate([offered, near, far], 0)
    wide_near, wide_far = pair_halo(line, "wide", 0)
    table = jnp.concatenate([own_modes, near, far, wide_near, wide_far], 0)

    tiles = tiles.reshape(R * K, BS, BS)
    resting = pltpu.with_memory_space_constraint(tiles, pltpu.HBM)
    listed = pltpu.SMEM((400,), jnp.int32)
    taken = pltpu.VMEM((S * K, BS, BS), jnp.float32)
    scales = pltpu.VMEM((R, GROUP, BS), jnp.float32)
    begun, message = pl.pallas_call(
        offer_kernel,
        out_shape=(shape(R * K, GROUP, BS), shape(BLOCK, BS)),
        in_specs=[SMEM, VMEM, HBM, VMEM],
        out_specs=(VMEM, VMEM),
        scratch_shapes=[
            scales,
            listed,
            taken,
            pltpu.SemaphoreType.DMA((S * K,)),
        ],
        compiler_params=params(16),
        name="offer",
    )(scalars, scalars, resting, table)

    narrow_near, narrow_far = pair_halo(message, "narrow", 0)
    prolong, blocks, weights = pl.pallas_call(
        rest_kernel,
        out_shape=(
            shape(R, 9 * C, BS),
            shape(2 * BLOCK, BS),
            shape(R, 256, 2 * BS, dtype=jnp.bfloat16),
        ),
        in_specs=[SMEM, VMEM, HBM, VMEM, VMEM],
        out_specs=(HBM, VMEM, VMEM),
        scratch_shapes=[
            pltpu.VMEM((R, 9 * C, BS), jnp.float32),
            pltpu.VMEM((R * K, GROUP, BS), jnp.float32),
            scales,
            listed,
            pltpu.SMEM((R + 8,), jnp.int32),
            pltpu.SMEM((R,), jnp.int32),
            pltpu.VMEM((K, BS), jnp.int32),
            pltpu.SMEM((K, BS), jnp.int32),
            pltpu.VMEM((9 * AGG, GROUP, BS), jnp.float32),
            pltpu.VMEM((9 * AGG, GROUP, BS), jnp.float32),
            taken,
            pltpu.SemaphoreType.DMA,
            pltpu.SemaphoreType.DMA((R,)),
            pltpu.SemaphoreType.DMA((S * K,)),
        ],
        compiler_params=params(24),
        cost_estimate=pl.CostEstimate(flops=2 * 10**9, bytes_accessed=2 * 10**7, transcendentals=0),
        name="rest",
    )(scalars, scalars, resting, table, begun)
    line = jnp.concatenate([message, narrow_near, narrow_far], 0)
    line, weights = lax.optimization_barrier((line, weights))
    wide_near, wide_far = pair_halo(line, "wide", 0)

    def coupling(blocks):
        return [
            pltpu.VMEM((blocks * K, BS), jnp.int32),
            pltpu.SMEM((blocks * K, BS), jnp.int32),
            listed,
            pltpu.VMEM((UNROLL * K * MODES, 3 * BS), jnp.bfloat16),
            pltpu.VMEM((UNROLL * K * MODES + GROUP, 256), jnp.float32),
            pltpu.VMEM((25 * AGG + 52, GROUP, 256), jnp.float32),
        ]

    table = jnp.concatenate([blocks, narrow_near, narrow_far, wide_near], 0)
    total = pl.pallas_call(
        beside_kernel,
        out_shape=shape(25 * AGG, GROUP, 256),
        in_specs=[SMEM] + [VMEM] * 3,
        out_specs=VMEM,
        scratch_shapes=coupling(7) + [pltpu.SemaphoreType.DMA],
        compiler_params=params(16),
        cost_estimate=pl.CostEstimate(flops=8 * 10**9, bytes_accessed=3 * 10**7, transcendentals=0),
        name="beside",
    )(scalars, tiles, weights, table)
    own, near, far = pl.pallas_call(
        corner_kernel,
        out_shape=(shape(3 * C, 25 * C),) * 3,
        in_specs=[SMEM] + [VMEM] * 4,
        out_specs=(VMEM,) * 3,
        scratch_shapes=coupling(3)
        + [pltpu.VMEM((25 * C, 256), jnp.float32), pltpu.SemaphoreType.DMA],
        compiler_params=params(16),
        name="corner",
    )(scalars, tiles, weights, total, wide_far)

    size = lax.axis_size("wide")
    pairs = [(i, i ^ 1) for i in range(size)]
    far_pairs = [(i, i + 1) if i % 2 else (i, i - 1) for i in range(1, size - 1)]
    near, far = lax.ppermute(near, "wide", pairs), lax.ppermute(far, "wide", far_pairs)
    own, near, far = pl.pallas_call(
        merge_kernel,
        out_shape=(shape(C, 35 * C),) * 3,
        in_specs=[SMEM] + [VMEM] * 3,
        out_specs=(VMEM,) * 3,
        compiler_params=params(4),
        name="merge",
    )(scalars, own, near, far)
    size = lax.axis_size("narrow")
    pairs = [(i, i ^ 1) for i in range(size)]
    far_pairs = [(i, i + 1) if i % 2 else (i, i - 1) for i in range(1, size - 1)]
    near, far = lax.ppermute(near, "narrow", pairs), lax.ppermute(far, "narrow", far_pairs)
    coarse = pl.pallas_call(
        place_kernel,
        out_shape=shape(C, 49 * C),
        in_specs=[SMEM] + [VMEM] * 3,
        out_specs=VMEM,
        compiler_params=params(4),
        name="place",
    )(scalars, own, near, far)
    return prolong[None, None], coarse[None, None]


def solution(mesh):
    in_specs = (
        P("wide", "narrow", None, None, None, None),
        P("wide", "narrow", None, None),
        P("wide", "narrow", None, None),
        P("wide", "narrow", None, None),
        P("wide", "narrow", None),
        P("wide", "narrow", None),
        P("wide", "narrow", None, None, None),
    )
    out_specs = (P("wide", "narrow", None, None, None), P("wide", "narrow", None, None))
    return jax.shard_map(body, mesh=mesh, in_specs=in_specs, out_specs=out_specs, check_vma=False)
```

time: 120 us -> 85.8 us (0.71)
  Pallas kernels: 54.8 us -> 40.2 us
  waiting for transfers between devices: 28.3 us -> 14.6 us
  local copies, waits for them, and re-layouts: 9.57 us -> 0.17 us
  starting transfers between devices: 24.7 us -> 27.2 us
    ppermute x8, waiting for transfers between devices: 21.5 us -> 7.88 us  [pair_halo(): return (lax.ppermute(block, axis, near), lax.ppermute(block, axis, far))]
    pallas_call x3 -> x4, Pallas kernels: 49.3 us -> 36.7 us  [the longest x1 13.6 us: body(): pl.pallas_call(beside_kernel, out_shape=shape(25 * AGG, GROUP, 256), in_s...]
    unnamed x22 -> x12, local copies, waits for them, and re-layouts: 9.54 us -> 0.06 us
    ppermute x1, starting transfers between devices: 3.49 us -> 5.01 us  [body(): lax.ppermute(far, 'narrow', far_pairs)]
  transfers between devices with their start and end apart: 12 -> 12, of which waited for: 9 -> 8; matrix products, arithmetic and copies ran while one was open for 2% -> 2% of each run, Pallas kernels for 7% -> 27%
where the time goes in v2:
time: 85.8 us; the launch traced here: 84.8 us
  Pallas kernels  40.2 us (47%)
  starting transfers between devices  27.2 us (32%)
  waiting for transfers between devices  14.6 us (17%)
  other arithmetic  1.75 us (2%)
  between operations  0.97 us (1%)
    ppermute x8, starting transfers between devices, pair_halo(): return (lax.ppermute(block, axis, near), lax.ppermute(block, axis, far))  16.4 us
    pallas_call x1, Pallas kernels, body(): pl.pallas_call(beside_kernel, out_shape=shape(25 * AGG, GROUP, 256), in_s...  13.6 us
    pallas_call x1, Pallas kernels, body(): pl.pallas_call(rest_kernel, out_shape=(shape(R, 9 * C, BS), shape(2 * BLO...  9.08 us
    pallas_call x1, Pallas kernels, body(): pl.pallas_call(corner_kernel, out_shape=(shape(3 * C, 25 * C),) * 3, in_s...  8.5 us
    ppermute x8, waiting for transfers between devices, pair_halo(): return (lax.ppermute(block, axis, near), lax.ppermute(block, axis, far))  7.88 us
    pallas_call x1, Pallas kernels, body(): pl.pallas_call(offer_kernel, out_shape=(shape(R * K, GROUP, BS), shape(BL...  5.5 us
    ppermute x1, starting transfers between devices, body(): lax.ppermute(far, 'narrow', far_pairs)  5.01 us
    ppermute x1, starting transfers between devices, body(): lax.ppermute(far, 'wide', far_pairs)  4.7 us
  transfers between devices with their start and end apart: 12, of which 8 were waited for; matrix products, arithmetic and copies ran while one was open for 2% of the time, Pallas kernels for 27%

profile of v2, /device:TPU:14, one launch (start us, length us, event | category | flops | bytes accessed | tf_op | source)
XLA Modules:
  0.0 84.8 jit_solution(2898027377315943776)
XLA Ops:
  0.6 1.0 %pack.1 = (f32[32,8,128]{2,1,0:T(8,128)S(1)}, f32[16,8,128]{2,1,0:T(8,128)S(1)}) custom-call(s32[16]{0:T(128)} %bitcast.63, s32[32]{0:T(128)} %bitcast.65, f32[6,32,128]{2,1,0:T(8,128)} %bitcast.62), custom_call_target="tpu_custom_call" | custom-call | tf_op jit(solution)/shard_map/pack/pallas_call | solution.py:402
  1.7 3.5 %collective-permute-start.1 = (f32[16,8,128]{2,1,0:T(8,128)S(1)}, f32[16,8,128]{2,1,0:T(8,128)S(1)}, u32[]{:S(2)}, u32[]{:S(2)}) collective-permute-start(f32[16,8,128]{2,1,0:T(8,128)S(1)} %get-tuple-element.18), channel_id=1, source_target_pairs={{1,2},{2,1},{5,6},{6,5},{9,10},{10,9},{13,14},{14,13},{17,18},{18,... | collective-permute-start | bytes 196616 | tf_op jit(solution)/shard_map/ppermute | solution.py:41
  5.2 0.1 collective-permute-start
  5.3 0.1 pad.20.clone
  5.4 0.8 fusion.6
  6.2 3.3 %collective-permute-done = f32[16,8,128]{2,1,0:T(8,128)S(1)} collective-permute-done((f32[16,8,128]{2,1,0:T(8,128)S(1)}, f32[16,8,128]{2,1,0:T(8,128)S(1)}, u32[]{:S(2)}, u32[]{:S(2)}) %collective-permute-start) | collective-permute-done | bytes 65568 | tf_op jit(solution)/shard_map/ppermute | solution.py:41
  9.5 0.0 collective-permute-done.1
  9.6 4.3 %collective-permute-start.3 = (f32[48,8,128]{2,1,0:T(8,128)S(1)}, f32[48,8,128]{2,1,0:T(8,128)S(1)}, u32[]{:S(2)}, u32[]{:S(2)}) collective-permute-start(f32[48,8,128]{2,1,0:T(8,128)S(1)} %get-tuple-element.32), channel_id=1, source_target_pairs={{4,8},{8,4},{12,16},{16,12},{20,24},{24,20},{28,32},{32,28},{36,40... | collective-permute-start | bytes 589832 | tf_op jit(solution)/shard_map/ppermute | solution.py:41
  13.8 0.1 collective-permute-start.2
  13.9 0.7 fusion.1.scalars.ints.where
  14.6 0.7 collective-permute-done.2
  15.4 3.3 %collective-permute-done.3 = f32[48,8,128]{2,1,0:T(8,128)S(1)} collective-permute-done((f32[48,8,128]{2,1,0:T(8,128)S(1)}, f32[48,8,128]{2,1,0:T(8,128)S(1)}, u32[]{:S(2)}, u32[]{:S(2)}) %collective-permute-start.3) | collective-permute-done | bytes 196640 | tf_op jit(solution)/shard_map/ppermute | solution.py:41
  18.7 0.0 slice-start
  18.7 0.0 slice-start.1
  18.7 5.5 %offer.1 = (f32[256,8,128]{2,1,0:T(8,128)S(1)}, f32[776,128]{1,0:T(8,128)S(1)}) custom-call(s32[16,128]{1,0:T(8,128)S(1)} %fusion.1.scalars.ints.where, s32[16,128]{1,0:T(8,128)S(1)} %fusion.1.scalars.ints.where, f32[256,128,128]{2,1,0:T(8,128)} %bitcast.55, f32[160,8,128]{2,1,0:T(8,128)S(1)} %constant_dynamic-update-slice_fusion.3.table), custom_call_target="tpu_custom_call" | custom-call | tf_op jit(solution)/shard_map/offer/pallas_call | solution.py:431
  24.2 2.4 %collective-permute-start.5 = (f32[776,128]{1,0:T(8,128)S(1)}, f32[776,128]{1,0:T(8,128)S(1)}, u32[]{:S(2)}, u32[]{:S(2)}) collective-permute-start(f32[776,128]{1,0:T(8,128)S(1)} %get-tuple-element.21), channel_id=1, source_target_pairs={{1,2},{2,1},{5,6},{6,5},{9,10},{10,9},{13,14},{14,13},{17,18},{18,... | collective-permute-start | bytes 1191944 | tf_op jit(solution)/shard_map/ppermute | solution.py:41
  26.6 0.1 collective-permute-start.4
  26.7 0.0 slice-start.2
  26.7 0.0 slice-start.3
  26.7 9.1 %rest.1 = (f32[32,216,128]{2,1,0:T(8,128)}, f32[1552,128]{1,0:T(8,128)S(1)}, bf16[32,256,256]{2,1,0:T(8,128)(2,1)S(1)}) custom-call(s32[16,128]{1,0:T(8,128)S(1)} %fusion.1.scalars.ints.where, s32[16,128]{1,0:T(8,128)S(1)} %fusion.1.scalars.ints.where, f32[256,128,128]{2,1,0:T(8,128)} %bitcast.56, ...), custom_call_target="tpu_custom_call" | custom-call | flops 2000000000 | bytes 20000000 | tf_op jit(solution)/shard_map/rest/pallas_call | solution.py:447
  35.8 0.3 collective-permute-done.5
  36.1 0.1 collective-permute-done.4
  36.2 0.1 pad_maximum_fusion.1
  36.3 0.1 collective-permute-start.6
  36.4 6.0 %collective-permute-start.7 = (f32[2328,128]{1,0:T(8,128)S(1)}, f32[2328,128]{1,0:T(8,128)S(1)}, u32[]{:S(2)}, u32[]{:S(2)}) collective-permute-start(f32[2328,128]{1,0:T(8,128)S(1)} %pad_maximum_fusion.1), channel_id=1, source_target_pairs={{4,8},{8,4},{12,16},{16,12},{20,24},{24,20},{28,32},{32,28},{36,40... | collective-permute-start | bytes 3575816 | tf_op jit(solution)/shard_map/ppermute | solution.py:41
  42.4 0.0 collective-permute-done.6
  42.4 0.2 pad_maximum_fusion.table
  42.6 0.0 slice-done
  42.6 0.0 slice-done.1
  42.6 0.0 slice-done.2
  42.6 0.0 slice-done.3
  42.6 13.6 %beside.1.begun = f32[100,8,256]{2,1,0:T(8,128)S(1)} custom-call(s32[16,128]{1,0:T(8,128)S(1)} %fusion.1.scalars.ints.where, f32[256,128,128]{2,1,0:T(8,128)S(1)} %bitcast.59, bf16[32,256,256]{2,1,0:T(8,128)(2,1)S(1)} %get-tuple-element.23.weights, f32[5432,128]{1,0:T(8,128)S(1)} %pad_maximum_fusion.table), custom_call_target="tpu_custom_call" | custom-call | flops 8000000000 | bytes 30000000 | tf_op jit(solution)/shard_map/beside/pallas_call | solution.py:491
  56.3 0.1 collective-permute-done.7.table
  56.4 8.5 %corner.1 = (f32[72,600]{1,0:T(8,128)S(1)}, f32[72,600]{1,0:T(8,128)S(1)}, f32[72,600]{1,0:T(8,128)S(1)}) custom-call(s32[16,128]{1,0:T(8,128)S(1)} %fusion.1.scalars.ints.where, f32[256,128,128]{2,1,0:T(8,128)S(1)} %bitcast.60, bf16[32,256,256]{2,1,0:T(8,128)(2,1)S(1)} %get-tuple-element.23.weights, f32[100,8,256]{2,1,0:T(8,128)S(1)} %beside.1.begun, ...), custom_call_target="tpu_custom_call" | custom-call | tf_op jit(solution)/shard_map/corner/pallas_call | solution.py:501
  64.9 0.1 collective-permute-start.8
  65.0 4.7 %collective-permute-start.9 = (f32[72,600]{1,0:T(8,128)S(1)}, f32[72,600]{1,0:T(8,128)S(1)}, u32[]{:S(2)}, u32[]{:S(2)}) collective-permute-start(f32[72,600]{1,0:T(8,128)S(1)} %get-tuple-element.28), channel_id=1, source_target_pairs={{4,8},{8,4},{12,16},{16,12},{20,24},{24,20},{28,32},{32,28},{36,40... | collective-permute-start | bytes 518408 | tf_op jit(solution)/shard_map/ppermute | solution.py:515
  69.7 0.0 collective-permute-done.8.near
  69.7 4.3 %collective-permute-done.9.far = f32[72,600]{1,0:T(8,128)S(1)} collective-permute-done((f32[72,600]{1,0:T(8,128)S(1)}, f32[72,600]{1,0:T(8,128)S(1)}, u32[]{:S(2)}, u32[]{:S(2)}) %collective-permute-start.9) | collective-permute-done | bytes 172832 | tf_op jit(solution)/shard_map/ppermute | solution.py:515
  73.9 0.8 merge.1
  74.8 1.0 %collective-permute-start.10 = (f32[24,840]{1,0:T(8,128)S(1)}, f32[24,840]{1,0:T(8,128)S(1)}, u32[]{:S(2)}, u32[]{:S(2)}) collective-permute-start(f32[24,840]{1,0:T(8,128)S(1)} %get-tuple-element.30), channel_id=1, source_target_pairs={{0,1},{1,0},{2,3},{3,2},{4,5},{5,4},{6,7},{7,6},{8,9},{9,8},{10,11... | collective-permute-start | bytes 241928 | tf_op jit(solution)/shard_map/ppermute | solution.py:527
  75.8 5.0 %collective-permute-start.11 = (f32[24,840]{1,0:T(8,128)S(1)}, f32[24,840]{1,0:T(8,128)S(1)}, u32[]{:S(2)}, u32[]{:S(2)}) collective-permute-start(f32[24,840]{1,0:T(8,128)S(1)} %get-tuple-element.31), channel_id=1, source_target_pairs={{1,2},{2,1},{5,6},{6,5},{9,10},{10,9},{13,14},{14,13},{17,18},{18,... | collective-permute-start | bytes 241928 | tf_op jit(solution)/shard_map/ppermute | solution.py:527
  80.8 0.0 collective-permute-done.10.near
  80.8 2.4 %collective-permute-done.11.far = f32[24,840]{1,0:T(8,128)S(1)} collective-permute-done((f32[24,840]{1,0:T(8,128)S(1)}, f32[24,840]{1,0:T(8,128)S(1)}, u32[]{:S(2)}, u32[]{:S(2)}) %collective-permute-start.11) | collective-permute-done | bytes 80672 | tf_op jit(solution)/shard_map/ppermute | solution.py:527
  83.2 1.6 %place.1 = f32[24,1176]{1,0:T(8,128)} custom-call(s32[16,128]{1,0:T(8,128)S(1)} %fusion.1.scalars.ints.where, f32[24,840]{1,0:T(8,128)S(1)} %get-tuple-element.29.own, f32[24,840]{1,0:T(8,128)S(1)} %collective-permute-done.10.near, f32[24,840]{1,0:T(8,128)S(1)} %collective-permute-done.11.far), custom_call_target="tpu_custom_call" | custom-call | tf_op jit(solution)/shard_map/place/pallas_call | solution.py:528
  (10 shorter events, 0.1 us)
Async XLA Ops:
  1.7 7.9 %collective-permute-start.1 = (f32[16,8,128]{2,1,0:T(8,128)S(1)}, f32[16,8,128]{2,1,0:T(8,128)S(1)}, u32[]{:S(2)}, u32[]{:S(2)}) collective-permute-start(f32[16,8,128]{2,1,0:T(8,128)S(1)} %get-tuple-element.18), channel_id=1, source_target_pairs={{1,2},{2,1},{5,6},{6,5},{9,10},{10,9},{13,14},{14,13},{17,18},{18,... | collective-permute-start | bytes 196616 | tf_op jit(solution)/shard_map/ppermute | solution.py:41
  5.2 4.3 %collective-permute-start = (f32[16,8,128]{2,1,0:T(8,128)S(1)}, f32[16,8,128]{2,1,0:T(8,128)S(1)}, u32[]{:S(2)}, u32[]{:S(2)}) collective-permute-start(f32[16,8,128]{2,1,0:T(8,128)S(1)} %get-tuple-element.18), channel_id=1, source_target_pairs={{0,1},{1,0},{2,3},{3,2},{4,5},{5,4},{6,7},{7,6},{8,9},{9,8},{10,11... | collective-permute-start | bytes 196616 | tf_op jit(solution)/shard_map/ppermute | solution.py:41
  9.6 9.1 %collective-permute-start.3 = (f32[48,8,128]{2,1,0:T(8,128)S(1)}, f32[48,8,128]{2,1,0:T(8,128)S(1)}, u32[]{:S(2)}, u32[]{:S(2)}) collective-permute-start(f32[48,8,128]{2,1,0:T(8,128)S(1)} %get-tuple-element.32), channel_id=1, source_target_pairs={{4,8},{8,4},{12,16},{16,12},{20,24},{24,20},{28,32},{32,28},{36,40... | collective-permute-start | bytes 589832 | tf_op jit(solution)/shard_map/ppermute | solution.py:41
  13.8 1.5 %collective-permute-start.2 = (f32[48,8,128]{2,1,0:T(8,128)S(1)}, f32[48,8,128]{2,1,0:T(8,128)S(1)}, u32[]{:S(2)}, u32[]{:S(2)}) collective-permute-start(f32[48,8,128]{2,1,0:T(8,128)S(1)} %get-tuple-element.32), channel_id=1, source_target_pairs={{0,4},{4,0},{8,12},{12,8},{16,20},{20,16},{24,28},{28,24},{32,36},... | collective-permute-start | bytes 589832 | tf_op jit(solution)/shard_map/ppermute | solution.py:41
  18.7 23.9 %slice-start = ((s8[16777216]{0:T(1024)(128)(4,1)}), s8[4194304]{0:T(1024)(128)(4,1)S(1)}, s32[]{:S(2)}) async-start(s8[16777216]{0:T(1024)(128)(4,1)} %bitcast.57), calls=%async_computation | async-start | bytes 8388608
  18.7 23.9 %slice-start.1 = ((s8[16777216]{0:T(1024)(128)(4,1)}), s8[4194304]{0:T(1024)(128)(4,1)S(1)}, s32[]{:S(2)}) async-start(s8[16777216]{0:T(1024)(128)(4,1)} %bitcast.57), calls=%async_computation.1 | async-start | bytes 8388608
  24.2 11.9 %collective-permute-start.5 = (f32[776,128]{1,0:T(8,128)S(1)}, f32[776,128]{1,0:T(8,128)S(1)}, u32[]{:S(2)}, u32[]{:S(2)}) collective-permute-start(f32[776,128]{1,0:T(8,128)S(1)} %get-tuple-element.21), channel_id=1, source_target_pairs={{1,2},{2,1},{5,6},{6,5},{9,10},{10,9},{13,14},{14,13},{17,18},{18,... | collective-permute-start | bytes 1191944 | tf_op jit(solution)/shard_map/ppermute | solution.py:41
  26.6 9.7 %collective-permute-start.4 = (f32[776,128]{1,0:T(8,128)S(1)}, f32[776,128]{1,0:T(8,128)S(1)}, u32[]{:S(2)}, u32[]{:S(2)}) collective-permute-start(f32[776,128]{1,0:T(8,128)S(1)} %get-tuple-element.21), channel_id=1, source_target_pairs={{0,1},{1,0},{2,3},{3,2},{4,5},{5,4},{6,7},{7,6},{8,9},{9,8},{10,11... | collective-permute-start | bytes 1191944 | tf_op jit(solution)/shard_map/ppermute | solution.py:41
  26.7 15.9 %slice-start.2 = ((s8[16777216]{0:T(1024)(128)(4,1)}), s8[4194304]{0:T(1024)(128)(4,1)S(1)}, s32[]{:S(2)}) async-start(s8[16777216]{0:T(1024)(128)(4,1)} %bitcast.57), calls=%async_computation.2 | async-start | bytes 8388608
  26.7 15.9 %slice-start.3 = ((s8[16777216]{0:T(1024)(128)(4,1)}), s8[4194304]{0:T(1024)(128)(4,1)S(1)}, s32[]{:S(2)}) async-start(s8[16777216]{0:T(1024)(128)(4,1)} %bitcast.57), calls=%async_computation.3 | async-start | bytes 8388608
  36.3 6.1 %collective-permute-start.6 = (f32[2328,128]{1,0:T(8,128)S(1)}, f32[2328,128]{1,0:T(8,128)S(1)}, u32[]{:S(2)}, u32[]{:S(2)}) collective-permute-start(f32[2328,128]{1,0:T(8,128)S(1)} %pad_maximum_fusion.1), channel_id=1, source_target_pairs={{0,4},{4,0},{8,12},{12,8},{16,20},{20,16},{24,28},{28,24},{32,36},... | collective-permute-start | bytes 3575816 | tf_op jit(solution)/shard_map/ppermute | solution.py:41
  36.4 20.0 %collective-permute-start.7 = (f32[2328,128]{1,0:T(8,128)S(1)}, f32[2328,128]{1,0:T(8,128)S(1)}, u32[]{:S(2)}, u32[]{:S(2)}) collective-permute-start(f32[2328,128]{1,0:T(8,128)S(1)} %pad_maximum_fusion.1), channel_id=1, source_target_pairs={{4,8},{8,4},{12,16},{16,12},{20,24},{24,20},{28,32},{32,28},{36,40... | collective-permute-start | bytes 3575816 | tf_op jit(solution)/shard_map/ppermute | solution.py:41
  64.9 4.8 %collective-permute-start.8 = (f32[72,600]{1,0:T(8,128)S(1)}, f32[72,600]{1,0:T(8,128)S(1)}, u32[]{:S(2)}, u32[]{:S(2)}) collective-permute-start(f32[72,600]{1,0:T(8,128)S(1)} %get-tuple-element.27), channel_id=1, source_target_pairs={{0,4},{4,0},{8,12},{12,8},{16,20},{20,16},{24,28},{28,24},{32,36},... | collective-permute-start | bytes 518408 | tf_op jit(solution)/shard_map/ppermute | solution.py:515
  65.0 9.0 %collective-permute-start.9 = (f32[72,600]{1,0:T(8,128)S(1)}, f32[72,600]{1,0:T(8,128)S(1)}, u32[]{:S(2)}, u32[]{:S(2)}) collective-permute-start(f32[72,600]{1,0:T(8,128)S(1)} %get-tuple-element.28), channel_id=1, source_target_pairs={{4,8},{8,4},{12,16},{16,12},{20,24},{24,20},{28,32},{32,28},{36,40... | collective-permute-start | bytes 518408 | tf_op jit(solution)/shard_map/ppermute | solution.py:515
  74.8 6.0 %collective-permute-start.10 = (f32[24,840]{1,0:T(8,128)S(1)}, f32[24,840]{1,0:T(8,128)S(1)}, u32[]{:S(2)}, u32[]{:S(2)}) collective-permute-start(f32[24,840]{1,0:T(8,128)S(1)} %get-tuple-element.30), channel_id=1, source_target_pairs={{0,1},{1,0},{2,3},{3,2},{4,5},{5,4},{6,7},{7,6},{8,9},{9,8},{10,11... | collective-permute-start | bytes 241928 | tf_op jit(solution)/shard_map/ppermute | solution.py:527
  75.8 7.5 %collective-permute-start.11 = (f32[24,840]{1,0:T(8,128)S(1)}, f32[24,840]{1,0:T(8,128)S(1)}, u32[]{:S(2)}, u32[]{:S(2)}) collective-permute-start(f32[24,840]{1,0:T(8,128)S(1)} %get-tuple-element.31), channel_id=1, source_target_pairs={{1,2},{2,1},{5,6},{6,5},{9,10},{10,9},{13,14},{14,13},{17,18},{18,... | collective-permute-start | bytes 241928 | tf_op jit(solution)/shard_map/ppermute | solution.py:527

commit v3 on v2

v3 whole, which is shorter than its diff:
```python
import functools

import jax
import jax.numpy as jnp
from jax import lax
from jax.experimental import pallas as pl
from jax.experimental.pallas import tpu as pltpu
from jax.sharding import PartitionSpec as P

MODES = 6
GROUP = 8
AGG = 4
BS = 128
R = 32
K = 8
S = 16
C = 24
OMEGA = 0.7
BLOCK = S * K * MODES + GROUP
T_ENTRIES = R + 8 * S
UNROLL = 16
SMOOTH = 32
LIST = 384
LISTS = K + 2
NT = (((1,), (1,)), ((), ()))
VMEM = pl.BlockSpec(memory_space=pltpu.VMEM)
SMEM = pl.BlockSpec(memory_space=pltpu.SMEM)
HBM = pl.BlockSpec(memory_space=pltpu.HBM)


def params(mib):
    return pltpu.CompilerParams(vmem_limit_bytes=mib * 2**20)


def split(value):
    high = value.astype(jnp.bfloat16)
    return high, (value - high.astype(jnp.float32)).astype(jnp.bfloat16)


def pair_near(block, axis):
    return lax.ppermute(block, axis, [(i, i ^ 1) for i in range(lax.axis_size(axis))])


def pair_far(block, axis):
    pairs = [(i, i + 1) if i % 2 else (i, i - 1) for i in range(1, lax.axis_size(axis) - 1)]
    return lax.ppermute(block, axis, pairs)


def pair_halo(block, axis):
    far = pair_far(block, axis)
    return pair_near(block, axis), far


def pack_kernel(send_hbm, aggregate_hbm, modes_hbm, own, message, send, aggregate, modes, sems):
    copies = [
        pltpu.make_async_copy(source, target, sems.at[i])
        for i, (source, target) in enumerate(
            ((modes_hbm, modes), (aggregate_hbm, aggregate), (send_hbm, send))
        )
    ]
    for copy in copies:
        copy.start()
    for copy in copies:
        copy.wait()
    for b in range(R):
        for m in range(MODES):
            own[b, m] = modes[m, b]
        own[b, MODES] = jnp.full((BS,), aggregate[b].astype(jnp.float32))
        own[b, MODES + 1] = jnp.zeros((BS,), jnp.float32)
    for s in range(S):
        message[s] = own[send[s]]


def plan_kernel(where, send_hbm, slab, column, live, plan, wide, raw, send, sems):
    wide_odd, narrow_odd = where[0], where[1]
    copies = [
        pltpu.make_async_copy(source, target, sems.at[i])
        for i, (source, target) in enumerate(
            ((slab, raw.at[0]), (column, raw.at[1]), (live, raw.at[2]), (send_hbm, send))
        )
    ]
    for copy in copies:
        copy.start()
    wide[...] = jnp.zeros_like(wide)
    for copy in copies:
        copy.wait()
    wide[:, :, 0:R] = raw[...]
    window, col, used = wide[0], wide[1], wide[2]
    window_row = (window * 11) >> 5
    down, across = window_row - 1, window - 3 * window_row - 1
    row_block = jnp.where(down == 0, 0, jnp.where(down == 1 - 2 * wide_odd, 1, 2))
    col_block = jnp.where(across == 0, 0, jnp.where(across == 1 - 2 * narrow_odd, 1, 2))
    block = 1 + 3 * row_block + col_block
    source = jnp.where(window == 4, col, block * S + col)
    kind = jnp.where(used == 0, 0, jnp.where((row_block == 2) & (across != 0), 2, 1))
    slot = lax.broadcasted_iota(jnp.int32, (K, BS), 0)
    lane = lax.broadcasted_iota(jnp.int32, (K, BS), 1)
    inside = lane < R
    entries = (
        (lane * K + slot)
        + (source << 8)
        + ((5 * window_row + across + 1) << 16)
        + (kind << 21)
        + (window << 23)
    )
    entries = jnp.where(inside, entries, 0)
    first = lane[0:1]
    offered = jnp.zeros((1, BS), jnp.int32)
    sent = jnp.zeros((1, BS), jnp.int32)
    for s in range(S):
        offered = jnp.where(first == send[s], 1, offered)
        sent = jnp.where(first == s, send[s], sent)
    is_live = (used != 0) & inside
    is_offered = jnp.broadcast_to(offered, (K, BS)) == 1
    before = (
        lax.broadcasted_iota(jnp.int32, (BS, BS), 0) < lax.broadcasted_iota(jnp.int32, (BS, BS), 1)
    ).astype(jnp.bfloat16)

    def counted(mask, even):
        ones = mask.astype(jnp.float32)
        ahead = [jnp.zeros((1, BS), jnp.float32)]
        for k in range(K):
            ahead.append(ahead[-1] + ones[k : k + 1])
        length = ahead.pop()
        if even:
            length = 2.0 * jnp.floor(0.5 * (length + 1.0))
        rows = jnp.broadcast_to(length, (K, BS))
        start = jnp.dot(rows.astype(jnp.bfloat16), before, preferred_element_type=jnp.float32)
        return start + jnp.concatenate(ahead, 0), jnp.sum(length, axis=1, keepdims=True)

    places, totals = [], []
    for rows in (is_offered, jnp.logical_not(is_offered)):
        top = is_live & rows & (slot == 0)
        other = is_live & rows & (slot != 0)
        place, _ = counted(top, False)
        place_other, total = counted(other, False)
        places.append((jnp.where(top, place, jnp.where(other, place_other + S, -1.0)), BS))
        totals.append(total + S)
    for i in (1, 2):
        mask = is_live & (kind == i)
        place, total = counted(mask, True)
        places.append((jnp.where(mask, place, -1.0), LIST))
        totals.append(total)
    choices = []
    for place, length in places:
        turned = place.T
        at = lax.broadcasted_iota(jnp.int32, (R, length), 1).astype(jnp.float32)
        choices.append(
            jnp.concatenate(
                [(turned[0:R, k : k + 1] == at).astype(jnp.bfloat16) for k in range(K)], 0
            )
        )
    rows = [
        jnp.concatenate([((entries >> (8 * i)) & 255)[k : k + 1, 0:R] for k in range(K)], 1)
        for i in range(4)
    ]
    rows.append(jnp.ones((1, K * R), jnp.int32))
    rows.append(jnp.zeros((11, K * R), jnp.int32))
    bytes_of = jnp.concatenate(rows, 0).astype(jnp.float32).astype(jnp.bfloat16)
    found = jnp.dot(
        bytes_of, jnp.concatenate(choices, 1), preferred_element_type=jnp.float32
    ).astype(jnp.int32)
    lists = found[0:1] + (found[1:2] << 8) + (found[2:3] << 16) + (found[3:4] << 24)
    filled = found[4:5] != 0
    plan[...] = jnp.zeros_like(plan)
    plan[0:K, 0:BS] = entries
    plan[K : K + 1, 0:BS] = sent
    numbers = jnp.where(first == 0, wide_odd, narrow_odd)
    for i, total in enumerate(totals):
        numbers = jnp.where(first == 2 + i, total.astype(jnp.int32), numbers)
    plan[K + 1 : K + 2, 0:BS] = numbers
    start = 0
    for i, ((_, length), block) in enumerate(zip(places, (0, 0, 0, 8))):
        part = slice(start, start + length)
        dummy = (25 << 16) + (block * S << 8)
        plan[LISTS + i : LISTS + i + 1, 0:length] = jnp.where(
            filled[:, part], lists[:, part], dummy
        )
        start += length


def pair_rows(high, low):
    zero = jnp.zeros_like(low)
    return jnp.concatenate(
        [jnp.concatenate([high, high], 1), jnp.concatenate([low, zero], 1)], 0
    )


def times_halves(value, halves):
    length = value.shape[0]
    both = lax.dot_general(
        pair_rows(*split(value)), halves, NT, preferred_element_type=jnp.float32
    )
    return both[:length] + both[length:]


def times_tile(value, tile):
    return times_halves(value, jnp.concatenate(split(tile), 1))


def scale_of(tile):
    eye = lax.broadcasted_iota(jnp.int32, (BS, BS), 0) == lax.broadcasted_iota(
        jnp.int32, (BS, BS), 1
    )
    diagonal = jnp.sum(jnp.where(eye, tile, 0.0), axis=0, keepdims=True)
    return jnp.broadcast_to(-OMEGA / diagonal, (GROUP, BS))


def member_marks(ints, table):
    source = (ints[0:K, 0:BS] >> 8) & 255

    def some(i, marks):
        for j in range(8):
            at = i * 8 + j
            marks = jnp.where(source == at, table[at, MODES : MODES + 1, :], marks)
        return marks

    return lax.fori_loop(0, T_ENTRIES // 8, some, jnp.zeros((K, BS), jnp.float32))


def coarse_marks(ints, members):
    return members + (((ints[0:K, 0:BS] >> 16) & 31) * AGG).astype(jnp.float32)


def fetch(tiles, entry, taken, at, sems):
    return pltpu.make_async_copy(tiles.at[entry & 255], taken.at[at], sems.at[at])


def start_batch(i, index, plan, tiles, taken, sems):
    for j in range(UNROLL):
        at = i * UNROLL + j
        pltpu.make_async_copy(
            tiles.at[plan[LISTS + index, at] & 255], taken.at[at], sems.at[i]
        ).start()


def wait_batch(i, tiles, taken, sems):
    at = pl.ds(i * UNROLL, UNROLL)
    pltpu.make_async_copy(tiles.at[pl.ds(0, UNROLL)], taken.at[at], sems.at[i]).wait()


def walk(index, plan, tiles, taken, sems, first, then):
    steps = (plan[K + 1, 2 + index] + UNROLL - 1) // UNROLL
    start_batch(0, index, plan, tiles, taken, sems)

    def start(i):
        @pl.when(i < steps)
        def _():
            start_batch(i, index, plan, tiles, taken, sems)

    start(1)
    start(2)
    wait_batch(0, tiles, taken, sems)
    first()

    def step(i, carry):
        start(i + 2)
        wait_batch(i, tiles, taken, sems)
        then(i)
        return carry

    lax.fori_loop(1, steps, step, 0)


def smooth_tiles(index, plan, tiles, table, slots, scale):
    count = plan[K + 1, 2 + index]
    for s in range(S):
        entry = plan[LISTS + index, s]
        at = entry & 255
        tile = tiles[at]
        modes = table[(entry >> 8) & 255]
        factor = scale_of(tile)
        scale[at // K] = factor
        slots[at] = times_tile(modes, tile) * factor + modes

    def some(i, carry):
        for j in range(SMOOTH):
            entry = plan[LISTS + index, jnp.minimum(S + i * SMOOTH + j, count - 1)]
            at = entry & 255
            value = times_tile(table[(entry >> 8) & 255], tiles[at])
            slots[at] = value * scale[at // K]
        return carry

    lax.fori_loop(0, (count - S + SMOOTH - 1) // SMOOTH, some, 0)


def bring_kernel(plan, tiles, halves, scale, taken, sems):
    def first():
        for s in range(S):
            tile = taken[s]
            scale[(plan[LISTS, s] & 255) // K] = scale_of(tile)
            halves[s] = jnp.concatenate(split(tile), 1)

    def then(i):
        for j in range(UNROLL):
            at = i * UNROLL + j
            halves[at] = jnp.concatenate(split(taken[at]), 1)

    walk(0, plan, tiles, taken, sems, first, then)


def offer_kernel(plan, ints, halves, scale, table, slots, message):
    count = plan[K + 1, 2]
    slots[...] = jnp.zeros_like(slots)
    marks = coarse_marks(ints, member_marks(ints, table))
    chosen = lax.broadcasted_iota(jnp.int32, (BS, BS), 0) == ints[K : K + 1, 0:BS]
    message[S * K * MODES :, :] = jnp.dot(
        marks, chosen.astype(jnp.float32), preferred_element_type=jnp.float32
    )

    def some(i, carry):
        for j in range(SMOOTH):
            place = jnp.minimum(i * SMOOTH + j, count - 1)
            entry = plan[LISTS, place]
            at = entry & 255
            modes = table[(entry >> 8) & 255]
            first = (at % K == 0).astype(jnp.float32)
            value = times_halves(modes, halves[place])
            slots[at] = value * scale[at // K] + first * modes
        return carry

    lax.fori_loop(0, (count + SMOOTH - 1) // SMOOTH, some, 0)
    for s in range(S):
        b = plan[K, s]
        for k in range(K):
            first = (s * K + k) * MODES
            message[first : first + MODES, :] = slots[b * K + k, :MODES]


def rest_kernel(
    plan, ints, tiles, table, begun, prolong_hbm, blocks, weights,
    prolong, slots, scale, marks, lab, dense_even, dense_odd, sem, sems
):
    members = member_marks(ints, table)
    coarse = coarse_marks(ints, members)
    blocks[S * K * MODES : BLOCK, :] = coarse
    blocks[BLOCK + S * K * MODES :, :] = jnp.concatenate([coarse[:, S:], coarse[:, :S]], 1)
    marks[...] = members.astype(jnp.int32) + ((ints[0:K, 0:BS] >> 23) & 15) * AGG
    copy = pltpu.make_async_copy(marks, lab, sem)
    copy.start()
    slots[...] = begun[...]
    smooth_tiles(1, plan, tiles, table, slots, scale)
    copy.wait()

    def send_row(b):
        return pltpu.make_async_copy(prolong.at[b], prolong_hbm.at[b], sems.at[b])

    def rows(i, carry):
        for j, dense in enumerate((dense_even, dense_odd)):
            b = i * 2 + j
            dense[...] = jnp.zeros_like(dense)
            for k in range(K):
                dense[lab[k, b]] += slots[b * K + k]
            for g in range(9 * AGG):
                prolong[b, MODES * g : MODES * (g + 1), :] = dense[g, :MODES]
            block, place = b // S, b % S
            start = pl.multiple_of(block * BLOCK + place * K * MODES, GROUP)
            own = jnp.concatenate([slots[b * K + k, :MODES] for k in range(K)], 0)
            blocks[pl.ds(start, K * MODES), :] = own
            high, low = split(prolong[b])
            weights[b, 0 : 9 * C, 0:BS] = high
            weights[b, 0 : 9 * C, BS:] = low
        for j in range(2):
            send_row(i * 2 + j).start()
        return carry

    lax.fori_loop(0, R // 2, rows, 0)

    def finish(b, carry):
        send_row(b).wait()
        return carry

    lax.fori_loop(0, R, finish, 0)


def couple_tiles(
    index, plan, first_block, tiles, weights, table, marks, lab, parts, products, last, totals, sem
):
    steps = jnp.maximum((plan[K + 1, 2 + index] + UNROLL - 1) // UNROLL, 2)
    for i in range(table.shape[0] // BLOCK):
        first = i * BLOCK + S * K * MODES
        marks[i * K : (i + 1) * K, :] = table[first : first + K, :].astype(jnp.int32)
    copy = pltpu.make_async_copy(marks, lab, sem)
    copy.start()
    length = K * MODES

    def apply_step(i, tiles_of=range(UNROLL)):
        for j in tiles_of:
            entry = plan[LISTS + index, i * UNROLL + j]
            source = (entry >> 8) & 255
            first = ((source >> 4) - first_block) * BLOCK + (source & 15) * length
            rows = table[pl.ds(pl.multiple_of(first, GROUP), length), :]
            high, low = split(times_tile(rows, tiles[entry & 255]))
            parts[length * j : length * (j + 1), :] = jnp.concatenate([high, low, high], 1)

    def product_step(i, products=products, tiles_of=range(UNROLL)):
        for j in tiles_of[::2]:
            b = (plan[LISTS + index, i * UNROLL + j] & 255) // K
            both = weights[b]
            at = slice(j * length, (j + 2) * length)
            products[at, :] = lax.dot_general(
                parts[at, :],
                jnp.concatenate([both[:, :BS], both], 1),
                NT,
                preferred_element_type=jnp.float32,
            )

    def place_step(i, products=products, tiles_of=range(UNROLL)):
        for j in tiles_of:
            entry = plan[LISTS + index, i * UNROLL + j]
            source = (entry >> 8) & 255
            shift = ((entry >> 16) & 31) * AGG
            major, minor = ((source >> 4) - first_block) * K, source & 15
            for g in range(K):
                at = (K * j + g) * MODES
                totals[g % 2][lab[major + g, minor] + shift] += products[at : at + GROUP, :]

    apply_step(0)
    product_step(0)
    apply_step(1)
    copy.wait()

    def step(i, carry):
        for j in range(0, UNROLL, 4):
            some = range(j, j + 4)
            place_step(i - 2, tiles_of=some)
            product_step(i - 1, tiles_of=some)
            apply_step(i, tiles_of=some)
        return carry

    lax.fori_loop(2, steps, step, 0)
    product_step(steps - 1, last)
    place_step(steps - 2)
    place_step(steps - 1, last)


def beside_kernel(
    plan, tiles, weights, table, out, marks, lab, parts, products, last, totals, sem
):
    for part in totals:
        part[0 : 25 * AGG] = jnp.zeros((25 * AGG, GROUP, 256), jnp.float32)
    couple_tiles(
        2, plan, 0, tiles, weights, table, marks, lab, parts, products, last, totals, sem
    )
    out[...] = totals[0][0 : 25 * AGG] + totals[1][0 : 25 * AGG]


def corner_kernel(
    plan, tiles, weights, begun, table, own_out, near_out, far_out,
    marks, lab, parts, products, last, totals, turned, sem
):
    totals[0][0 : 25 * AGG] = begun[...]
    totals[1][0 : 25 * AGG] = jnp.zeros((25 * AGG, GROUP, 256), jnp.float32)
    couple_tiles(
        3, plan, 8, tiles, weights, table, marks, lab, parts, products, last, totals, sem
    )
    for g in range(25 * AGG):
        turned[MODES * g : MODES * (g + 1), :] = totals[0][g, :MODES, :] + totals[1][g, :MODES, :]
    flat = turned[...].T
    even = plan[K + 1, 0] == 0
    low, mid, top = (flat[3 * C * i : 3 * C * (i + 1)] for i in range(3))
    own_out[...] = mid
    near_out[...] = jnp.where(even, top, low)
    far_out[...] = jnp.where(even, low, top)


def merge_kernel(where, own, near, far, own_out, near_out, far_out):
    even = where[0] == 0
    span = 5 * C
    low = jnp.where(even, near[...], far[...])
    top = jnp.where(even, far[...], near[...])
    zeros = jnp.zeros((3 * C, span), jnp.float32)
    mid = own[...]
    length = 5 * span
    summed = (
        jnp.concatenate([top[:, :length], zeros, zeros], 1)
        + jnp.concatenate([zeros, mid[:, :length], zeros], 1)
        + jnp.concatenate([zeros, zeros, low[:, :length]], 1)
    )
    even = where[1] == 0
    low, mid, top = (summed[C * i : C * (i + 1)] for i in range(3))
    own_out[...] = mid
    near_out[...] = jnp.where(even, top, low)
    far_out[...] = jnp.where(even, low, top)


def place_kernel(where, own, near, far, coarse):
    even = where[1] == 0
    low = jnp.where(even, near[...], far[...])
    top = jnp.where(even, far[...], near[...])
    mid = own[...]
    zeros = jnp.zeros((C, C), jnp.float32)
    pieces = []
    for u in range(7):
        lanes = slice(5 * C * u, 5 * C * (u + 1))
        pieces.append(
            jnp.concatenate([top[:, lanes], zeros, zeros], 1)
            + jnp.concatenate([zeros, mid[:, lanes], zeros], 1)
            + jnp.concatenate([zeros, zeros, low[:, lanes]], 1)
        )
    coarse[...] = jnp.concatenate(pieces, 1)


def shape(*dims, dtype=jnp.float32):
    return jax.ShapeDtypeStruct(dims, dtype)


def body(operator_tiles, tile_slab, tile_column, tile_live, send_list, aggregate, null_modes):
    tiles = operator_tiles[0, 0]
    slab = tile_slab[0, 0].T
    column = tile_column[0, 0].T
    live = tile_live[0, 0].T
    send = send_list[0, 0]
    wide_odd = lax.axis_index("wide") % 2
    narrow_odd = lax.axis_index("narrow") % 2
    where = jnp.stack([wide_odd, narrow_odd]).astype(jnp.int32)

    own_modes, offered = pl.pallas_call(
        pack_kernel,
        out_shape=(shape(R, GROUP, BS), shape(S, GROUP, BS)),
        in_specs=[HBM] * 3,
        out_specs=(VMEM, VMEM),
        scratch_shapes=[
            pltpu.SMEM((S,), jnp.int32),
            pltpu.SMEM((R,), jnp.int32),
            pltpu.VMEM((MODES, R, BS), jnp.float32),
            pltpu.SemaphoreType.DMA((3,)),
        ],
        compiler_params=params(4),
        name="pack",
    )(
        *(
            pltpu.with_memory_space_constraint(x, pltpu.HBM)
            for x in (send, aggregate[0, 0], null_modes[0, 0].transpose(1, 0, 2))
        )
    )
    near, far = pair_halo(offered, "narrow")
    plan = pl.pallas_call(
        plan_kernel,
        out_shape=shape(16, LIST, dtype=jnp.int32),
        in_specs=[SMEM] + [HBM] * 4,
        out_specs=VMEM,
        scratch_shapes=[
            pltpu.VMEM((3, K, BS), jnp.int32),
            pltpu.VMEM((3, K, R), jnp.int32),
            pltpu.SMEM((S,), jnp.int32),
            pltpu.SemaphoreType.DMA((4,)),
        ],
        compiler_params=params(8),
        cost_estimate=pl.CostEstimate(flops=10**8, bytes_accessed=5 * 10**6, transcendentals=0),
        name="plan",
    )(where, *(pltpu.with_memory_space_constraint(x, pltpu.HBM) for x in (send, slab, column, live)))
    line = jnp.concatenate([offered, near, far], 0)
    line, plan = lax.optimization_barrier((line, plan))
    wide_near, wide_far = pair_halo(line, "wide")
    table = jnp.concatenate([own_modes, near, far, wide_near, wide_far], 0)

    tiles = tiles.reshape(R * K, BS, BS)
    resting = pltpu.with_memory_space_constraint(tiles, pltpu.HBM)
    taken = pltpu.VMEM((S * K, BS, BS), jnp.float32)
    scales = pltpu.VMEM((R, GROUP, BS), jnp.float32)
    halves, offered_scale = pl.pallas_call(
        bring_kernel,
        out_shape=(shape(S * K, BS, 2 * BS, dtype=jnp.bfloat16), shape(R, GROUP, BS)),
        in_specs=[SMEM, HBM],
        out_specs=(VMEM, VMEM),
        scratch_shapes=[taken, pltpu.SemaphoreType.DMA((S * K // UNROLL,))],
        compiler_params=params(24),
        cost_estimate=pl.CostEstimate(flops=10**8, bytes_accessed=10**7, transcendentals=0),
        name="bring",
    )(plan, resting)
    begun, message = pl.pallas_call(
        offer_kernel,
        out_shape=(shape(R * K, GROUP, BS), shape(BLOCK, BS)),
        in_specs=[SMEM, VMEM, VMEM, VMEM, VMEM],
        out_specs=(VMEM, VMEM),
        compiler_params=params(16),
        cost_estimate=pl.CostEstimate(flops=10**8, bytes_accessed=4 * 10**7, transcendentals=0),
        name="offer",
    )(plan, plan, halves, offered_scale, table)

    narrow_near, narrow_far = pair_halo(message, "narrow")
    wide_own = pair_far(message, "wide")
    prolong, blocks, weights = pl.pallas_call(
        rest_kernel,
        out_shape=(
            shape(R, 9 * C, BS),
            shape(2 * BLOCK, BS),
            shape(R, 256, 2 * BS, dtype=jnp.bfloat16),
        ),
        in_specs=[SMEM, VMEM, VMEM, VMEM, VMEM],
        out_specs=(HBM, VMEM, VMEM),
        scratch_shapes=[
            pltpu.VMEM((R, 9 * C, BS), jnp.float32),
            pltpu.VMEM((R * K, GROUP, BS), jnp.float32),
            scales,
            pltpu.VMEM((K, BS), jnp.int32),
            pltpu.SMEM((K, BS), jnp.int32),
            pltpu.VMEM((9 * AGG, GROUP, BS), jnp.float32),
            pltpu.VMEM((9 * AGG, GROUP, BS), jnp.float32),
            pltpu.SemaphoreType.DMA,
            pltpu.SemaphoreType.DMA((R,)),
        ],
        compiler_params=params(24),
        cost_estimate=pl.CostEstimate(flops=2 * 10**9, bytes_accessed=2 * 10**7, transcendentals=0),
        name="rest",
    )(plan, plan, tiles, table, begun)
    sides = jnp.concatenate([narrow_near, narrow_far], 0)
    line = jnp.concatenate([message, narrow_near, narrow_far], 0)
    line, sides, weights, wide_own = lax.optimization_barrier((line, sides, weights, wide_own))
    wide_near = pair_near(line, "wide")
    wide_far = pair_far(sides, "wide")

    def coupling(blocks):
        return [
            pltpu.VMEM((blocks * K, BS), jnp.int32),
            pltpu.SMEM((blocks * K, BS), jnp.int32),
            pltpu.VMEM((UNROLL * K * MODES, 3 * BS), jnp.bfloat16),
            pltpu.VMEM((UNROLL * K * MODES + GROUP, 256), jnp.float32),
            pltpu.VMEM((UNROLL * K * MODES + GROUP, 256), jnp.float32),
            [pltpu.VMEM((25 * AGG + 52, GROUP, 256), jnp.float32)] * 2,
        ]

    table = jnp.concatenate([blocks, narrow_near, narrow_far, wide_near, wide_own], 0)
    total = pl.pallas_call(
        beside_kernel,
        out_shape=shape(25 * AGG, GROUP, 256),
        in_specs=[SMEM] + [VMEM] * 3,
        out_specs=VMEM,
        scratch_shapes=coupling(8) + [pltpu.SemaphoreType.DMA],
        compiler_params=params(16),
        cost_estimate=pl.CostEstimate(flops=8 * 10**9, bytes_accessed=3 * 10**7, transcendentals=0),
        name="beside",
    )(plan, tiles, weights, table)
    own, near, far = pl.pallas_call(
        corner_kernel,
        out_shape=(shape(3 * C, 25 * C),) * 3,
        in_specs=[SMEM] + [VMEM] * 4,
        out_specs=(VMEM,) * 3,
        scratch_shapes=coupling(2)
        + [pltpu.VMEM((25 * C, 256), jnp.float32), pltpu.SemaphoreType.DMA],
        compiler_params=params(16),
        name="corner",
    )(plan, tiles, weights, total, wide_far)

    size = lax.axis_size("wide")
    pairs = [(i, i ^ 1) for i in range(size)]
    far_pairs = [(i, i + 1) if i % 2 else (i, i - 1) for i in range(1, size - 1)]
    near, far = lax.ppermute(near, "wide", pairs), lax.ppermute(far, "wide", far_pairs)
    own, near, far = pl.pallas_call(
        merge_kernel,
        out_shape=(shape(C, 35 * C),) * 3,
        in_specs=[SMEM] + [VMEM] * 3,
        out_specs=(VMEM,) * 3,
        compiler_params=params(4),
        name="merge",
    )(where, own, near, far)
    size = lax.axis_size("narrow")
    pairs = [(i, i ^ 1) for i in range(size)]
    far_pairs = [(i, i + 1) if i % 2 else (i, i - 1) for i in range(1, size - 1)]
    near, far = lax.ppermute(near, "narrow", pairs), lax.ppermute(far, "narrow", far_pairs)
    coarse = pl.pallas_call(
        place_kernel,
        out_shape=shape(C, 49 * C),
        in_specs=[SMEM] + [VMEM] * 3,
        out_specs=VMEM,
        compiler_params=params(4),
        name="place",
    )(where, own, near, far)
    return prolong[None, None], coarse[None, None]


def solution(mesh):
    in_specs = (
        P("wide", "narrow", None, None, None, None),
        P("wide", "narrow", None, None),
        P("wide", "narrow", None, None),
        P("wide", "narrow", None, None),
        P("wide", "narrow", None),
        P("wide", "narrow", None),
        P("wide", "narrow", None, None, None),
    )
    out_specs = (P("wide", "narrow", None, None, None), P("wide", "narrow", None, None))
    return jax.shard_map(body, mesh=mesh, in_specs=in_specs, out_specs=out_specs, check_vma=False)
```

time: 85.8 us -> 80.5 us (0.938)
  waiting for transfers between devices: 14.6 us -> 9.9 us
  starting transfers between devices: 27.2 us -> 29.3 us
  Pallas kernels: 40.2 us -> 38.5 us
  other arithmetic: 1.75 us -> 0.22 us
    ppermute x8 -> x9, waiting for transfers between devices: 7.88 us -> 0.39 us  [the longest x5 0.38 us: pair_far(): return lax.ppermute(block, axis, pairs)]
    ppermute x8 -> x9, starting transfers between devices: 16.4 us -> 23.4 us  [the longest x5 22.7 us: pair_far(): return lax.ppermute(block, axis, pairs)]
    pallas_call x0 -> x2, Pallas kernels: none -> 6.66 us  [the longest x1 4.62 us: body(): pl.pallas_call(bring_kernel, out_shape=(shape(S * K, BS, 2 * BS, dtype=jn...]
    pallas_call x1, Pallas kernels: 8.5 us -> 5.36 us  [body(): pl.pallas_call(corner_kernel, out_shape=(shape(3 * C, 25 * C),) * 3, in_s...]
    ppermute x1, starting transfers between devices: 5.01 us -> 2.16 us  [body(): lax.ppermute(far, 'narrow', far_pairs)]
    pallas_call x1, Pallas kernels: 9.08 us -> 6.65 us  [body(): pl.pallas_call(rest_kernel, out_shape=(shape(R, 9 * C, BS), shape(2 * BLO...]
    ppermute x1, waiting for transfers between devices: 0.01 us -> 2.3 us  [body(): lax.ppermute(near, 'narrow', pairs)]
    pallas_call x1, Pallas kernels: 5.5 us -> 3.35 us  [body(): pl.pallas_call(offer_kernel, out_shape=(shape(R * K, GROUP, BS), shape(BL...]
  transfers between devices with their start and end apart: 12 -> 13, of which waited for: 8 -> 5; matrix products, arithmetic and copies ran while one was open for 2% -> 1% of each run, Pallas kernels for 27% -> 34%
where the time goes in v3:
time: 80.5 us; the launch traced here: 79.2 us
  Pallas kernels  38.5 us (48%)
  starting transfers between devices  29.3 us (36%)
  waiting for transfers between devices  9.9 us (12%)
  between operations  0.97 us (1%)
    ppermute x5, starting transfers between devices, pair_far(): return lax.ppermute(block, axis, pairs)  22.7 us
    pallas_call x1, Pallas kernels, body(): pl.pallas_call(beside_kernel, out_shape=shape(25 * AGG, GROUP, 256), in_s...  13.3 us
    pallas_call x1, Pallas kernels, body(): pl.pallas_call(rest_kernel, out_shape=(shape(R, 9 * C, BS), shape(2 * BLO...  6.65 us
    pallas_call x1, Pallas kernels, body(): pl.pallas_call(corner_kernel, out_shape=(shape(3 * C, 25 * C),) * 3, in_s...  5.36 us
    ppermute x1, waiting for transfers between devices, body(): lax.ppermute(far, 'wide', far_pairs)  5.3 us
    pallas_call x1, Pallas kernels, body(): pl.pallas_call(bring_kernel, out_shape=(shape(S * K, BS, 2 * BS, dtype=jn...  4.62 us
    ppermute x1, starting transfers between devices, body(): lax.ppermute(far, 'wide', far_pairs)  3.57 us
    pallas_call x1, Pallas kernels, body(): pl.pallas_call(offer_kernel, out_shape=(shape(R * K, GROUP, BS), shape(BL...  3.35 us
  transfers between devices with their start and end apart: 13, of which 5 were waited for; matrix products, arithmetic and copies ran while one was open for 1% of the time, Pallas kernels for 34%

profile of v3, /device:TPU:14, one launch (start us, length us, event | category | flops | bytes accessed | tf_op | source)
XLA Modules:
  0.0 79.2 jit_solution(7015831385267476548)
XLA Ops:
  0.6 1.0 %pack.1 = (f32[32,8,128]{2,1,0:T(8,128)S(1)}, f32[16,8,128]{2,1,0:T(8,128)S(1)}) custom-call(s32[16]{0:T(128)} %bitcast.26, s32[32]{0:T(128)} %bitcast.25, f32[6,32,128]{2,1,0:T(8,128)} %bitcast.24), custom_call_target="tpu_custom_call" | custom-call | tf_op jit(solution)/shard_map/pack/pallas_call | solution.py:518
  1.7 0.5 collective-permute-start
  2.2 4.3 %collective-permute-start.1 = (f32[16,8,128]{2,1,0:T(8,128)S(1)}, f32[16,8,128]{2,1,0:T(8,128)S(1)}, u32[]{:S(2)}, u32[]{:S(2)}) collective-permute-start(f32[16,8,128]{2,1,0:T(8,128)S(1)} %get-tuple-element.23), channel_id=1, source_target_pairs={{1,2},{2,1},{5,6},{6,5},{9,10},{10,9},{13,14},{14,13},{17,18},{18,... | collective-permute-start | bytes 196616 | tf_op jit(solution)/shard_map/ppermute | solution.py:46
  6.5 0.1 pad_add_fusion.where
  6.6 2.0 %plan.1.ints = s32[16,384]{1,0:T(8,128)S(1)} custom-call(s32[2]{0:T(128)S(1)} %pad_add_fusion.where, s32[16]{0:T(128)} %bitcast.27, s32[8,32]{1,0:T(8,128)} %bitcast.29, s32[8,32]{1,0:T(8,128)} %bitcast.30, s32[8,32]{1,0:T(8,128)} %bitcast.31), custom_call_target="tpu_custom_call" | custom-call | flops 100000000 | bytes 5000000 | tf_op jit(solution)/shard_map/plan/pallas_call | solution.py:538
  8.7 0.0 collective-permute-done
  8.7 0.1 collective-permute-done.1
  8.8 0.1 collective-permute-start.2
  8.9 6.3 %collective-permute-start.3 = (f32[48,8,128]{2,1,0:T(8,128)S(1)}, f32[48,8,128]{2,1,0:T(8,128)S(1)}, u32[]{:S(2)}, u32[]{:S(2)}) collective-permute-start(f32[48,8,128]{2,1,0:T(8,128)S(1)} %pad_maximum_fusion.2), channel_id=1, source_target_pairs={{4,8},{8,4},{12,16},{16,12},{20,24},{24,20},{28,32},{32,28},{36,40... | collective-permute-start | bytes 589832 | tf_op jit(solution)/shard_map/ppermute | solution.py:46
  15.2 0.0 copy-start
  15.2 4.6 %bring.1 = (bf16[128,128,256]{2,1,0:T(8,128)(2,1)S(1)}, f32[32,8,128]{2,1,0:T(8,128)S(1)}) custom-call(s32[16,384]{1,0:T(8,128)S(1)} %plan.1.ints, f32[256,128,128]{2,1,0:T(8,128)} %bitcast.19), custom_call_target="tpu_custom_call" | custom-call | flops 100000000 | bytes 10000000 | tf_op jit(solution)/shard_map/bring/pallas_call | solution.py:562
  19.8 0.0 collective-permute-done.2
  19.9 0.0 collective-permute-done.3
  19.9 3.3 %offer.1 = (f32[256,8,128]{2,1,0:T(8,128)S(1)}, f32[776,128]{1,0:T(8,128)S(1)}) custom-call(s32[16,384]{1,0:T(8,128)S(1)} %plan.1.ints, s32[16,384]{1,0:T(8,128)S(1)} %plan.1.ints, bf16[128,128,256]{2,1,0:T(8,128)(2,1)S(1)} %get-tuple-element.27.halves, f32[32,8,128]{2,1,0:T(8,128)S(1)} %get-tuple-element.28.scale, ...), custom_call_target="tpu_custom_call" | custom-call | flops 100000000 | bytes 40000000 | tf_op jit(solution)/shard_map/offer/pallas_call | solution.py:572
  23.3 0.1 collective-permute-start.4
  23.4 3.9 %collective-permute-start.5 = (f32[776,128]{1,0:T(8,128)S(1)}, f32[776,128]{1,0:T(8,128)S(1)}, u32[]{:S(2)}, u32[]{:S(2)}) collective-permute-start(f32[776,128]{1,0:T(8,128)S(1)} %get-tuple-element.31), channel_id=1, source_target_pairs={{1,2},{2,1},{5,6},{6,5},{9,10},{10,9},{13,14},{14,13},{17,18},{18,... | collective-permute-start | bytes 1191944 | tf_op jit(solution)/shard_map/ppermute | solution.py:46
  27.3 4.1 %collective-permute-start.6 = (f32[776,128]{1,0:T(8,128)S(1)}, f32[776,128]{1,0:T(8,128)S(1)}, u32[]{:S(2)}, u32[]{:S(2)}) collective-permute-start(f32[776,128]{1,0:T(8,128)S(1)} %get-tuple-element.31), channel_id=1, source_target_pairs={{4,8},{8,4},{12,16},{16,12},{20,24},{24,20},{28,32},{32,28},{36,40... | collective-permute-start | bytes 1191944 | tf_op jit(solution)/shard_map/ppermute | solution.py:46
  31.4 0.0 copy-done
  31.4 6.7 %rest.1 = (f32[32,216,128]{2,1,0:T(8,128)}, f32[1552,128]{1,0:T(8,128)S(1)}, bf16[32,256,256]{2,1,0:T(8,128)(2,1)S(1)}) custom-call(s32[16,384]{1,0:T(8,128)S(1)} %plan.1.ints, s32[16,384]{1,0:T(8,128)S(1)} %plan.1.ints, f32[256,128,128]{2,1,0:T(8,128)S(1)} %bitcast.20, f32[160,8,128]{2,1,0:T(8,128)S(1)} %constant_dynamic-update-slice_fusion.table, ...), custom_call_target="tpu_custom_call" | custom-call | flops 2000000000 | bytes 20000000 | tf_op jit(solution)/shard_map/rest/pallas_call | solution.py:584
  38.0 0.0 collective-permute-done.4
  38.1 0.0 collective-permute-done.5
  38.1 0.1 pad_maximum_fusion.1
  38.1 0.1 pad_maximum_fusion
  38.2 0.3 collective-permute-done.6
  38.5 0.0 collective-permute-start.7
  38.5 0.1 constant_dynamic-update-slice_fusion.9
  38.6 4.1 %collective-permute-start.8 = (f32[1552,128]{1,0:T(8,128)S(1)}, f32[1552,128]{1,0:T(8,128)S(1)}, u32[]{:S(2)}, u32[]{:S(2)}) collective-permute-start(f32[1552,128]{1,0:T(8,128)S(1)} %pad_maximum_fusion.1), channel_id=1, source_target_pairs={{4,8},{8,4},{12,16},{16,12},{20,24},{24,20},{28,32},{32,28},{36,40... | collective-permute-start | bytes 2383880 | tf_op jit(solution)/shard_map/ppermute | solution.py:46
  42.8 0.0 collective-permute-done.7
  42.8 0.1 constant_dynamic-update-slice_fusion.6
  42.9 13.3 %beside.1.begun = f32[100,8,256]{2,1,0:T(8,128)S(1)} custom-call(s32[16,384]{1,0:T(8,128)S(1)} %plan.1.ints, f32[256,128,128]{2,1,0:T(8,128)S(1)} %bitcast.21, bf16[32,256,256]{2,1,0:T(8,128)(2,1)S(1)} %get-tuple-element.33.weights, f32[6208,128]{1,0:T(8,128)S(1)} %constant_dynamic-update-slice_fusion.5.table), custom_call_target="tpu_custom_call" | custom-call | flops 8000000000 | bytes 30000000 | tf_op jit(solution)/shard_map/beside/pallas_call | solution.py:625
  56.2 0.0 collective-permute-done.8.table
  56.2 5.4 %corner.1 = (f32[72,600]{1,0:T(8,128)S(1)}, f32[72,600]{1,0:T(8,128)S(1)}, f32[72,600]{1,0:T(8,128)S(1)}) custom-call(s32[16,384]{1,0:T(8,128)S(1)} %plan.1.ints, f32[256,128,128]{2,1,0:T(8,128)S(1)} %bitcast.22, bf16[32,256,256]{2,1,0:T(8,128)(2,1)S(1)} %get-tuple-element.33.weights, f32[100,8,256]{2,1,0:T(8,128)S(1)} %beside.1.begun, ...), custom_call_target="tpu_custom_call" | custom-call | tf_op jit(solution)/shard_map/corner/pallas_call | solution.py:635
  61.6 3.6 %collective-permute-start.10 = (f32[72,600]{1,0:T(8,128)S(1)}, f32[72,600]{1,0:T(8,128)S(1)}, u32[]{:S(2)}, u32[]{:S(2)}) collective-permute-start(f32[72,600]{1,0:T(8,128)S(1)} %get-tuple-element.40), channel_id=1, source_target_pairs={{4,8},{8,4},{12,16},{16,12},{20,24},{24,20},{28,32},{32,28},{36,40... | collective-permute-start | bytes 518408 | tf_op jit(solution)/shard_map/ppermute | solution.py:649
  65.2 0.1 collective-permute-start.9
  65.3 5.3 %collective-permute-done.10.far = f32[72,600]{1,0:T(8,128)S(1)} collective-permute-done((f32[72,600]{1,0:T(8,128)S(1)}, f32[72,600]{1,0:T(8,128)S(1)}, u32[]{:S(2)}, u32[]{:S(2)}) %collective-permute-start.10) | collective-permute-done | bytes 172832 | tf_op jit(solution)/shard_map/ppermute | solution.py:649
  70.6 0.0 collective-permute-done.9.near
  70.6 0.7 merge.1
  71.3 0.1 collective-permute-start.11
  71.4 2.2 %collective-permute-start.12 = (f32[24,840]{1,0:T(8,128)S(1)}, f32[24,840]{1,0:T(8,128)S(1)}, u32[]{:S(2)}, u32[]{:S(2)}) collective-permute-start(f32[24,840]{1,0:T(8,128)S(1)} %get-tuple-element.43), channel_id=1, source_target_pairs={{1,2},{2,1},{5,6},{6,5},{9,10},{10,9},{13,14},{14,13},{17,18},{18,... | collective-permute-start | bytes 241928 | tf_op jit(solution)/shard_map/ppermute | solution.py:661
  73.6 2.3 %collective-permute-done.11.near = f32[24,840]{1,0:T(8,128)S(1)} collective-permute-done((f32[24,840]{1,0:T(8,128)S(1)}, f32[24,840]{1,0:T(8,128)S(1)}, u32[]{:S(2)}, u32[]{:S(2)}) %collective-permute-start.11) | collective-permute-done | bytes 80672 | tf_op jit(solution)/shard_map/ppermute | solution.py:661
  75.9 1.9 %collective-permute-done.12.far = f32[24,840]{1,0:T(8,128)S(1)} collective-permute-done((f32[24,840]{1,0:T(8,128)S(1)}, f32[24,840]{1,0:T(8,128)S(1)}, u32[]{:S(2)}, u32[]{:S(2)}) %collective-permute-start.12) | collective-permute-done | bytes 80672 | tf_op jit(solution)/shard_map/ppermute | solution.py:661
  77.8 1.5 %place.1 = f32[24,1176]{1,0:T(8,128)} custom-call(s32[2]{0:T(128)S(1)} %pad_add_fusion.where, f32[24,840]{1,0:T(8,128)S(1)} %get-tuple-element.41.own, f32[24,840]{1,0:T(8,128)S(1)} %collective-permute-done.11.near, f32[24,840]{1,0:T(8,128)S(1)} %collective-permute-done.12.far), custom_call_target="tpu_custom_call" | custom-call | tf_op jit(solution)/shard_map/place/pallas_call | solution.py:662
  (9 shorter events, 0.2 us)
Async XLA Ops:
  1.7 7.0 %collective-permute-start = (f32[16,8,128]{2,1,0:T(8,128)S(1)}, f32[16,8,128]{2,1,0:T(8,128)S(1)}, u32[]{:S(2)}, u32[]{:S(2)}) collective-permute-start(f32[16,8,128]{2,1,0:T(8,128)S(1)} %get-tuple-element.23), channel_id=1, source_target_pairs={{0,1},{1,0},{2,3},{3,2},{4,5},{5,4},{6,7},{7,6},{8,9},{9,8},{10,11... | collective-permute-start | bytes 196616 | tf_op jit(solution)/shard_map/ppermute | solution.py:41
  2.2 6.5 %collective-permute-start.1 = (f32[16,8,128]{2,1,0:T(8,128)S(1)}, f32[16,8,128]{2,1,0:T(8,128)S(1)}, u32[]{:S(2)}, u32[]{:S(2)}) collective-permute-start(f32[16,8,128]{2,1,0:T(8,128)S(1)} %get-tuple-element.23), channel_id=1, source_target_pairs={{1,2},{2,1},{5,6},{6,5},{9,10},{10,9},{13,14},{14,13},{17,18},{18,... | collective-permute-start | bytes 196616 | tf_op jit(solution)/shard_map/ppermute | solution.py:46
  8.8 11.1 %collective-permute-start.2 = (f32[48,8,128]{2,1,0:T(8,128)S(1)}, f32[48,8,128]{2,1,0:T(8,128)S(1)}, u32[]{:S(2)}, u32[]{:S(2)}) collective-permute-start(f32[48,8,128]{2,1,0:T(8,128)S(1)} %pad_maximum_fusion.2), channel_id=1, source_target_pairs={{0,4},{4,0},{8,12},{12,8},{16,20},{20,16},{24,28},{28,24},{32,36},... | collective-permute-start | bytes 589832 | tf_op jit(solution)/shard_map/ppermute | solution.py:41
  8.9 11.0 %collective-permute-start.3 = (f32[48,8,128]{2,1,0:T(8,128)S(1)}, f32[48,8,128]{2,1,0:T(8,128)S(1)}, u32[]{:S(2)}, u32[]{:S(2)}) collective-permute-start(f32[48,8,128]{2,1,0:T(8,128)S(1)} %pad_maximum_fusion.2), channel_id=1, source_target_pairs={{4,8},{8,4},{12,16},{16,12},{20,24},{24,20},{28,32},{32,28},{36,40... | collective-permute-start | bytes 589832 | tf_op jit(solution)/shard_map/ppermute | solution.py:46
  15.2 16.2 %copy-start = (f32[1,1,32,8,128,128]{5,4,3,2,1,0:T(8,128)S(1)}, f32[1,1,32,8,128,128]{5,4,3,2,1,0:T(8,128)}, u32[]{:S(2)}) copy-start(f32[1,1,32,8,128,128]{5,4,3,2,1,0:T(8,128)} %param.7) | copy-start | bytes 50331652
  23.3 14.8 %collective-permute-start.4 = (f32[776,128]{1,0:T(8,128)S(1)}, f32[776,128]{1,0:T(8,128)S(1)}, u32[]{:S(2)}, u32[]{:S(2)}) collective-permute-start(f32[776,128]{1,0:T(8,128)S(1)} %get-tuple-element.31), channel_id=1, source_target_pairs={{0,1},{1,0},{2,3},{3,2},{4,5},{5,4},{6,7},{7,6},{8,9},{9,8},{10,11... | collective-permute-start | bytes 1191944 | tf_op jit(solution)/shard_map/ppermute | solution.py:41
  23.4 14.7 %collective-permute-start.5 = (f32[776,128]{1,0:T(8,128)S(1)}, f32[776,128]{1,0:T(8,128)S(1)}, u32[]{:S(2)}, u32[]{:S(2)}) collective-permute-start(f32[776,128]{1,0:T(8,128)S(1)} %get-tuple-element.31), channel_id=1, source_target_pairs={{1,2},{2,1},{5,6},{6,5},{9,10},{10,9},{13,14},{14,13},{17,18},{18,... | collective-permute-start | bytes 1191944 | tf_op jit(solution)/shard_map/ppermute | solution.py:46
  27.3 11.2 %collective-permute-start.6 = (f32[776,128]{1,0:T(8,128)S(1)}, f32[776,128]{1,0:T(8,128)S(1)}, u32[]{:S(2)}, u32[]{:S(2)}) collective-permute-start(f32[776,128]{1,0:T(8,128)S(1)} %get-tuple-element.31), channel_id=1, source_target_pairs={{4,8},{8,4},{12,16},{16,12},{20,24},{24,20},{28,32},{32,28},{36,40... | collective-permute-start | bytes 1191944 | tf_op jit(solution)/shard_map/ppermute | solution.py:46
  38.5 4.2 %collective-permute-start.7 = (f32[2328,128]{1,0:T(8,128)S(1)}, f32[2328,128]{1,0:T(8,128)S(1)}, u32[]{:S(2)}, u32[]{:S(2)}) collective-permute-start(f32[2328,128]{1,0:T(8,128)S(1)} %pad_maximum_fusion), channel_id=1, source_target_pairs={{0,4},{4,0},{8,12},{12,8},{16,20},{20,16},{24,28},{28,24},{32,36},... | collective-permute-start | bytes 3575816 | tf_op jit(solution)/shard_map/ppermute | solution.py:41
  38.6 17.7 %collective-permute-start.8 = (f32[1552,128]{1,0:T(8,128)S(1)}, f32[1552,128]{1,0:T(8,128)S(1)}, u32[]{:S(2)}, u32[]{:S(2)}) collective-permute-start(f32[1552,128]{1,0:T(8,128)S(1)} %pad_maximum_fusion.1), channel_id=1, source_target_pairs={{4,8},{8,4},{12,16},{16,12},{20,24},{24,20},{28,32},{32,28},{36,40... | collective-permute-start | bytes 2383880 | tf_op jit(solution)/shard_map/ppermute | solution.py:46
  61.6 9.0 %collective-permute-start.10 = (f32[72,600]{1,0:T(8,128)S(1)}, f32[72,600]{1,0:T(8,128)S(1)}, u32[]{:S(2)}, u32[]{:S(2)}) collective-permute-start(f32[72,600]{1,0:T(8,128)S(1)} %get-tuple-element.40), channel_id=1, source_target_pairs={{4,8},{8,4},{12,16},{16,12},{20,24},{24,20},{28,32},{32,28},{36,40... | collective-permute-start | bytes 518408 | tf_op jit(solution)/shard_map/ppermute | solution.py:649
  65.2 5.4 %collective-permute-start.9 = (f32[72,600]{1,0:T(8,128)S(1)}, f32[72,600]{1,0:T(8,128)S(1)}, u32[]{:S(2)}, u32[]{:S(2)}) collective-permute-start(f32[72,600]{1,0:T(8,128)S(1)} %get-tuple-element.39), channel_id=1, source_target_pairs={{0,4},{4,0},{8,12},{12,8},{16,20},{20,16},{24,28},{28,24},{32,36},... | collective-permute-start | bytes 518408 | tf_op jit(solution)/shard_map/ppermute | solution.py:649
  71.3 4.6 %collective-permute-start.11 = (f32[24,840]{1,0:T(8,128)S(1)}, f32[24,840]{1,0:T(8,128)S(1)}, u32[]{:S(2)}, u32[]{:S(2)}) collective-permute-start(f32[24,840]{1,0:T(8,128)S(1)} %get-tuple-element.42), channel_id=1, source_target_pairs={{0,1},{1,0},{2,3},{3,2},{4,5},{5,4},{6,7},{7,6},{8,9},{9,8},{10,11... | collective-permute-start | bytes 241928 | tf_op jit(solution)/shard_map/ppermute | solution.py:661
  71.4 6.4 %collective-permute-start.12 = (f32[24,840]{1,0:T(8,128)S(1)}, f32[24,840]{1,0:T(8,128)S(1)}, u32[]{:S(2)}, u32[]{:S(2)}) collective-permute-start(f32[24,840]{1,0:T(8,128)S(1)} %get-tuple-element.43), channel_id=1, source_target_pairs={{1,2},{2,1},{5,6},{6,5},{9,10},{10,9},{13,14},{14,13},{17,18},{18,... | collective-permute-start | bytes 241928 | tf_op jit(solution)/shard_map/ppermute | solution.py:661

commit v4 on v3

--- a/solution.py
+++ b/solution.py
@@ -19,6 +19,7 @@
 BLOCK = S * K * MODES + GROUP
 T_ENTRIES = R + 8 * S
 UNROLL = 16
+ROWS = 4
 SMOOTH = 32
 LIST = 384
 LISTS = K + 2
@@ -88,11 +89,11 @@
     window, col, used = wide[0], wide[1], wide[2]
     window_row = (window * 11) >> 5
     down, across = window_row - 1, window - 3 * window_row - 1
-    row_block = jnp.where(down == 0, 0, jnp.where(down == 1 - 2 * wide_odd, 1, 2))
-    col_block = jnp.where(across == 0, 0, jnp.where(across == 1 - 2 * narrow_odd, 1, 2))
-    block = 1 + 3 * row_block + col_block
+    is_near, is_far = down == 1 - 2 * wide_odd, down == 2 * wide_odd - 1
+    side = jnp.where(across == 0, 2, jnp.where(across == 1 - 2 * narrow_odd, 1, 0))
+    block = side + jnp.where(is_near, 7, jnp.where(is_far, 4, 2))
     source = jnp.where(window == 4, col, block * S + col)
-    kind = jnp.where(used == 0, 0, jnp.where((row_block == 2) & (across != 0), 2, 1))
+    kind = jnp.where(used == 0, 0, jnp.where(is_far & (across != 0), 2, 1))
     slot = lax.broadcasted_iota(jnp.int32, (K, BS), 0)
     lane = lax.broadcasted_iota(jnp.int32, (K, BS), 1)
     inside = lane < R
@@ -170,7 +171,7 @@
         numbers = jnp.where(first == 2 + i, total.astype(jnp.int32), numbers)
     plan[K + 1 : K + 2, 0:BS] = numbers
     start = 0
-    for i, ((_, length), block) in enumerate(zip(places, (0, 0, 0, 8))):
+    for i, ((_, length), block) in enumerate(zip(places, (0, 0, 0, 4))):
         part = slice(start, start + length)
         dummy = (25 << 16) + (block * S << 8)
         plan[LISTS + i : LISTS + i + 1, 0:length] = jnp.where(
@@ -252,14 +253,14 @@
     start(2)
     wait_batch(0, tiles, taken, sems)
     first()
-
-    def step(i, carry):
-        start(i + 2)
-        wait_batch(i, tiles, taken, sems)
-        then(i)
-        return carry
-
-    lax.fori_loop(1, steps, step, 0)
+    for i in range(1, S * K // UNROLL):
+
+        @pl.when(i < steps)
+        def _(i=i):
+            if i + 2 < S * K // UNROLL:
+                start(i + 2)
+            wait_batch(i, tiles, taken, sems)
+            then(i)
 
 
 def smooth_tiles(index, plan, tiles, table, slots, scale):
@@ -329,7 +330,7 @@
 
 def rest_kernel(
     plan, ints, tiles, table, begun, prolong_hbm, blocks, weights,
-    prolong, slots, scale, marks, lab, dense_even, dense_odd, sem, sems
+    prolong, slots, scale, marks, lab, dense_refs, sem, sems
 ):
     members = member_marks(ints, table)
     coarse = coarse_marks(ints, members)
@@ -346,8 +347,8 @@
         return pltpu.make_async_copy(prolong.at[b], prolong_hbm.at[b], sems.at[b])
 
     def rows(i, carry):
-        for j, dense in enumerate((dense_even, dense_odd)):
-            b = i * 2 + j
+        for j, dense in enumerate(dense_refs):
+            b = i * ROWS + j
             dense[...] = jnp.zeros_like(dense)
             for k in range(K):
                 dense[lab[k, b]] += slots[b * K + k]
@@ -360,11 +361,11 @@
             high, low = split(prolong[b])
             weights[b, 0 : 9 * C, 0:BS] = high
             weights[b, 0 : 9 * C, BS:] = low
-        for j in range(2):
-            send_row(i * 2 + j).start()
+        for j in range(ROWS):
+            send_row(i * ROWS + j).start()
         return carry
 
-    lax.fori_loop(0, R // 2, rows, 0)
+    lax.fori_loop(0, R // ROWS, rows, 0)
 
     def finish(b, carry):
         send_row(b).wait()
@@ -452,7 +453,7 @@
     totals[0][0 : 25 * AGG] = begun[...]
     totals[1][0 : 25 * AGG] = jnp.zeros((25 * AGG, GROUP, 256), jnp.float32)
     couple_tiles(
-        3, plan, 8, tiles, weights, table, marks, lab, parts, products, last, totals, sem
+        3, plan, 4, tiles, weights, table, marks, lab, parts, products, last, totals, sem
     )
     for g in range(25 * AGG):
         turned[MODES * g : MODES * (g + 1), :] = totals[0][g, :MODES, :] + totals[1][g, :MODES, :]
@@ -464,13 +465,13 @@
     far_out[...] = jnp.where(even, low, top)
 
 
-def merge_kernel(where, own, near, far, own_out, near_out, far_out):
+def merge_kernel(where, blocks, own_out, near_out, far_out):
     even = where[0] == 0
     span = 5 * C
-    low = jnp.where(even, near[...], far[...])
-    top = jnp.where(even, far[...], near[...])
+    mid, near, far = (blocks[3 * C * i : 3 * C * (i + 1), :] for i in range(3))
+    low = jnp.where(even, near, far)
+    top = jnp.where(even, far, near)
     zeros = jnp.zeros((3 * C, span), jnp.float32)
-    mid = own[...]
     length = 5 * span
     summed = (
         jnp.concatenate([top[:, :length], zeros, zeros], 1)
@@ -550,10 +551,10 @@
         cost_estimate=pl.CostEstimate(flops=10**8, bytes_accessed=5 * 10**6, transcendentals=0),
         name="plan",
     )(where, *(pltpu.with_memory_space_constraint(x, pltpu.HBM) for x in (send, slab, column, live)))
-    line = jnp.concatenate([offered, near, far], 0)
+    line = jnp.concatenate([far, near, offered], 0)
     line, plan = lax.optimization_barrier((line, plan))
     wide_near, wide_far = pair_halo(line, "wide")
-    table = jnp.concatenate([own_modes, near, far, wide_near, wide_far], 0)
+    table = jnp.concatenate([own_modes, far, near, wide_far, wide_near], 0)
 
     tiles = tiles.reshape(R * K, BS, BS)
     resting = pltpu.with_memory_space_constraint(tiles, pltpu.HBM)
@@ -596,8 +597,7 @@
             scales,
             pltpu.VMEM((K, BS), jnp.int32),
             pltpu.SMEM((K, BS), jnp.int32),
-            pltpu.VMEM((9 * AGG, GROUP, BS), jnp.float32),
-            pltpu.VMEM((9 * AGG, GROUP, BS), jnp.float32),
+            [pltpu.VMEM((9 * AGG, GROUP, BS), jnp.float32)] * ROWS,
             pltpu.SemaphoreType.DMA,
             pltpu.SemaphoreType.DMA((R,)),
         ],
@@ -605,8 +605,8 @@
         cost_estimate=pl.CostEstimate(flops=2 * 10**9, bytes_accessed=2 * 10**7, transcendentals=0),
         name="rest",
     )(plan, plan, tiles, table, begun)
-    sides = jnp.concatenate([narrow_near, narrow_far], 0)
-    line = jnp.concatenate([message, narrow_near, narrow_far], 0)
+    sides = jnp.concatenate([narrow_far, narrow_near], 0)
+    line = jnp.concatenate([narrow_far, narrow_near, message], 0)
     line, sides, weights, wide_own = lax.optimization_barrier((line, sides, weights, wide_own))
     wide_near = pair_near(line, "wide")
     wide_far = pair_far(sides, "wide")
@@ -621,13 +621,13 @@
             [pltpu.VMEM((25 * AGG + 52, GROUP, 256), jnp.float32)] * 2,
         ]
 
-    table = jnp.concatenate([blocks, narrow_near, narrow_far, wide_near, wide_own], 0)
+    table = jnp.concatenate([blocks, sides, sides, wide_own, wide_near], 0)
     total = pl.pallas_call(
         beside_kernel,
         out_shape=shape(25 * AGG, GROUP, 256),
         in_specs=[SMEM] + [VMEM] * 3,
         out_specs=VMEM,
-        scratch_shapes=coupling(8) + [pltpu.SemaphoreType.DMA],
+        scratch_shapes=coupling(10) + [pltpu.SemaphoreType.DMA],
         compiler_params=params(16),
         cost_estimate=pl.CostEstimate(flops=8 * 10**9, bytes_accessed=3 * 10**7, transcendentals=0),
         name="beside",
@@ -650,11 +650,11 @@
     own, near, far = pl.pallas_call(
         merge_kernel,
         out_shape=(shape(C, 35 * C),) * 3,
-        in_specs=[SMEM] + [VMEM] * 3,
+        in_specs=[SMEM, VMEM],
         out_specs=(VMEM,) * 3,
         compiler_params=params(4),
         name="merge",
-    )(where, own, near, far)
+    )(where, jnp.concatenate([own, near, far], 0))
     size = lax.axis_size("narrow")
     pairs = [(i, i ^ 1) for i in range(size)]
     far_pairs = [(i, i + 1) if i % 2 else (i, i - 1) for i in range(1, size - 1)]

time: 80.5 us -> 78.4 us (0.974)
  starting transfers between devices: 29.3 us -> 27.4 us
    ppermute x5, starting transfers between devices: 22.7 us -> 19.5 us  [pair_far(): return lax.ppermute(block, axis, pairs)]
    ppermute x1, waiting for transfers between devices: 5.3 us -> 3.67 us  [body(): lax.ppermute(far, 'wide', far_pairs)]
    ppermute x1, starting transfers between devices: 3.57 us -> 5.19 us  [body(): lax.ppermute(far, 'wide', far_pairs)]
    ppermute x5, waiting for transfers between devices: 0.38 us -> 1.61 us  [pair_far(): return lax.ppermute(block, axis, pairs)]
  transfers between devices with their start and end apart: 13 -> 13, of which waited for: 5 -> 6; matrix products, arithmetic and copies ran while one was open for 1% -> 1% of each run, Pallas kernels for 34% -> 34%
where the time goes in v4:
time: 78.4 us; the launch traced here: 77.3 us
  Pallas kernels  38.6 us (49%)
  starting transfers between devices  27.4 us (35%)
  waiting for transfers between devices  9.75 us (12%)
  between operations  0.96 us (1%)
    ppermute x5, starting transfers between devices, pair_far(): return lax.ppermute(block, axis, pairs)  19.5 us
    pallas_call x1, Pallas kernels, body(): pl.pallas_call(beside_kernel, out_shape=shape(25 * AGG, GROUP, 256), in_s...  13.5 us
    pallas_call x1, Pallas kernels, body(): pl.pallas_call(rest_kernel, out_shape=(shape(R, 9 * C, BS), shape(2 * BLO...  5.93 us
    pallas_call x1, Pallas kernels, body(): pl.pallas_call(corner_kernel, out_shape=(shape(3 * C, 25 * C),) * 3, in_s...  5.36 us
    pallas_call x1, Pallas kernels, body(): pl.pallas_call(bring_kernel, out_shape=(shape(S * K, BS, 2 * BS, dtype=jn...  5.24 us
    ppermute x1, starting transfers between devices, body(): lax.ppermute(far, 'wide', far_pairs)  5.19 us
    ppermute x1, waiting for transfers between devices, body(): lax.ppermute(far, 'wide', far_pairs)  3.67 us
    pallas_call x1, Pallas kernels, body(): pl.pallas_call(offer_kernel, out_shape=(shape(R * K, GROUP, BS), shape(BL...  3.35 us
  transfers between devices with their start and end apart: 13, of which 6 were waited for; matrix products, arithmetic and copies ran while one was open for 1% of the time, Pallas kernels for 34%

profile of v4, /device:TPU:14, one launch (start us, length us, event | category | flops | bytes accessed | tf_op | source)
XLA Modules:
  0.0 77.3 jit_solution(8150910962952972540)
XLA Ops:
  0.6 1.0 %pack.1 = (f32[32,8,128]{2,1,0:T(8,128)S(1)}, f32[16,8,128]{2,1,0:T(8,128)S(1)}) custom-call(s32[16]{0:T(128)} %bitcast.26, s32[32]{0:T(128)} %bitcast.25, f32[6,32,128]{2,1,0:T(8,128)} %bitcast.24), custom_call_target="tpu_custom_call" | custom-call | tf_op jit(solution)/shard_map/pack/pallas_call | solution.py:519
  1.7 0.5 collective-permute-start.1
  2.2 4.3 %collective-permute-start = (f32[16,8,128]{2,1,0:T(8,128)S(1)}, f32[16,8,128]{2,1,0:T(8,128)S(1)}, u32[]{:S(2)}, u32[]{:S(2)}) collective-permute-start(f32[16,8,128]{2,1,0:T(8,128)S(1)} %get-tuple-element.23), channel_id=1, source_target_pairs={{1,2},{2,1},{5,6},{6,5},{9,10},{10,9},{13,14},{14,13},{17,18},{18,... | collective-permute-start | bytes 196616 | tf_op jit(solution)/shard_map/ppermute | solution.py:47
  6.5 0.1 pad_add_fusion.where
  6.6 2.0 %plan.1.ints = s32[16,384]{1,0:T(8,128)S(1)} custom-call(s32[2]{0:T(128)S(1)} %pad_add_fusion.where, s32[16]{0:T(128)} %bitcast.27, s32[8,32]{1,0:T(8,128)} %bitcast.29, s32[8,32]{1,0:T(8,128)} %bitcast.30, s32[8,32]{1,0:T(8,128)} %bitcast.31), custom_call_target="tpu_custom_call" | custom-call | flops 100000000 | bytes 5000000 | tf_op jit(solution)/shard_map/plan/pallas_call | solution.py:539
  8.7 0.0 collective-permute-done.1
  8.7 0.1 collective-permute-done
  8.8 5.0 %collective-permute-start.2 = (f32[48,8,128]{2,1,0:T(8,128)S(1)}, f32[48,8,128]{2,1,0:T(8,128)S(1)}, u32[]{:S(2)}, u32[]{:S(2)}) collective-permute-start(f32[48,8,128]{2,1,0:T(8,128)S(1)} %pad_maximum_fusion.3), channel_id=1, source_target_pairs={{4,8},{8,4},{12,16},{16,12},{20,24},{24,20},{28,32},{32,28},{36,40... | collective-permute-start | bytes 589832 | tf_op jit(solution)/shard_map/ppermute | solution.py:47
  13.8 0.1 collective-permute-start.3
  13.9 0.0 copy-start
  13.9 5.2 %bring.1 = (bf16[128,128,256]{2,1,0:T(8,128)(2,1)S(1)}, f32[32,8,128]{2,1,0:T(8,128)S(1)}) custom-call(s32[16,384]{1,0:T(8,128)S(1)} %plan.1.ints, f32[256,128,128]{2,1,0:T(8,128)} %bitcast.19), custom_call_target="tpu_custom_call" | custom-call | flops 100000000 | bytes 10000000 | tf_op jit(solution)/shard_map/bring/pallas_call | solution.py:563
  19.2 0.0 collective-permute-done.2
  19.2 0.0 collective-permute-done.3
  19.3 3.3 %offer.1 = (f32[256,8,128]{2,1,0:T(8,128)S(1)}, f32[776,128]{1,0:T(8,128)S(1)}) custom-call(s32[16,384]{1,0:T(8,128)S(1)} %plan.1.ints, s32[16,384]{1,0:T(8,128)S(1)} %plan.1.ints, bf16[128,128,256]{2,1,0:T(8,128)(2,1)S(1)} %get-tuple-element.27.halves, f32[32,8,128]{2,1,0:T(8,128)S(1)} %get-tuple-element.28.scale, ...), custom_call_target="tpu_custom_call" | custom-call | flops 100000000 | bytes 40000000 | tf_op jit(solution)/shard_map/offer/pallas_call | solution.py:573
  22.6 0.1 collective-permute-start.5
  22.7 2.9 %collective-permute-start.4 = (f32[776,128]{1,0:T(8,128)S(1)}, f32[776,128]{1,0:T(8,128)S(1)}, u32[]{:S(2)}, u32[]{:S(2)}) collective-permute-start(f32[776,128]{1,0:T(8,128)S(1)} %get-tuple-element.31), channel_id=1, source_target_pairs={{1,2},{2,1},{5,6},{6,5},{9,10},{10,9},{13,14},{14,13},{17,18},{18,... | collective-permute-start | bytes 1191944 | tf_op jit(solution)/shard_map/ppermute | solution.py:47
  25.6 3.6 %collective-permute-start.6 = (f32[776,128]{1,0:T(8,128)S(1)}, f32[776,128]{1,0:T(8,128)S(1)}, u32[]{:S(2)}, u32[]{:S(2)}) collective-permute-start(f32[776,128]{1,0:T(8,128)S(1)} %get-tuple-element.31), channel_id=1, source_target_pairs={{4,8},{8,4},{12,16},{16,12},{20,24},{24,20},{28,32},{32,28},{36,40... | collective-permute-start | bytes 1191944 | tf_op jit(solution)/shard_map/ppermute | solution.py:47
  29.2 0.0 copy-done
  29.3 5.9 %rest.1 = (f32[32,216,128]{2,1,0:T(8,128)}, f32[1552,128]{1,0:T(8,128)S(1)}, bf16[32,256,256]{2,1,0:T(8,128)(2,1)S(1)}) custom-call(s32[16,384]{1,0:T(8,128)S(1)} %plan.1.ints, s32[16,384]{1,0:T(8,128)S(1)} %plan.1.ints, f32[256,128,128]{2,1,0:T(8,128)S(1)} %bitcast.20, f32[160,8,128]{2,1,0:T(8,128)S(1)} %constant_dynamic-update-slice_fusion.table, ...), custom_call_target="tpu_custom_call" | custom-call | flops 2000000000 | bytes 20000000 | tf_op jit(solution)/shard_map/rest/pallas_call | solution.py:585
  35.2 0.0 collective-permute-done.5
  35.2 0.4 collective-permute-done.4
  35.6 0.1 pad_maximum_fusion.1
  35.6 0.1 pad_maximum_fusion
  35.7 1.2 %collective-permute-done.6 = f32[776,128]{1,0:T(8,128)S(1)} collective-permute-done((f32[776,128]{1,0:T(8,128)S(1)}, f32[776,128]{1,0:T(8,128)S(1)}, u32[]{:S(2)}, u32[]{:S(2)}) %collective-permute-start.6) | collective-permute-done | bytes 397344 | tf_op jit(solution)/shard_map/ppermute | solution.py:47
  36.9 0.0 collective-permute-start.7
  36.9 0.1 constant_dynamic-update-slice_fusion.9
  36.9 3.6 %collective-permute-start.8 = (f32[1552,128]{1,0:T(8,128)S(1)}, f32[1552,128]{1,0:T(8,128)S(1)}, u32[]{:S(2)}, u32[]{:S(2)}) collective-permute-start(f32[1552,128]{1,0:T(8,128)S(1)} %pad_maximum_fusion.1), channel_id=1, source_target_pairs={{4,8},{8,4},{12,16},{16,12},{20,24},{24,20},{28,32},{32,28},{36,40... | collective-permute-start | bytes 2383880 | tf_op jit(solution)/shard_map/ppermute | solution.py:47
  40.5 0.1 constant_dynamic-update-slice_fusion.8
  40.6 0.1 constant_dynamic-update-slice_fusion.7
  40.7 0.0 collective-permute-done.7
  40.7 0.1 constant_dynamic-update-slice_fusion.5.table
  40.8 13.5 %beside.1.begun = f32[100,8,256]{2,1,0:T(8,128)S(1)} custom-call(s32[16,384]{1,0:T(8,128)S(1)} %plan.1.ints, f32[256,128,128]{2,1,0:T(8,128)S(1)} %bitcast.21, bf16[32,256,256]{2,1,0:T(8,128)(2,1)S(1)} %get-tuple-element.33.weights, f32[7760,128]{1,0:T(8,128)S(1)} %constant_dynamic-update-slice_fusion.5.table), custom_call_target="tpu_custom_call" | custom-call | flops 8000000000 | bytes 30000000 | tf_op jit(solution)/shard_map/beside/pallas_call | solution.py:625
  54.3 0.0 collective-permute-done.8.table
  54.3 5.4 %corner.1 = (f32[72,600]{1,0:T(8,128)S(1)}, f32[72,600]{1,0:T(8,128)S(1)}, f32[72,600]{1,0:T(8,128)S(1)}) custom-call(s32[16,384]{1,0:T(8,128)S(1)} %plan.1.ints, f32[256,128,128]{2,1,0:T(8,128)S(1)} %bitcast.22, bf16[32,256,256]{2,1,0:T(8,128)(2,1)S(1)} %get-tuple-element.33.weights, f32[100,8,256]{2,1,0:T(8,128)S(1)} %beside.1.begun, ...), custom_call_target="tpu_custom_call" | custom-call | tf_op jit(solution)/shard_map/corner/pallas_call | solution.py:635
  59.7 5.2 %collective-permute-start.10 = (f32[72,600]{1,0:T(8,128)S(1)}, f32[72,600]{1,0:T(8,128)S(1)}, u32[]{:S(2)}, u32[]{:S(2)}) collective-permute-start(f32[72,600]{1,0:T(8,128)S(1)} %get-tuple-element.40), channel_id=1, source_target_pairs={{4,8},{8,4},{12,16},{16,12},{20,24},{24,20},{28,32},{32,28},{36,40... | collective-permute-start | bytes 518408 | tf_op jit(solution)/shard_map/ppermute | solution.py:649
  64.9 0.1 collective-permute-start.9
  64.9 3.7 %collective-permute-done.10 = f32[72,600]{1,0:T(8,128)S(1)} collective-permute-done((f32[72,600]{1,0:T(8,128)S(1)}, f32[72,600]{1,0:T(8,128)S(1)}, u32[]{:S(2)}, u32[]{:S(2)}) %collective-permute-start.10) | collective-permute-done | bytes 172832 | tf_op jit(solution)/shard_map/ppermute | solution.py:649
  68.6 0.0 collective-permute-done.9
  68.7 0.7 merge.1
  69.4 0.1 collective-permute-start.11
  69.5 1.9 %collective-permute-start.12 = (f32[24,840]{1,0:T(8,128)S(1)}, f32[24,840]{1,0:T(8,128)S(1)}, u32[]{:S(2)}, u32[]{:S(2)}) collective-permute-start(f32[24,840]{1,0:T(8,128)S(1)} %get-tuple-element.43), channel_id=1, source_target_pairs={{1,2},{2,1},{5,6},{6,5},{9,10},{10,9},{13,14},{14,13},{17,18},{18,... | collective-permute-start | bytes 241928 | tf_op jit(solution)/shard_map/ppermute | solution.py:661
  71.4 2.5 %collective-permute-done.11.near = f32[24,840]{1,0:T(8,128)S(1)} collective-permute-done((f32[24,840]{1,0:T(8,128)S(1)}, f32[24,840]{1,0:T(8,128)S(1)}, u32[]{:S(2)}, u32[]{:S(2)}) %collective-permute-start.11) | collective-permute-done | bytes 80672 | tf_op jit(solution)/shard_map/ppermute | solution.py:661
  73.9 1.9 %collective-permute-done.12.far = f32[24,840]{1,0:T(8,128)S(1)} collective-permute-done((f32[24,840]{1,0:T(8,128)S(1)}, f32[24,840]{1,0:T(8,128)S(1)}, u32[]{:S(2)}, u32[]{:S(2)}) %collective-permute-start.12) | collective-permute-done | bytes 80672 | tf_op jit(solution)/shard_map/ppermute | solution.py:661
  75.8 1.5 %place.1 = f32[24,1176]{1,0:T(8,128)} custom-call(s32[2]{0:T(128)S(1)} %pad_add_fusion.where, f32[24,840]{1,0:T(8,128)S(1)} %get-tuple-element.41.own, f32[24,840]{1,0:T(8,128)S(1)} %collective-permute-done.11.near, f32[24,840]{1,0:T(8,128)S(1)} %collective-permute-done.12.far), custom_call_target="tpu_custom_call" | custom-call | tf_op jit(solution)/shard_map/place/pallas_call | solution.py:662
  (8 shorter events, 0.1 us)
Async XLA Ops:
  1.7 7.0 %collective-permute-start.1 = (f32[16,8,128]{2,1,0:T(8,128)S(1)}, f32[16,8,128]{2,1,0:T(8,128)S(1)}, u32[]{:S(2)}, u32[]{:S(2)}) collective-permute-start(f32[16,8,128]{2,1,0:T(8,128)S(1)} %get-tuple-element.23), channel_id=1, source_target_pairs={{0,1},{1,0},{2,3},{3,2},{4,5},{5,4},{6,7},{7,6},{8,9},{9,8},{10,11... | collective-permute-start | bytes 196616 | tf_op jit(solution)/shard_map/ppermute | solution.py:42
  2.2 6.5 %collective-permute-start = (f32[16,8,128]{2,1,0:T(8,128)S(1)}, f32[16,8,128]{2,1,0:T(8,128)S(1)}, u32[]{:S(2)}, u32[]{:S(2)}) collective-permute-start(f32[16,8,128]{2,1,0:T(8,128)S(1)} %get-tuple-element.23), channel_id=1, source_target_pairs={{1,2},{2,1},{5,6},{6,5},{9,10},{10,9},{13,14},{14,13},{17,18},{18,... | collective-permute-start | bytes 196616 | tf_op jit(solution)/shard_map/ppermute | solution.py:47
  8.8 10.4 %collective-permute-start.2 = (f32[48,8,128]{2,1,0:T(8,128)S(1)}, f32[48,8,128]{2,1,0:T(8,128)S(1)}, u32[]{:S(2)}, u32[]{:S(2)}) collective-permute-start(f32[48,8,128]{2,1,0:T(8,128)S(1)} %pad_maximum_fusion.3), channel_id=1, source_target_pairs={{4,8},{8,4},{12,16},{16,12},{20,24},{24,20},{28,32},{32,28},{36,40... | collective-permute-start | bytes 589832 | tf_op jit(solution)/shard_map/ppermute | solution.py:47
  13.8 5.4 %collective-permute-start.3 = (f32[48,8,128]{2,1,0:T(8,128)S(1)}, f32[48,8,128]{2,1,0:T(8,128)S(1)}, u32[]{:S(2)}, u32[]{:S(2)}) collective-permute-start(f32[48,8,128]{2,1,0:T(8,128)S(1)} %pad_maximum_fusion.3), channel_id=1, source_target_pairs={{0,4},{4,0},{8,12},{12,8},{16,20},{20,16},{24,28},{28,24},{32,36},... | collective-permute-start | bytes 589832 | tf_op jit(solution)/shard_map/ppermute | solution.py:42
  13.9 15.3 %copy-start = (f32[1,1,32,8,128,128]{5,4,3,2,1,0:T(8,128)S(1)}, f32[1,1,32,8,128,128]{5,4,3,2,1,0:T(8,128)}, u32[]{:S(2)}) copy-start(f32[1,1,32,8,128,128]{5,4,3,2,1,0:T(8,128)} %param.7) | copy-start | bytes 50331652
  22.6 12.6 %collective-permute-start.5 = (f32[776,128]{1,0:T(8,128)S(1)}, f32[776,128]{1,0:T(8,128)S(1)}, u32[]{:S(2)}, u32[]{:S(2)}) collective-permute-start(f32[776,128]{1,0:T(8,128)S(1)} %get-tuple-element.31), channel_id=1, source_target_pairs={{0,1},{1,0},{2,3},{3,2},{4,5},{5,4},{6,7},{7,6},{8,9},{9,8},{10,11... | collective-permute-start | bytes 1191944 | tf_op jit(solution)/shard_map/ppermute | solution.py:42
  22.7 12.9 %collective-permute-start.4 = (f32[776,128]{1,0:T(8,128)S(1)}, f32[776,128]{1,0:T(8,128)S(1)}, u32[]{:S(2)}, u32[]{:S(2)}) collective-permute-start(f32[776,128]{1,0:T(8,128)S(1)} %get-tuple-element.31), channel_id=1, source_target_pairs={{1,2},{2,1},{5,6},{6,5},{9,10},{10,9},{13,14},{14,13},{17,18},{18,... | collective-permute-start | bytes 1191944 | tf_op jit(solution)/shard_map/ppermute | solution.py:47
  25.6 11.2 %collective-permute-start.6 = (f32[776,128]{1,0:T(8,128)S(1)}, f32[776,128]{1,0:T(8,128)S(1)}, u32[]{:S(2)}, u32[]{:S(2)}) collective-permute-start(f32[776,128]{1,0:T(8,128)S(1)} %get-tuple-element.31), channel_id=1, source_target_pairs={{4,8},{8,4},{12,16},{16,12},{20,24},{24,20},{28,32},{32,28},{36,40... | collective-permute-start | bytes 1191944 | tf_op jit(solution)/shard_map/ppermute | solution.py:47
  36.9 3.8 %collective-permute-start.7 = (f32[2328,128]{1,0:T(8,128)S(1)}, f32[2328,128]{1,0:T(8,128)S(1)}, u32[]{:S(2)}, u32[]{:S(2)}) collective-permute-start(f32[2328,128]{1,0:T(8,128)S(1)} %pad_maximum_fusion), channel_id=1, source_target_pairs={{0,4},{4,0},{8,12},{12,8},{16,20},{20,16},{24,28},{28,24},{32,36},... | collective-permute-start | bytes 3575816 | tf_op jit(solution)/shard_map/ppermute | solution.py:42
  36.9 17.3 %collective-permute-start.8 = (f32[1552,128]{1,0:T(8,128)S(1)}, f32[1552,128]{1,0:T(8,128)S(1)}, u32[]{:S(2)}, u32[]{:S(2)}) collective-permute-start(f32[1552,128]{1,0:T(8,128)S(1)} %pad_maximum_fusion.1), channel_id=1, source_target_pairs={{4,8},{8,4},{12,16},{16,12},{20,24},{24,20},{28,32},{32,28},{36,40... | collective-permute-start | bytes 2383880 | tf_op jit(solution)/shard_map/ppermute | solution.py:47
  59.7 9.0 %collective-permute-start.10 = (f32[72,600]{1,0:T(8,128)S(1)}, f32[72,600]{1,0:T(8,128)S(1)}, u32[]{:S(2)}, u32[]{:S(2)}) collective-permute-start(f32[72,600]{1,0:T(8,128)S(1)} %get-tuple-element.40), channel_id=1, source_target_pairs={{4,8},{8,4},{12,16},{16,12},{20,24},{24,20},{28,32},{32,28},{36,40... | collective-permute-start | bytes 518408 | tf_op jit(solution)/shard_map/ppermute | solution.py:649
  64.9 3.8 %collective-permute-start.9 = (f32[72,600]{1,0:T(8,128)S(1)}, f32[72,600]{1,0:T(8,128)S(1)}, u32[]{:S(2)}, u32[]{:S(2)}) collective-permute-start(f32[72,600]{1,0:T(8,128)S(1)} %get-tuple-element.39), channel_id=1, source_target_pairs={{0,4},{4,0},{8,12},{12,8},{16,20},{20,16},{24,28},{28,24},{32,36},... | collective-permute-start | bytes 518408 | tf_op jit(solution)/shard_map/ppermute | solution.py:649
  69.4 4.6 %collective-permute-start.11 = (f32[24,840]{1,0:T(8,128)S(1)}, f32[24,840]{1,0:T(8,128)S(1)}, u32[]{:S(2)}, u32[]{:S(2)}) collective-permute-start(f32[24,840]{1,0:T(8,128)S(1)} %get-tuple-element.42), channel_id=1, source_target_pairs={{0,1},{1,0},{2,3},{3,2},{4,5},{5,4},{6,7},{7,6},{8,9},{9,8},{10,11... | collective-permute-start | bytes 241928 | tf_op jit(solution)/shard_map/ppermute | solution.py:661
  69.5 6.4 %collective-permute-start.12 = (f32[24,840]{1,0:T(8,128)S(1)}, f32[24,840]{1,0:T(8,128)S(1)}, u32[]{:S(2)}, u32[]{:S(2)}) collective-permute-start(f32[24,840]{1,0:T(8,128)S(1)} %get-tuple-element.43), channel_id=1, source_target_pairs={{1,2},{2,1},{5,6},{6,5},{9,10},{10,9},{13,14},{14,13},{17,18},{18,... | collective-permute-start | bytes 241928 | tf_op jit(solution)/shard_map/ppermute | solution.py:661

commit v5 on v4

--- a/solution.py
+++ b/solution.py
@@ -52,11 +52,21 @@
     return pair_near(block, axis), far
 
 
-def pack_kernel(send_hbm, aggregate_hbm, modes_hbm, own, message, send, aggregate, modes, sems):
+def pack_kernel(
+    send_hbm, aggregate_hbm, modes_hbm, slab, column, live, own, message, raw, rows,
+    send, aggregate, modes, sems
+):
     copies = [
         pltpu.make_async_copy(source, target, sems.at[i])
         for i, (source, target) in enumerate(
-            ((modes_hbm, modes), (aggregate_hbm, aggregate), (send_hbm, send))
+            (
+                (modes_hbm, modes),
+                (aggregate_hbm, aggregate),
+                (send_hbm, send),
+                (slab, raw.at[0]),
+                (column, raw.at[1]),
+                (live, raw.at[2]),
+            )
         )
     ]
     for copy in copies:
@@ -68,23 +78,19 @@
             own[b, m] = modes[m, b]
         own[b, MODES] = jnp.full((BS,), aggregate[b].astype(jnp.float32))
         own[b, MODES + 1] = jnp.zeros((BS,), jnp.float32)
+    lane = lax.broadcasted_iota(jnp.int32, (1, BS), 1)
+    sent = jnp.zeros((1, BS), jnp.int32)
+    offered = jnp.zeros((1, BS), jnp.int32)
     for s in range(S):
         message[s] = own[send[s]]
-
-
-def plan_kernel(where, send_hbm, slab, column, live, plan, wide, raw, send, sems):
+        sent = jnp.where(lane == s, send[s], sent)
+        offered = jnp.where(lane == send[s], 1, offered)
+    rows[...] = jnp.concatenate([sent, offered, jnp.zeros((6, BS), jnp.int32)], 0)
+
+
+def plan_kernel(where, raw, rows_ref, plan, wide):
     wide_odd, narrow_odd = where[0], where[1]
-    copies = [
-        pltpu.make_async_copy(source, target, sems.at[i])
-        for i, (source, target) in enumerate(
-            ((slab, raw.at[0]), (column, raw.at[1]), (live, raw.at[2]), (send_hbm, send))
-        )
-    ]
-    for copy in copies:
-        copy.start()
     wide[...] = jnp.zeros_like(wide)
-    for copy in copies:
-        copy.wait()
     wide[:, :, 0:R] = raw[...]
     window, col, used = wide[0], wide[1], wide[2]
     window_row = (window * 11) >> 5
@@ -106,11 +112,7 @@
     )
     entries = jnp.where(inside, entries, 0)
     first = lane[0:1]
-    offered = jnp.zeros((1, BS), jnp.int32)
-    sent = jnp.zeros((1, BS), jnp.int32)
-    for s in range(S):
-        offered = jnp.where(first == send[s], 1, offered)
-        sent = jnp.where(first == s, send[s], sent)
+    sent, offered = rows_ref[0:1, :], rows_ref[1:2, :]
     is_live = (used != 0) & inside
     is_offered = jnp.broadcast_to(offered, (K, BS)) == 1
     before = (
@@ -516,41 +518,43 @@
     narrow_odd = lax.axis_index("narrow") % 2
     where = jnp.stack([wide_odd, narrow_odd]).astype(jnp.int32)
 
-    own_modes, offered = pl.pallas_call(
+    own_modes, offered, raw, rows = pl.pallas_call(
         pack_kernel,
-        out_shape=(shape(R, GROUP, BS), shape(S, GROUP, BS)),
-        in_specs=[HBM] * 3,
-        out_specs=(VMEM, VMEM),
+        out_shape=(
+            shape(R, GROUP, BS),
+            shape(S, GROUP, BS),
+            shape(3, K, R, dtype=jnp.int32),
+            shape(8, BS, dtype=jnp.int32),
+        ),
+        in_specs=[HBM] * 6,
+        out_specs=(VMEM,) * 4,
         scratch_shapes=[
             pltpu.SMEM((S,), jnp.int32),
             pltpu.SMEM((R,), jnp.int32),
             pltpu.VMEM((MODES, R, BS), jnp.float32),
-            pltpu.SemaphoreType.DMA((3,)),
+            pltpu.SemaphoreType.DMA((6,)),
         ],
         compiler_params=params(4),
         name="pack",
     )(
         *(
             pltpu.with_memory_space_constraint(x, pltpu.HBM)
-            for x in (send, aggregate[0, 0], null_modes[0, 0].transpose(1, 0, 2))
+            for x in (
+                send, aggregate[0, 0], null_modes[0, 0].transpose(1, 0, 2), slab, column, live
+            )
         )
     )
     near, far = pair_halo(offered, "narrow")
     plan = pl.pallas_call(
         plan_kernel,
         out_shape=shape(16, LIST, dtype=jnp.int32),
-        in_specs=[SMEM] + [HBM] * 4,
+        in_specs=[SMEM] + [VMEM] * 2,
         out_specs=VMEM,
-        scratch_shapes=[
-            pltpu.VMEM((3, K, BS), jnp.int32),
-            pltpu.VMEM((3, K, R), jnp.int32),
-            pltpu.SMEM((S,), jnp.int32),
-            pltpu.SemaphoreType.DMA((4,)),
-        ],
+        scratch_shapes=[pltpu.VMEM((3, K, BS), jnp.int32)],
         compiler_params=params(8),
         cost_estimate=pl.CostEstimate(flops=10**8, bytes_accessed=5 * 10**6, transcendentals=0),
         name="plan",
-    )(where, *(pltpu.with_memory_space_constraint(x, pltpu.HBM) for x in (send, slab, column, live)))
+    )(where, raw, rows)
     line = jnp.concatenate([far, near, offered], 0)
     line, plan = lax.optimization_barrier((line, plan))
     wide_near, wide_far = pair_halo(line, "wide")

time: 78.4 us -> 79.6 us (1.015)
  starting transfers between devices: 27.4 us -> 34.2 us
  Pallas kernels: 38.6 us -> 34.9 us
  waiting for transfers between devices: 9.75 us -> 7.35 us
    ppermute x5, starting transfers between devices: 19.5 us -> 23.3 us  [pair_far(): return lax.ppermute(block, axis, pairs)]
    ppermute x1, starting transfers between devices: 1.92 us -> 5.05 us  [body(): lax.ppermute(far, 'narrow', far_pairs)]
    ppermute x1, waiting for transfers between devices: 2.54 us -> 0.01 us  [body(): lax.ppermute(near, 'narrow', pairs)]
    pallas_call x1, Pallas kernels: 13.5 us -> 12.3 us  [body(): pl.pallas_call(beside_kernel, out_shape=shape(25 * AGG, GROUP, 256), in_s...]
    pallas_call x1, Pallas kernels: 5.36 us -> 4.25 us  [body(): pl.pallas_call(corner_kernel, out_shape=(shape(3 * C, 25 * C),) * 3, in_s...]
    pallas_call x1, Pallas kernels: 2.04 us -> 1.19 us  [body(): pl.pallas_call(plan_kernel, out_shape=shape(16, LIST, dtype=jnp.int32), i...]
  transfers between devices with their start and end apart: 13 -> 13, of which waited for: 6 -> 3; matrix products, arithmetic and copies ran while one was open for 1% -> 1% of each run, Pallas kernels for 34% -> 31%
where the time goes in v5:
time: 79.6 us; the launch traced here: 78 us
  Pallas kernels  34.9 us (44%)
  starting transfers between devices  34.2 us (43%)
  waiting for transfers between devices  7.35 us (9%)
  between operations  1 us (1%)
    ppermute x5, starting transfers between devices, pair_far(): return lax.ppermute(block, axis, pairs)  23.3 us
    pallas_call x1, Pallas kernels, body(): pl.pallas_call(beside_kernel, out_shape=shape(25 * AGG, GROUP, 256), in_s...  12.3 us
    pallas_call x1, Pallas kernels, body(): pl.pallas_call(rest_kernel, out_shape=(shape(R, 9 * C, BS), shape(2 * BLO...  5.93 us
    ppermute x1, starting transfers between devices, body(): lax.ppermute(far, 'narrow', far_pairs)  5.05 us
    ppermute x1, starting transfers between devices, body(): lax.ppermute(far, 'wide', far_pairs)  4.89 us
    pallas_call x1, Pallas kernels, body(): pl.pallas_call(bring_kernel, out_shape=(shape(S * K, BS, 2 * BS, dtype=jn...  4.63 us
    pallas_call x1, Pallas kernels, body(): pl.pallas_call(corner_kernel, out_shape=(shape(3 * C, 25 * C),) * 3, in_s...  4.25 us
    ppermute x1, waiting for transfers between devices, body(): lax.ppermute(far, 'wide', far_pairs)  3.98 us
  transfers between devices with their start and end apart: 13, of which 3 were waited for; matrix products, arithmetic and copies ran while one was open for 1% of the time, Pallas kernels for 31%

profile of v5, /device:TPU:14, one launch (start us, length us, event | category | flops | bytes accessed | tf_op | source)
XLA Modules:
  0.0 78.0 jit_solution(17863363781751292066)
XLA Ops:
  0.6 1.1 %pack.1 = (f32[32,8,128]{2,1,0:T(8,128)S(1)}, f32[16,8,128]{2,1,0:T(8,128)S(1)}, s32[3,8,32]{2,1,0:T(8,128)S(1)}, s32[8,128]{1,0:T(8,128)S(1)}) custom-call(s32[16]{0:T(128)} %bitcast.28, s32[32]{0:T(128)} %bitcast.29, f32[6,32,128]{2,1,0:T(8,128)} %bitcast.24, s32[8,32]{1,0:T(8,128)} %bitcast.25, s32[8,32]{1,0:T(8,128)} %bitcast.26, s32[8,32]{1,0:T(8,128)} %bitcast.27), custom_call_target="tpu_custom_call" | custom-call | tf_op jit(solution)/shard_map/pack/pallas_call | solution.py:521
  1.7 0.5 collective-permute-start.1
  2.2 4.3 %collective-permute-start = (f32[16,8,128]{2,1,0:T(8,128)S(1)}, f32[16,8,128]{2,1,0:T(8,128)S(1)}, u32[]{:S(2)}, u32[]{:S(2)}) collective-permute-start(f32[16,8,128]{2,1,0:T(8,128)S(1)} %get-tuple-element.25), channel_id=1, source_target_pairs={{1,2},{2,1},{5,6},{6,5},{9,10},{10,9},{13,14},{14,13},{17,18},{18,... | collective-permute-start | bytes 196616 | tf_op jit(solution)/shard_map/ppermute | solution.py:47
  6.6 0.1 pad_add_fusion.where
  6.6 1.2 %plan.1.ints = s32[16,384]{1,0:T(8,128)S(1)} custom-call(s32[2]{0:T(128)S(1)} %pad_add_fusion.where, s32[3,8,32]{2,1,0:T(8,128)S(1)} %get-tuple-element.26.raw, s32[8,128]{1,0:T(8,128)S(1)} %get-tuple-element.27.rows_ref), custom_call_target="tpu_custom_call" | custom-call | flops 100000000 | bytes 5000000 | tf_op jit(solution)/shard_map/plan/pallas_call | solution.py:548
  7.9 0.0 collective-permute-done.1
  7.9 0.9 %collective-permute-done = f32[16,8,128]{2,1,0:T(8,128)S(1)} collective-permute-done((f32[16,8,128]{2,1,0:T(8,128)S(1)}, f32[16,8,128]{2,1,0:T(8,128)S(1)}, u32[]{:S(2)}, u32[]{:S(2)}) %collective-permute-start) | collective-permute-done | bytes 65568 | tf_op jit(solution)/shard_map/ppermute | solution.py:47
  8.8 4.5 %collective-permute-start.2 = (f32[48,8,128]{2,1,0:T(8,128)S(1)}, f32[48,8,128]{2,1,0:T(8,128)S(1)}, u32[]{:S(2)}, u32[]{:S(2)}) collective-permute-start(f32[48,8,128]{2,1,0:T(8,128)S(1)} %pad_maximum_fusion.3), channel_id=1, source_target_pairs={{4,8},{8,4},{12,16},{16,12},{20,24},{24,20},{28,32},{32,28},{36,40... | collective-permute-start | bytes 589832 | tf_op jit(solution)/shard_map/ppermute | solution.py:47
  13.3 0.1 collective-permute-start.3
  13.4 0.0 copy-start
  13.4 4.6 %bring.1 = (bf16[128,128,256]{2,1,0:T(8,128)(2,1)S(1)}, f32[32,8,128]{2,1,0:T(8,128)S(1)}) custom-call(s32[16,384]{1,0:T(8,128)S(1)} %plan.1.ints, f32[256,128,128]{2,1,0:T(8,128)} %bitcast.19), custom_call_target="tpu_custom_call" | custom-call | flops 100000000 | bytes 10000000 | tf_op jit(solution)/shard_map/bring/pallas_call | solution.py:567
  18.1 0.0 collective-permute-done.2
  18.1 0.0 collective-permute-done.3
  18.1 3.3 %offer.1 = (f32[256,8,128]{2,1,0:T(8,128)S(1)}, f32[776,128]{1,0:T(8,128)S(1)}) custom-call(s32[16,384]{1,0:T(8,128)S(1)} %plan.1.ints, s32[16,384]{1,0:T(8,128)S(1)} %plan.1.ints, bf16[128,128,256]{2,1,0:T(8,128)(2,1)S(1)} %get-tuple-element.31.halves, f32[32,8,128]{2,1,0:T(8,128)S(1)} %get-tuple-element.32.scale, ...), custom_call_target="tpu_custom_call" | custom-call | flops 100000000 | bytes 40000000 | tf_op jit(solution)/shard_map/offer/pallas_call | solution.py:577
  21.5 0.1 collective-permute-start.5
  21.6 3.7 %collective-permute-start.4 = (f32[776,128]{1,0:T(8,128)S(1)}, f32[776,128]{1,0:T(8,128)S(1)}, u32[]{:S(2)}, u32[]{:S(2)}) collective-permute-start(f32[776,128]{1,0:T(8,128)S(1)} %get-tuple-element.35), channel_id=1, source_target_pairs={{1,2},{2,1},{5,6},{6,5},{9,10},{10,9},{13,14},{14,13},{17,18},{18,... | collective-permute-start | bytes 1191944 | tf_op jit(solution)/shard_map/ppermute | solution.py:47
  25.3 5.7 %collective-permute-start.6 = (f32[776,128]{1,0:T(8,128)S(1)}, f32[776,128]{1,0:T(8,128)S(1)}, u32[]{:S(2)}, u32[]{:S(2)}) collective-permute-start(f32[776,128]{1,0:T(8,128)S(1)} %get-tuple-element.35), channel_id=1, source_target_pairs={{4,8},{8,4},{12,16},{16,12},{20,24},{24,20},{28,32},{32,28},{36,40... | collective-permute-start | bytes 1191944 | tf_op jit(solution)/shard_map/ppermute | solution.py:47
  31.1 0.0 copy-done
  31.1 5.9 %rest.1 = (f32[32,216,128]{2,1,0:T(8,128)}, f32[1552,128]{1,0:T(8,128)S(1)}, bf16[32,256,256]{2,1,0:T(8,128)(2,1)S(1)}) custom-call(s32[16,384]{1,0:T(8,128)S(1)} %plan.1.ints, s32[16,384]{1,0:T(8,128)S(1)} %plan.1.ints, f32[256,128,128]{2,1,0:T(8,128)S(1)} %bitcast.20, f32[160,8,128]{2,1,0:T(8,128)S(1)} %constant_dynamic-update-slice_fusion.table, ...), custom_call_target="tpu_custom_call" | custom-call | flops 2000000000 | bytes 20000000 | tf_op jit(solution)/shard_map/rest/pallas_call | solution.py:589
  37.0 0.0 collective-permute-done.5
  37.0 0.0 collective-permute-done.4
  37.0 0.1 pad_maximum_fusion.1
  37.1 0.1 pad_maximum_fusion
  37.2 0.0 collective-permute-done.6
  37.2 0.1 collective-permute-start.7
  37.3 0.1 constant_dynamic-update-slice_fusion.9
  37.4 5.0 %collective-permute-start.8 = (f32[1552,128]{1,0:T(8,128)S(1)}, f32[1552,128]{1,0:T(8,128)S(1)}, u32[]{:S(2)}, u32[]{:S(2)}) collective-permute-start(f32[1552,128]{1,0:T(8,128)S(1)} %pad_maximum_fusion.1), channel_id=1, source_target_pairs={{4,8},{8,4},{12,16},{16,12},{20,24},{24,20},{28,32},{32,28},{36,40... | collective-permute-start | bytes 2383880 | tf_op jit(solution)/shard_map/ppermute | solution.py:47
  42.4 0.1 constant_dynamic-update-slice_fusion.8
  42.5 0.1 constant_dynamic-update-slice_fusion.7
  42.6 0.0 collective-permute-done.7
  42.6 0.1 constant_dynamic-update-slice_fusion.5.table
  42.7 12.3 %beside.1.begun = f32[100,8,256]{2,1,0:T(8,128)S(1)} custom-call(s32[16,384]{1,0:T(8,128)S(1)} %plan.1.ints, f32[256,128,128]{2,1,0:T(8,128)S(1)} %bitcast.21, bf16[32,256,256]{2,1,0:T(8,128)(2,1)S(1)} %get-tuple-element.37.weights, f32[7760,128]{1,0:T(8,128)S(1)} %constant_dynamic-update-slice_fusion.5.table), custom_call_target="tpu_custom_call" | custom-call | flops 8000000000 | bytes 30000000 | tf_op jit(solution)/shard_map/beside/pallas_call | solution.py:629
  55.0 0.0 collective-permute-done.8.table
  55.0 4.2 %corner.1 = (f32[72,600]{1,0:T(8,128)S(1)}, f32[72,600]{1,0:T(8,128)S(1)}, f32[72,600]{1,0:T(8,128)S(1)}) custom-call(s32[16,384]{1,0:T(8,128)S(1)} %plan.1.ints, f32[256,128,128]{2,1,0:T(8,128)S(1)} %bitcast.22, bf16[32,256,256]{2,1,0:T(8,128)(2,1)S(1)} %get-tuple-element.37.weights, f32[100,8,256]{2,1,0:T(8,128)S(1)} %beside.1.begun, ...), custom_call_target="tpu_custom_call" | custom-call | tf_op jit(solution)/shard_map/corner/pallas_call | solution.py:639
  59.3 4.9 %collective-permute-start.10 = (f32[72,600]{1,0:T(8,128)S(1)}, f32[72,600]{1,0:T(8,128)S(1)}, u32[]{:S(2)}, u32[]{:S(2)}) collective-permute-start(f32[72,600]{1,0:T(8,128)S(1)} %get-tuple-element.44), channel_id=1, source_target_pairs={{4,8},{8,4},{12,16},{16,12},{20,24},{24,20},{28,32},{32,28},{36,40... | collective-permute-start | bytes 518408 | tf_op jit(solution)/shard_map/ppermute | solution.py:653
  64.2 0.1 collective-permute-start.9
  64.2 4.0 %collective-permute-done.10 = f32[72,600]{1,0:T(8,128)S(1)} collective-permute-done((f32[72,600]{1,0:T(8,128)S(1)}, f32[72,600]{1,0:T(8,128)S(1)}, u32[]{:S(2)}, u32[]{:S(2)}) %collective-permute-start.10) | collective-permute-done | bytes 172832 | tf_op jit(solution)/shard_map/ppermute | solution.py:653
  68.2 0.0 collective-permute-done.9
  68.3 0.7 merge.1
  69.0 0.1 collective-permute-start.11
  69.1 5.0 %collective-permute-start.12 = (f32[24,840]{1,0:T(8,128)S(1)}, f32[24,840]{1,0:T(8,128)S(1)}, u32[]{:S(2)}, u32[]{:S(2)}) collective-permute-start(f32[24,840]{1,0:T(8,128)S(1)} %get-tuple-element.47), channel_id=1, source_target_pairs={{1,2},{2,1},{5,6},{6,5},{9,10},{10,9},{13,14},{14,13},{17,18},{18,... | collective-permute-start | bytes 241928 | tf_op jit(solution)/shard_map/ppermute | solution.py:665
  74.1 0.0 collective-permute-done.11.near
  74.1 2.4 %collective-permute-done.12.far = f32[24,840]{1,0:T(8,128)S(1)} collective-permute-done((f32[24,840]{1,0:T(8,128)S(1)}, f32[24,840]{1,0:T(8,128)S(1)}, u32[]{:S(2)}, u32[]{:S(2)}) %collective-permute-start.12) | collective-permute-done | bytes 80672 | tf_op jit(solution)/shard_map/ppermute | solution.py:665
  76.6 1.5 %place.1 = f32[24,1176]{1,0:T(8,128)} custom-call(s32[2]{0:T(128)S(1)} %pad_add_fusion.where, f32[24,840]{1,0:T(8,128)S(1)} %get-tuple-element.45.own, f32[24,840]{1,0:T(8,128)S(1)} %collective-permute-done.11.near, f32[24,840]{1,0:T(8,128)S(1)} %collective-permute-done.12.far), custom_call_target="tpu_custom_call" | custom-call | tf_op jit(solution)/shard_map/place/pallas_call | solution.py:666
  (8 shorter events, 0.1 us)
Async XLA Ops:
  1.7 6.2 %collective-permute-start.1 = (f32[16,8,128]{2,1,0:T(8,128)S(1)}, f32[16,8,128]{2,1,0:T(8,128)S(1)}, u32[]{:S(2)}, u32[]{:S(2)}) collective-permute-start(f32[16,8,128]{2,1,0:T(8,128)S(1)} %get-tuple-element.25), channel_id=1, source_target_pairs={{0,1},{1,0},{2,3},{3,2},{4,5},{5,4},{6,7},{7,6},{8,9},{9,8},{10,11... | collective-permute-start | bytes 196616 | tf_op jit(solution)/shard_map/ppermute | solution.py:42
  2.2 6.5 %collective-permute-start = (f32[16,8,128]{2,1,0:T(8,128)S(1)}, f32[16,8,128]{2,1,0:T(8,128)S(1)}, u32[]{:S(2)}, u32[]{:S(2)}) collective-permute-start(f32[16,8,128]{2,1,0:T(8,128)S(1)} %get-tuple-element.25), channel_id=1, source_target_pairs={{1,2},{2,1},{5,6},{6,5},{9,10},{10,9},{13,14},{14,13},{17,18},{18,... | collective-permute-start | bytes 196616 | tf_op jit(solution)/shard_map/ppermute | solution.py:47
  8.8 9.3 %collective-permute-start.2 = (f32[48,8,128]{2,1,0:T(8,128)S(1)}, f32[48,8,128]{2,1,0:T(8,128)S(1)}, u32[]{:S(2)}, u32[]{:S(2)}) collective-permute-start(f32[48,8,128]{2,1,0:T(8,128)S(1)} %pad_maximum_fusion.3), channel_id=1, source_target_pairs={{4,8},{8,4},{12,16},{16,12},{20,24},{24,20},{28,32},{32,28},{36,40... | collective-permute-start | bytes 589832 | tf_op jit(solution)/shard_map/ppermute | solution.py:47
  13.3 4.8 %collective-permute-start.3 = (f32[48,8,128]{2,1,0:T(8,128)S(1)}, f32[48,8,128]{2,1,0:T(8,128)S(1)}, u32[]{:S(2)}, u32[]{:S(2)}) collective-permute-start(f32[48,8,128]{2,1,0:T(8,128)S(1)} %pad_maximum_fusion.3), channel_id=1, source_target_pairs={{0,4},{4,0},{8,12},{12,8},{16,20},{20,16},{24,28},{28,24},{32,36},... | collective-permute-start | bytes 589832 | tf_op jit(solution)/shard_map/ppermute | solution.py:42
  13.4 17.7 %copy-start = (f32[1,1,32,8,128,128]{5,4,3,2,1,0:T(8,128)S(1)}, f32[1,1,32,8,128,128]{5,4,3,2,1,0:T(8,128)}, u32[]{:S(2)}) copy-start(f32[1,1,32,8,128,128]{5,4,3,2,1,0:T(8,128)} %param.7) | copy-start | bytes 50331652
  21.5 15.5 %collective-permute-start.5 = (f32[776,128]{1,0:T(8,128)S(1)}, f32[776,128]{1,0:T(8,128)S(1)}, u32[]{:S(2)}, u32[]{:S(2)}) collective-permute-start(f32[776,128]{1,0:T(8,128)S(1)} %get-tuple-element.35), channel_id=1, source_target_pairs={{0,1},{1,0},{2,3},{3,2},{4,5},{5,4},{6,7},{7,6},{8,9},{9,8},{10,11... | collective-permute-start | bytes 1191944 | tf_op jit(solution)/shard_map/ppermute | solution.py:42
  21.6 15.4 %collective-permute-start.4 = (f32[776,128]{1,0:T(8,128)S(1)}, f32[776,128]{1,0:T(8,128)S(1)}, u32[]{:S(2)}, u32[]{:S(2)}) collective-permute-start(f32[776,128]{1,0:T(8,128)S(1)} %get-tuple-element.35), channel_id=1, source_target_pairs={{1,2},{2,1},{5,6},{6,5},{9,10},{10,9},{13,14},{14,13},{17,18},{18,... | collective-permute-start | bytes 1191944 | tf_op jit(solution)/shard_map/ppermute | solution.py:47
  25.3 11.9 %collective-permute-start.6 = (f32[776,128]{1,0:T(8,128)S(1)}, f32[776,128]{1,0:T(8,128)S(1)}, u32[]{:S(2)}, u32[]{:S(2)}) collective-permute-start(f32[776,128]{1,0:T(8,128)S(1)} %get-tuple-element.35), channel_id=1, source_target_pairs={{4,8},{8,4},{12,16},{16,12},{20,24},{24,20},{28,32},{32,28},{36,40... | collective-permute-start | bytes 1191944 | tf_op jit(solution)/shard_map/ppermute | solution.py:47
  37.2 5.3 %collective-permute-start.7 = (f32[2328,128]{1,0:T(8,128)S(1)}, f32[2328,128]{1,0:T(8,128)S(1)}, u32[]{:S(2)}, u32[]{:S(2)}) collective-permute-start(f32[2328,128]{1,0:T(8,128)S(1)} %pad_maximum_fusion), channel_id=1, source_target_pairs={{0,4},{4,0},{8,12},{12,8},{16,20},{20,16},{24,28},{28,24},{32,36},... | collective-permute-start | bytes 3575816 | tf_op jit(solution)/shard_map/ppermute | solution.py:42
  37.4 17.6 %collective-permute-start.8 = (f32[1552,128]{1,0:T(8,128)S(1)}, f32[1552,128]{1,0:T(8,128)S(1)}, u32[]{:S(2)}, u32[]{:S(2)}) collective-permute-start(f32[1552,128]{1,0:T(8,128)S(1)} %pad_maximum_fusion.1), channel_id=1, source_target_pairs={{4,8},{8,4},{12,16},{16,12},{20,24},{24,20},{28,32},{32,28},{36,40... | collective-permute-start | bytes 2383880 | tf_op jit(solution)/shard_map/ppermute | solution.py:47
  59.3 9.0 %collective-permute-start.10 = (f32[72,600]{1,0:T(8,128)S(1)}, f32[72,600]{1,0:T(8,128)S(1)}, u32[]{:S(2)}, u32[]{:S(2)}) collective-permute-start(f32[72,600]{1,0:T(8,128)S(1)} %get-tuple-element.44), channel_id=1, source_target_pairs={{4,8},{8,4},{12,16},{16,12},{20,24},{24,20},{28,32},{32,28},{36,40... | collective-permute-start | bytes 518408 | tf_op jit(solution)/shard_map/ppermute | solution.py:653
  64.2 4.1 %collective-permute-start.9 = (f32[72,600]{1,0:T(8,128)S(1)}, f32[72,600]{1,0:T(8,128)S(1)}, u32[]{:S(2)}, u32[]{:S(2)}) collective-permute-start(f32[72,600]{1,0:T(8,128)S(1)} %get-tuple-element.43), channel_id=1, source_target_pairs={{0,4},{4,0},{8,12},{12,8},{16,20},{20,16},{24,28},{28,24},{32,36},... | collective-permute-start | bytes 518408 | tf_op jit(solution)/shard_map/ppermute | solution.py:653
  69.0 5.2 %collective-permute-start.11 = (f32[24,840]{1,0:T(8,128)S(1)}, f32[24,840]{1,0:T(8,128)S(1)}, u32[]{:S(2)}, u32[]{:S(2)}) collective-permute-start(f32[24,840]{1,0:T(8,128)S(1)} %get-tuple-element.46), channel_id=1, source_target_pairs={{0,1},{1,0},{2,3},{3,2},{4,5},{5,4},{6,7},{7,6},{8,9},{9,8},{10,11... | collective-permute-start | bytes 241928 | tf_op jit(solution)/shard_map/ppermute | solution.py:665
  69.1 7.5 %collective-permute-start.12 = (f32[24,840]{1,0:T(8,128)S(1)}, f32[24,840]{1,0:T(8,128)S(1)}, u32[]{:S(2)}, u32[]{:S(2)}) collective-permute-start(f32[24,840]{1,0:T(8,128)S(1)} %get-tuple-element.47), channel_id=1, source_target_pairs={{1,2},{2,1},{5,6},{6,5},{9,10},{10,9},{13,14},{14,13},{17,18},{18,... | collective-permute-start | bytes 241928 | tf_op jit(solution)/shard_map/ppermute | solution.py:665
